TPU v7x, 512 devices: a whole 4x4x16 slice. The times are simulated.
512 devices in a mesh: fsdp: 64 (over z, x), seq: 8 (over y, core).
Axes of the slice: x: 4, y: 4, z: 16, core: 2. Of those that a mesh axis runs over, the one named last changes fastest.
Arguments:
- queries: bfloat16 [65536, 2048], P(('fsdp', 'seq')), may hold values from -20 to 20
- neighbours: bfloat16 [131072, 896], P(('fsdp', 'seq')), may hold values from -6 to 6
- neighbour_slot: int32 [2048], P('fsdp'), may hold values from 0 to 2047, as said below
- enc_gain: float32 [896], replicated, may hold values from 0.1 to 1.9
- enc_up: bfloat16 [896, 1792], P(None, 'fsdp'), may hold values from -0.1875 to 0.1875
- enc_down: bfloat16 [1792, 896], P('fsdp'), may hold values from -0.125 to 0.125
- key_proj: bfloat16 [896, 2048], P(None, 'fsdp'), may hold values from -0.1875 to 0.1875
- value_proj: bfloat16 [896, 2048], P(None, 'fsdp'), may hold values from -0.1875 to 0.1875
- grad_attn: bfloat16 [65536, 2048], P(('fsdp', 'seq')), may hold values from -6 to 6
Outputs:
- attended: bfloat16 [65536, 2048], P(('fsdp', 'seq'))
- grad_queries: bfloat16 [65536, 2048], P(('fsdp', 'seq'))
- grad_encoded: bfloat16 [131072, 896], P(('fsdp', 'seq'))
Inputs may be any that keep to these rules, and one draw needn't show every extreme that they name: neighbour_slot is a permutation of the 2048 slots; a neighbour's slot belongs to a span on a device of the same index of fsdp as the neighbour; the 4 neighbours of one device fill exactly 1 slot on each of 4 devices of its seq group and none on the other 4.
All inputs are finite; a program needn't handle non-finite values.
Results may differ from a plain program's by a relative error of at most 0.015.
The roundings to bfloat16 on the way count: a program that leaves them out, or rounds other values in their place, can miss the bound.
Values may be sent and summed in bfloat16 or wider, within the bound.
No kernel may reach another device: no remote copies, remote signals or barrier semaphores. Data moves between devices by JAX's collectives and lax.ppermute only.
A program may use at most 64 MiB of HBM per device.

v0:
```python
import jax
import jax.numpy as jnp
from jax import lax
from jax.sharding import PartitionSpec as P

E = 896
HEADS = 16
HD = 128
CL = 64
NLEN = 64
NPC = 2
CH_DEV = 2


EPS = 1e-06


def encode(raw_rows, enc_gain, enc_up, enc_down):
    floats = raw_rows.astype(jnp.float32)
    normed = (
        floats * lax.rsqrt(jnp.mean(floats * floats, axis=-1, keepdims=True) + EPS) * enc_gain
    ).astype(jnp.bfloat16)
    product = jnp.dot(
        normed,
        lax.all_gather(enc_up, "fsdp", axis=1, tiled=True),
        preferred_element_type=jnp.float32,
    )
    hidden = jax.nn.gelu(product, approximate=True).astype(jnp.bfloat16)
    summed = jnp.dot(
        hidden,
        lax.all_gather(enc_down, "fsdp", axis=0, tiled=True),
        preferred_element_type=jnp.float32,
    )
    return (floats + summed).astype(jnp.bfloat16)


def routing(neighbour_slot, seq_count, per_device, capacity):
    group_size = seq_count * per_device
    my_index = lax.axis_index("seq")
    offset = lax.axis_index("fsdp") * group_size
    slot_local = neighbour_slot - offset
    target = slot_local // per_device
    positions = jnp.arange(group_size, dtype=jnp.int32)
    source = positions // per_device
    earlier = (
        (source[:, None] == source[None, :])
        & (target[:, None] == target[None, :])
        & (positions[None, :] < positions[:, None])
    )
    rank_within = jnp.sum(earlier.astype(jnp.int32), axis=1)
    buffer_index = target * capacity + rank_within
    sender_index = source * capacity + rank_within
    my_buffer = lax.dynamic_slice_in_dim(buffer_index, my_index * per_device, per_device)
    buffer_slots = jnp.arange(seq_count * capacity, dtype=jnp.int32)
    send_onehot = (buffer_slots[:, None] == my_buffer[None, :]).astype(jnp.bfloat16)
    wanted = my_index * per_device + jnp.arange(per_device, dtype=jnp.int32)
    matches = (wanted[:, None] == slot_local[None, :]).astype(jnp.float32)
    picked = (sender_index[:, None] == buffer_slots[None, :]).astype(jnp.float32)
    recv_onehot = jnp.dot(matches, picked).astype(jnp.bfloat16)
    return (send_onehot, recv_onehot)


def deliver(flat_rows, send_onehot, recv_onehot):
    outgoing = jnp.dot(send_onehot, flat_rows, preferred_element_type=jnp.float32).astype(
        jnp.bfloat16
    )
    incoming = lax.all_to_all(outgoing, "seq", split_axis=0, concat_axis=0, tiled=True)
    return jnp.dot(recv_onehot, incoming, preferred_element_type=jnp.float32).astype(jnp.bfloat16)


def body(
    queries, neighbours, neighbour_slot, enc_gain, enc_up, enc_down, key_proj, value_proj, grad_attn
):
    seq_count = lax.axis_size("seq")
    per_device = CH_DEV * NPC
    capacity = per_device // min(seq_count, per_device)
    row_count = per_device * NLEN
    send_onehot, recv_onehot = routing(neighbour_slot, seq_count, per_device, capacity)
    encoded = encode(neighbours, enc_gain, enc_up, enc_down)
    placed = deliver(encoded.reshape(per_device, NLEN * E), send_onehot, recv_onehot).reshape(
        row_count, E
    )
    key_full, value_full = (
        lax.all_gather(key_proj, "fsdp", axis=1, tiled=True),
        lax.all_gather(value_proj, "fsdp", axis=1, tiled=True),
    )
    key_rows = jnp.dot(placed, key_full, preferred_element_type=jnp.float32).astype(jnp.bfloat16)
    value_rows = jnp.dot(placed, value_full, preferred_element_type=jnp.float32).astype(
        jnp.bfloat16
    )
    score_scale = HD ** (-0.5)
    key_heads = key_rows.reshape(CH_DEV, NPC * NLEN, HEADS, HD)
    value_heads = value_rows.reshape(CH_DEV, NPC * NLEN, HEADS, HD)
    query_heads = queries.reshape(CH_DEV, CL, HEADS, HD)
    grad_heads = grad_attn.reshape(CH_DEV, CL, HEADS, HD)
    scores = (
        jnp.einsum("cqhd,ckhd->chqk", query_heads, key_heads, preferred_element_type=jnp.float32)
        * score_scale
    )
    exponent = jnp.exp(scores - jnp.max(scores, axis=-1, keepdims=True))
    probabilities = exponent / jnp.sum(exponent, axis=-1, keepdims=True)
    prob_low = probabilities.astype(jnp.bfloat16)
    attended = jnp.einsum(
        "chqk,ckhd->cqhd", prob_low, value_heads, preferred_element_type=jnp.float32
    ).astype(jnp.bfloat16)
    grad_probs = jnp.einsum(
        "cqhd,ckhd->chqk", grad_heads, value_heads, preferred_element_type=jnp.float32
    )
    row_delta = jnp.sum(probabilities * grad_probs, axis=-1, keepdims=True)
    grad_scores = (probabilities * (grad_probs - row_delta) * score_scale).astype(jnp.bfloat16)
    grad_queries = jnp.einsum(
        "chqk,ckhd->cqhd", grad_scores, key_heads, preferred_element_type=jnp.float32
    ).astype(jnp.bfloat16)
    grad_keys = jnp.einsum(
        "chqk,cqhd->ckhd", grad_scores, query_heads, preferred_element_type=jnp.float32
    ).astype(jnp.bfloat16)
    grad_values = jnp.einsum(
        "chqk,cqhd->ckhd", prob_low, grad_heads, preferred_element_type=jnp.float32
    ).astype(jnp.bfloat16)
    grad_keys = grad_keys.reshape(row_count, HEADS * HD)
    grad_values = grad_values.reshape(row_count, HEADS * HD)
    contract_dims = (((1,), (1,)), ((), ()))
    grad_encoded = (
        lax.dot_general(grad_keys, key_full, contract_dims, preferred_element_type=jnp.float32)
        + lax.dot_general(
            grad_values, value_full, contract_dims, preferred_element_type=jnp.float32
        )
    ).astype(jnp.bfloat16)
    return (
        attended.reshape(CH_DEV * CL, HEADS * HD),
        grad_queries.reshape(CH_DEV * CL, HEADS * HD),
        grad_encoded,
    )


def solution(mesh):
    in_specs = (
        P(("fsdp", "seq"), None),
        P(("fsdp", "seq"), None),
        P("fsdp"),
        P(),
        P(None, "fsdp"),
        P("fsdp", None),
        P(None, "fsdp"),
        P(None, "fsdp"),
        P(("fsdp", "seq"), None),
    )
    out_specs = (P(("fsdp", "seq"), None), P(("fsdp", "seq"), None), P(("fsdp", "seq"), None))
    return jax.shard_map(body, mesh=mesh, in_specs=in_specs, out_specs=out_specs, check_vma=False)
```

profile of v0, /device:TPU:1, one launch (start us, length us, event | category | flops | bytes accessed | tf_op | source)
XLA Modules:
  0.0 642.6 jit_solution(8656656157989176286)
XLA Ops:
  7.2 0.7 all-gather.13.cloned.1.call-update
  7.9 0.7 all-gather.11.cloned.1.call-update
  8.7 0.7 all-gather.7.cloned.1.call-update
  9.4 0.0 all-gather.9.cloned.1.call-start
  9.4 0.5 all-gather.9.cloned.1.call-update
  10.0 0.7 and_select_fusion
  10.6 0.2 convert_reduce_fusion
  10.8 0.1 dynamic_slice.3
  10.9 1.2 fusion.39
  12.1 140.2 %all-gather.13.cloned.1.call-done = bf16[64,28,896]{2,1,0:T(8,128)(2,1)} async-done(((bf16[1,28,896]{2,1,0:T(8,128)(2,1)}), bf16[64,28,896]{2,1,0:T(8,128)(2,1)}) %all-gather.13.cloned.1.call-update) | async-done | bytes 3211280 | tf_op jit(solution)/shard_map/all_gather | solution.py:31
  152.3 4.6 reshape.102
  156.9 138.1 %all-gather.11.cloned.1.call-done = bf16[64,28,896]{2,1,0:T(8,128)(2,1)} async-done(((bf16[1,28,896]{2,1,0:T(8,128)(2,1)}), bf16[64,28,896]{2,1,0:T(8,128)(2,1)}) %all-gather.11.cloned.1.call-update) | async-done | bytes 3211280 | tf_op jit(solution)/shard_map/all_gather | solution.py:25
  295.0 6.0 reshape.100
  301.0 5.0 fusion.23
  306.1 1.2 reshape.89
  307.3 0.4 fusion.2
  307.7 0.5 broadcast.118
  308.2 1.4 reduce
  309.6 1.7 reshape.103
  311.3 14.5 %all-to-all-start = ((bf16[8,2,28672]{2,1,0:T(2,128)(2,1)}), bf16[8,2,28672]{2,1,0:T(2,128)(2,1)S(1)}, u32[]{:S(2)}, u32[]{:S(2)}) async-start(bf16[8,2,28672]{2,1,0:T(2,128)(2,1)} %reshape.103), calls=%async_computation | async-start | bytes 1835008 | tf_op jit(solution)/shard_map/all_to_all | solution.py:67
  325.7 0.9 copy.73
  326.6 0.9 copy.76
  327.6 11.9 %all-to-all-done = bf16[8,2,28672]{2,1,0:T(2,128)(2,1)S(1)} async-done(((bf16[8,2,28672]{2,1,0:T(2,128)(2,1)}), bf16[8,2,28672]{2,1,0:T(2,128)(2,1)S(1)}, u32[]{:S(2)}, u32[]{:S(2)}) %all-to-all-start) | async-done | bytes 917536 | tf_op jit(solution)/shard_map/all_to_all | solution.py:67
  339.4 1.1 reshape.104
  340.5 1.3 convolution_convert_fusion.1
  341.8 0.3 reshape.90
  342.1 95.6 %all-gather.7.cloned.1.call-done = bf16[896,2048]{0,1:T(8,128)(2,1)} async-done(((bf16[896,32]{0,1:T(8,128)(2,1)}), bf16[896,2048]{0,1:T(8,128)(2,1)}) %all-gather.7.cloned.1.call-update) | async-done | bytes 3670032 | tf_op jit(solution)/shard_map/all_gather | solution.py:85
  437.7 3.3 fusion.15
  441.0 0.2 copy.74
  441.3 139.0 %all-gather.9.cloned.1.call-done = bf16[896,2048]{0,1:T(8,128)(2,1)} async-done(((bf16[896,32]{0,1:T(8,128)(2,1)}), bf16[896,2048]{0,1:T(8,128)(2,1)}) %all-gather.9.cloned.1.call-update) | async-done | bytes 3670032 | tf_op jit(solution)/shard_map/all_gather | solution.py:84
  580.3 3.4 fusion.16
  583.6 0.2 copy.72
  583.9 0.8 fusion.20
  584.7 1.3 fusion.86
  586.1 4.4 fusion.24
  590.5 2.9 convolution_bitcast_fusion
  593.4 14.1 %fusion.25 = bf16[2,64,16,128]{3,1,2,0:T(8,128)(2,1)} fusion(f32[2,16,64,128]{3,2,1,0:T(8,128)} %convolution_bitcast_fusion, bf16[2,128,16,128]{3,2,1,0:T(8,128)(2,1)S(1)} %bitcast.70, f32[2,16,64,128]{3,2,1,0:T(8,128)} %get-tuple-element.8, f32[2,16,64]{2,1,0:T(8,128)S(1)} %get-tuple-element.7), kind=kOutput, calls=%fused_computation.40 | convolution fusion | flops 69208192 | bytes 3678208 | tf_op jit(solution)/shard_map/chqk,ckhd->cqhd/dot_general | solution.py:111
  607.6 14.1 %fusion.12 = bf16[2,128,16,128]{3,1,2,0:T(8,128)(2,1)S(1)} fusion(f32[2,16,64,128]{3,2,1,0:T(8,128)} %convolution_bitcast_fusion, bf16[2,64,16,128]{3,2,1,0:T(8,128)(2,1)S(1)} %bitcast.74, f32[2,16,64,128]{3,2,1,0:T(8,128)} %get-tuple-element.8, f32[2,16,64]{2,1,0:T(8,128)S(1)} %get-tuple-element.7), kind=kOutput, calls=%fused_computation.22 | convolution fusion | flops 69470336 | bytes 3678208 | tf_op jit(solution)/shard_map/chqk,cqhd->ckhd/dot_general | solution.py:114
  621.7 5.2 fusion.13
  626.9 0.3 copy.62
  627.2 0.9 copy.111
  628.1 1.5 copy.66
  629.7 0.9 copy.110
  630.6 0.7 copy.68
  631.3 0.7 copy.70
  632.0 1.3 fusion.28
  633.3 0.8 copy-done.7
  634.0 2.0 fusion.22
  (25 shorter events, 0.2 us)
Async XLA Ops:
  7.2 145.2 %all-gather.13.cloned.1.call-start = ((), (), s32[]{:S(2)}) async-start(), calls=%async_computation.4 | async-start | bytes 3727360 | tf_op jit(solution)/shard_map/all_gather | solution.py:31
  7.9 287.1 %all-gather.11.cloned.1.call-start = ((), (), s32[]{:S(2)}) async-start(), calls=%async_computation.3 | async-start | bytes 3727360 | tf_op jit(solution)/shard_map/all_gather | solution.py:25
  8.6 429.1 %all-gather.7.cloned.1.call-start = ((), (), s32[]{:S(2)}) async-start(), calls=%async_computation.1 | async-start | bytes 3727360 | tf_op jit(solution)/shard_map/all_gather | solution.py:85
  9.4 570.9 %all-gather.9.cloned.1.call-start = ((), (), s32[]{:S(2)}) async-start(), calls=%async_computation.2 | async-start | bytes 3727360 | tf_op jit(solution)/shard_map/all_gather | solution.py:84
  156.9 144.1 %copy-start.9 = (f32[896]{0:T(1024)S(1)}, f32[896]{0:T(1024)}, u32[]{:S(2)}) copy-start(f32[896]{0:T(1024)} %param.12) | copy-start | bytes 10756
  307.3 18.5 %copy-start.4 = (bf16[128,2048]{1,0:T(8,128)(2,1)S(1)}, bf16[128,2048]{1,0:T(8,128)(2,1)}, u32[]{:S(2)}) copy-start(bf16[128,2048]{1,0:T(8,128)(2,1)} %param.9) | copy-start | bytes 1572868
  308.2 18.5 %copy-start.5 = (bf16[128,2048]{1,0:T(8,128)(2,1)S(1)}, bf16[128,2048]{1,0:T(8,128)(2,1)}, u32[]{:S(2)}) copy-start(bf16[128,2048]{1,0:T(8,128)(2,1)} %param.17) | copy-start | bytes 1572868
  311.3 28.2 %all-to-all-start = ((bf16[8,2,28672]{2,1,0:T(2,128)(2,1)}), bf16[8,2,28672]{2,1,0:T(2,128)(2,1)S(1)}, u32[]{:S(2)}, u32[]{:S(2)}) async-start(bf16[8,2,28672]{2,1,0:T(2,128)(2,1)} %reshape.103), calls=%async_computation | async-start | bytes 1835008 | tf_op jit(solution)/shard_map/all_to_all | solution.py:67
  580.3 3.6 copy-start.1
  593.4 14.1 %copy-start.2 = (bf16[16,8,16,128]{3,2,1,0:T(8,128)(2,1)S(1)}, bf16[16,8,16,128]{3,2,1,0:T(8,128)(2,1)}, u32[]{:S(2)}) copy-start(bf16[16,8,16,128]{3,2,1,0:T(8,128)(2,1)} %copy.73) | copy-start | bytes 1572868
  607.6 14.1 %copy-start = (bf16[16,8,16,128]{3,2,1,0:T(8,128)(2,1)S(1)}, bf16[16,8,16,128]{3,2,1,0:T(8,128)(2,1)}, u32[]{:S(2)}) copy-start(bf16[16,8,16,128]{3,2,1,0:T(8,128)(2,1)} %copy.76) | copy-start | bytes 1572868
  621.6 5.2 copy-start.6
  626.9 4.4 copy-start.3
  628.1 3.8 copy-start.8
  632.0 2.0 copy-start.7
Sparse Core Ops, SparseCore 0:
  10.9 141.3 all-gather.12
  155.3 139.7 all-gather.10
  298.0 139.7 all-gather.6
  440.5 139.7 all-gather.8
where the time goes:
time: 652 us; the launch traced here: 643 us
  waiting for transfers between devices  527 us (81%)
  matrix products  58.3 us (9%)
  local copies, waits for them, and re-layouts  23.6 us (4%)
  starting transfers between devices  14.6 us (2%)
  between operations  13.9 us (2%)
    all_gather x1, waiting for transfers between devices, encode(): lax.all_gather(enc_down, 'fsdp', axis=0, tiled=True)  140 us
    all_gather x1, waiting for transfers between devices, body(): lax.all_gather(key_proj, 'fsdp', axis=1, tiled=True)  139 us
    all_gather x1, waiting for transfers between devices, encode(): lax.all_gather(enc_up, 'fsdp', axis=1, tiled=True)  138 us
    all_gather x1, waiting for transfers between devices, body(): lax.all_gather(value_proj, 'fsdp', axis=1, tiled=True)  95.6 us
    unnamed x30, local copies, waits for them, and re-layouts  18.3 us
    all_to_all x1, starting transfers between devices, deliver(): lax.all_to_all(outgoing, 'seq', split_axis=0, concat_axis=0, tiled=True)  14.5 us
    dot_general x1, matrix products, body(): jnp.einsum('chqk,ckhd->cqhd', grad_scores, key_heads, preferred_element_t...  14.1 us
    dot_general x1, matrix products, body(): jnp.einsum('chqk,cqhd->ckhd', grad_scores, query_heads, preferred_element...  14.1 us
  transfers between devices with their start and end apart: 5, of which 5 were waited for; matrix products, arithmetic and copies ran while one was open for 5% of the time, Pallas kernels for 0%

commit v1 on v0

v1 whole, which is shorter than its diff:
```python
import jax
import jax.numpy as jnp
from jax import lax
from jax.experimental import pallas as pl
from jax.experimental.pallas import tpu as pltpu
from jax.sharding import Mesh, PartitionSpec as P

E = 896
HEADS = 16
HD = 128
CL = 64
NLEN = 64
NPC = 2
CH_DEV = 2
NZ, NX, NY, NC = 16, 4, 4, 2
PER_DEV = CH_DEV * NPC
ROWS = PER_DEV * NLEN
UNITS = 28
HALF = UNITS // 2
QUART = UNITS // 4
EPS = 1e-06
SCALE = HD ** (-0.5)
ALL = ("z", "x", "y", "c")
NT = (((1,), (1,)), ((), ()))
NN = (((1,), (0,)), ((), ()))
TN = (((0,), (0,)), ((), ()))


def dot(a, b, dims):
    return lax.dot_general(a, b, dims, preferred_element_type=jnp.float32)


def ring_pairs(step):
    pairs = []
    for x in range(NX):
        for y in range(NY):
            pairs.append(((x * NY + y) * NC, (x * NY + (y + step) % NY) * NC))
            pairs.append(((x * NY + y) * NC + 1, ((x + step) % NX * NY + y) * NC + 1))
    return pairs


def ring(rows, step):
    return lax.ppermute(rows, ("x", "y", "c"), ring_pairs(step))


def swap(rows):
    return lax.ppermute(rows, "c", [(0, 1), (1, 0)])


def send_kernel(meta, raw_ref, out_ref):
    for i in range(PER_DEV):
        out_ref[meta[PER_DEV * meta[32] + i] // PER_DEV] = raw_ref[i]


def send_blocks(meta, raw):
    return pl.pallas_call(
        send_kernel,
        out_shape=jax.ShapeDtypeStruct((NY * NC, NLEN, E), jnp.bfloat16),
        in_specs=[
            pl.BlockSpec(memory_space=pltpu.SMEM),
            pl.BlockSpec(memory_space=pltpu.VMEM),
        ],
        out_specs=pl.BlockSpec(memory_space=pltpu.VMEM),
        name="send_blocks",
    )(meta, raw)


def gelu(x):
    return 0.5 * x * (1.0 + jnp.tanh(0.7978845608028654 * (x + 0.044715 * (x * x * x))))


def encode_kernel(
    meta, recv_ref, gain_ref, o0, o1, o2, o3, o4, s0, s1, s2, s3, s4, out_ref, buf_y, buf_x, raw, sems
):
    core, y = meta[33], meta[34]
    half = NZ // 2

    def copies(pieces, buf, place, lane):
        own, left, right, far_a, far_b = pieces
        far = (place + 2) % 4
        targets = (
            (own, buf.at[place]),
            (left, buf.at[(place + 3) % 4]),
            (right, buf.at[(place + 1) % 4]),
            (far_a, buf.at[far, 0:half]),
            (far_b, buf.at[far, half:NZ]),
        )
        return [
            pltpu.make_async_copy(src, dst, sems.at[lane, i]) for i, (src, dst) in enumerate(targets)
        ]

    own, other = (o0, o1, o2, o3, o4), (s0, s1, s2, s3, s4)

    @pl.when(core == 0)
    def _():
        for copy in copies(own, buf_y, y, 0) + copies(other, buf_x, 0, 1):
            copy.start()

    @pl.when(core != 0)
    def _():
        for copy in copies(other, buf_y, y, 0) + copies(own, buf_x, 0, 1):
            copy.start()

    first = PER_DEV * meta[32]
    for n in range(NY * NC * PER_DEV):
        slot = meta[n] - first

        @pl.when((slot >= 0) & (slot < PER_DEV))
        def _():
            raw[slot] = recv_ref[n // PER_DEV]

    floats = raw[...].reshape(ROWS, E).astype(jnp.float32)
    mean = jnp.mean(floats * floats, axis=-1, keepdims=True)
    normed = (floats * lax.rsqrt(mean + EPS) * gain_ref[...]).astype(jnp.bfloat16)

    for copy in copies(own, buf_y, y, 0):
        copy.wait()
    acc = jnp.zeros((ROWS, E), jnp.float32)

    def block(acc, up, down):
        hidden = gelu(dot(normed, up, NT)).astype(jnp.bfloat16)
        return acc + dot(hidden, down, NN)

    for part in range(2):
        for z in range(0, NZ, 8):
            acc = block(
                acc,
                buf_y[part, z : z + 8].reshape(256, E),
                buf_y[part + 2, z : z + 8].reshape(256, E),
            )
    for copy in copies(own, buf_x, 0, 1):
        copy.wait()
    for part in range(4):
        acc = block(
            acc,
            buf_x[part, :, 0:16].reshape(256, E),
            buf_x[part, :, 16:32].reshape(256, E),
        )
    out_ref[...] = (floats + acc).astype(jnp.bfloat16)


def encode(meta, recv, gain, own, other):
    hbm = pl.BlockSpec(memory_space=pl.ANY)
    vmem = pl.BlockSpec(memory_space=pltpu.VMEM)
    return pl.pallas_call(
        encode_kernel,
        out_shape=jax.ShapeDtypeStruct((ROWS, E), jnp.bfloat16),
        in_specs=[pl.BlockSpec(memory_space=pltpu.SMEM), vmem, vmem] + [hbm] * 10,
        out_specs=vmem,
        scratch_shapes=[
            pltpu.VMEM((4, NZ, 32, E), jnp.bfloat16),
            pltpu.VMEM((4, NZ, 32, E), jnp.bfloat16),
            pltpu.VMEM((PER_DEV, NLEN, E), jnp.bfloat16),
            pltpu.SemaphoreType.DMA((2, 5)),
        ],
        compiler_params=pltpu.CompilerParams(vmem_limit_bytes=28 * 1024 * 1024),
        name="encode_rows",
    )(meta, recv, gain, *own, *other)


GROUP = 4
CHUNK = 4
CUT = 8
LAST = 256


def attend_kernel(enc_ref, w_hbm, q_hbm, g_hbm, att_hbm, gq_hbm, ge_ref, w, q_ref, g_ref, kv, gkv, att, gq, sems, outs):
    def fetch(i):
        return pltpu.make_async_copy(
            w_hbm.at[i * CUT : (i + 1) * CUT], w.at[i * CUT : (i + 1) * CUT], sems.at[i]
        )

    loads = [fetch(i) for i in range(2 * HEADS // CUT)]
    loads.append(pltpu.make_async_copy(q_hbm, q_ref, sems.at[len(loads)]))
    loads.append(pltpu.make_async_copy(g_hbm, g_ref, sems.at[len(loads)]))
    for copy in loads:
        copy.start()

    enc = enc_ref[...]
    for i in range(2 * HEADS // CUT):
        loads[i].wait()
        for j in range(i * CUT, (i + 1) * CUT, CHUNK):
            rows = w[j : j + CHUNK].reshape(CHUNK * HD, E)
            kv[:, j * HD : (j + CHUNK) * HD] = dot(enc, rows, NT).astype(jnp.bfloat16)
    loads[-2].wait()
    loads[-1].wait()

    shape = (CH_DEV * CL, ROWS)
    own_span = lax.broadcasted_iota(jnp.int32, shape, 0) // CL == (
        lax.broadcasted_iota(jnp.int32, shape, 1) // (NPC * NLEN)
    )
    for base in range(0, HEADS, GROUP):
        heads = range(base, base + GROUP)
        cols = [slice(h * HD, (h + 1) * HD) for h in heads]
        kcols = [slice(2 * h * HD, (2 * h + 1) * HD) for h in heads]
        vcols = [slice((2 * h + 1) * HD, (2 * h + 2) * HD) for h in heads]
        scores = [dot(q_ref[:, c], kv[:, k], NT) for c, k in zip(cols, kcols)]
        grad_probs = [dot(g_ref[:, c], kv[:, v], NT) for c, v in zip(cols, vcols)]
        scores = [jnp.where(own_span, s * SCALE, -jnp.inf) for s in scores]
        exponent = [jnp.exp(s - jnp.max(s, axis=-1, keepdims=True)) for s in scores]
        probs = [e * (1.0 / jnp.sum(e, axis=-1, keepdims=True)) for e in exponent]
        low = [p.astype(jnp.bfloat16) for p in probs]
        delta = [jnp.sum(p * gp, axis=-1, keepdims=True) for p, gp in zip(probs, grad_probs)]
        grad_scores = [
            (p * (gp - d) * SCALE).astype(jnp.bfloat16)
            for p, gp, d in zip(probs, grad_probs, delta)
        ]
        for i, (c, k, v) in enumerate(zip(cols, kcols, vcols)):
            att[:, c] = dot(low[i], kv[:, v], NN).astype(jnp.bfloat16)
            gkv[:, v] = dot(low[i], g_ref[:, c], TN).astype(jnp.bfloat16)
            gq[:, c] = dot(grad_scores[i], kv[:, k], NN).astype(jnp.bfloat16)
            gkv[:, k] = dot(grad_scores[i], q_ref[:, c], TN).astype(jnp.bfloat16)
    stores = [
        pltpu.make_async_copy(att, att_hbm, outs.at[0]),
        pltpu.make_async_copy(gq, gq_hbm, outs.at[1]),
    ]
    for copy in stores:
        copy.start()
    rows = w[...].reshape(2 * HEADS * HD, E)
    for j in range(0, E, LAST):
        wide = slice(j, min(j + LAST, E))
        ge_ref[:, wide] = dot(gkv[...], rows[:, wide], NN).astype(jnp.bfloat16)
    for copy in stores:
        copy.wait()


def attend(enc, weights, queries, grads):
    tokens = CH_DEV * CL
    hbm = pl.BlockSpec(memory_space=pltpu.HBM)
    vmem = pl.BlockSpec(memory_space=pltpu.VMEM)
    wide = jax.ShapeDtypeStruct((tokens, HEADS * HD), jnp.bfloat16)
    full = pltpu.VMEM((tokens, HEADS * HD), jnp.bfloat16)
    both = pltpu.VMEM((ROWS, 2 * HEADS * HD), jnp.bfloat16)
    return pl.pallas_call(
        attend_kernel,
        out_shape=(wide, wide, jax.ShapeDtypeStruct((ROWS, E), jnp.bfloat16)),
        in_specs=[vmem, hbm, hbm, hbm],
        out_specs=(hbm, hbm, vmem),
        scratch_shapes=[
            pltpu.VMEM((2 * HEADS, HD, E), jnp.bfloat16),
            full,
            full,
            both,
            both,
            full,
            full,
            pltpu.SemaphoreType.DMA((2 * HEADS // CUT + 2,)),
            pltpu.SemaphoreType.DMA((2,)),
        ],
        compiler_params=pltpu.CompilerParams(vmem_limit_bytes=56 * 1024 * 1024),
        name="attend_spans",
    )(enc, weights, queries, grads)


def body(queries, neighbours, slots, gain, up, down, key_proj, value_proj, grads):
    z, x, y, c = (lax.axis_index(name) for name in ALL)
    group = NY * NC * PER_DEV
    place = jnp.stack([y * NC + c, c, y, x]).astype(jnp.int32)
    meta = jnp.concatenate([slots - (z * NX + x) * group, place])

    up = up.T
    kv_unit = jnp.where(c == 0, key_proj.T, value_proj.T)
    halves = jnp.concatenate([up[:HALF], down[:HALF]])
    quarter = jnp.pad(lax.dynamic_slice_in_dim(halves, y * QUART, QUART), ((0, 1), (0, 0)))
    pad = ((0, 16 - HALF), (0, 0))
    whole = jnp.concatenate([jnp.pad(up[HALF:], pad), jnp.pad(down[HALF:], pad)])

    along_x = lax.all_gather(jnp.concatenate([kv_unit, quarter]), "x", axis=0, tiled=False)
    kv_head = along_x[:, :32].reshape(HD, E)
    weights = lax.all_gather(kv_head, ("z", "c"), axis=0, tiled=False)

    outgoing = send_blocks(meta, neighbours.reshape(PER_DEV, NLEN, E))
    ff_unit = jnp.where(c == 0, along_x[:, 32:].reshape(32, E), whole)
    ff_unit, outgoing = lax.optimization_barrier((ff_unit, outgoing))
    recv = lax.all_to_all(outgoing, ("y", "c"), 0, 0, tiled=True)
    own = lax.all_gather(ff_unit, "z", axis=0, tiled=False)
    own, recv = lax.optimization_barrier((own, recv))
    left = ring(own, 1)
    right = ring(own, -1)
    far_a = ring(left[: NZ // 2], 1)
    far_b = ring(right[NZ // 2 :], -1)
    pieces = (own, left, right, far_a, far_b)
    others = tuple(swap(piece) for piece in pieces)

    enc = encode(meta, recv, gain.reshape(1, E), pieces, others)
    return attend(enc, weights, queries, grads)


def solution(mesh):
    wide = Mesh(mesh.devices.reshape(NZ, NX, NY, NC), ALL)
    rows = P(ALL, None)
    fsdp = ("z", "x")
    in_specs = (
        rows,
        rows,
        P(fsdp),
        P(),
        P(None, fsdp),
        P(fsdp, None),
        P(None, fsdp),
        P(None, fsdp),
        rows,
    )
    return jax.shard_map(
        body, mesh=wide, in_specs=in_specs, out_specs=(rows, rows, rows), check_vma=False
    )
```

time: 652 us -> 143 us (0.22); the launches traced: 643 us -> 142 us
  waiting for transfers between devices: 527 us -> 1.78 us
  matrix products: 58.3 us -> 0 us
  blocking collectives: 0 us -> 48.2 us
  starting transfers between devices: 14.6 us -> 51.1 us
  Pallas kernels: 0 us -> 21.9 us
  local copies, waits for them, and re-layouts: 23.6 us -> 3.73 us
    all_gather x4 -> x1, waiting for transfers between devices: 513 us -> 0.01 us  [body(): weights = lax.all_gather(kv_head, ('z', 'c'), axis=0, tiled=False)]
    dot_general x13 -> x0, matrix products: 58.3 us -> none  [the longest x1 14.1 us: body(): jnp.einsum('chqk,ckhd->cqhd', grad_scores, key_heads, preferred_element_t...]
    all_gather x0 -> x2, blocking collectives: none -> 48.2 us  [the longest x1 37.5 us: body(): own = lax.all_gather(ff_unit, 'z', axis=0, tiled=False)]
    ppermute x0 -> x9, starting transfers between devices: none -> 39 us  [the longest x5 25.8 us: swap(): return lax.ppermute(rows, 'c', [(0, 1), (1, 0)])]
    pallas_call x0 -> x3, Pallas kernels: none -> 21.9 us  [the longest x1 11.9 us: attend(): pl.pallas_call(attend_kernel, out_shape=(wide, wide, jax.ShapeDtypeStruct...]
    unnamed x30 -> x6, local copies, waits for them, and re-layouts: 18.3 us -> 1.43 us
    all_to_all x1, waiting for transfers between devices: 11.9 us -> 0.01 us  [body(): recv = lax.all_to_all(outgoing, ('y', 'c'), 0, 0, tiled=True)]
  transfers between devices with their start and end apart: 5 -> 11, of which waited for: 5 -> 1; matrix products, arithmetic and copies ran while one was open for 5% -> 1% of each run, Pallas kernels for 0% -> 7%
where the time goes in v1:
time: 143 us; the launch traced here: 142 us
  starting transfers between devices  51.1 us (36%)
  blocking collectives  48.2 us (34%)
  Pallas kernels  21.9 us (15%)
  between operations  14.3 us (10%)
  local copies, waits for them, and re-layouts  3.73 us (3%)
  waiting for transfers between devices  1.78 us (1%)
  other arithmetic  1.58 us (1%)
    all_gather x1, blocking collectives, body(): own = lax.all_gather(ff_unit, 'z', axis=0, tiled=False)  37.5 us
    ppermute x5, starting transfers between devices, swap(): return lax.ppermute(rows, 'c', [(0, 1), (1, 0)])  25.8 us
    ppermute x4, starting transfers between devices, ring(): return lax.ppermute(rows, ('x', 'y', 'c'), ring_pairs(step))  13.2 us
    all_to_all x1, starting transfers between devices, body(): recv = lax.all_to_all(outgoing, ('y', 'c'), 0, 0, tiled=True)  12.1 us
    pallas_call x1, Pallas kernels, attend(): pl.pallas_call(attend_kernel, out_shape=(wide, wide, jax.ShapeDtypeStruct...  11.9 us
    all_gather x1, blocking collectives, body(): lax.all_gather(jnp.concatenate([kv_unit, quarter]), 'x', axis=0, tiled=Fa...  10.6 us
    pallas_call x1, Pallas kernels, encode(): pl.pallas_call(encode_kernel, out_shape=jax.ShapeDtypeStruct((ROWS, E), j...  7.86 us
  transfers between devices with their start and end apart: 11, of which 1 were waited for; matrix products, arithmetic and copies ran while one was open for 1% of the time, Pallas kernels for 7%

profile of v1, /device:TPU:1, one launch (start us, length us, event | category | flops | bytes accessed | tf_op | source)
XLA Modules:
  0.0 142.5 jit_solution(13685922759094430878)
XLA Ops:
  7.2 0.0 copy-start.2
  7.2 0.0 all-gather.4.cloned.1.call-start
  7.2 0.8 fusion.7
  8.1 0.8 select_bitcast_fusion
  9.0 10.6 %all-gather = bf16[160,896]{1,0:T(8,128)(2,1)S(1)} all-gather(bf16[40,896]{1,0:T(8,128)(2,1)S(1)} %fusion.3), channel_id=2, replica_groups=mesh['z'=16,'x'=4,'y'=4,'c'=2] {'x'}, dimensions={0}, use_global_device_ids=true | all-gather | bytes 358400 | tf_op jit(solution)/shard_map/all_gather | solution.py:268
  19.6 0.7 slice.37
  20.3 0.0 all-gather.4.cloned.1.call-update
  20.4 0.7 broadcast_subtract_fusion
  21.0 0.7 concatenate.12.meta
  21.7 2.0 %send_blocks.1 = bf16[8,64,896]{2,1,0:T(8,128)(2,1)} custom-call(s32[36]{0:T(128)} %concatenate.12.meta, bf16[4,64,896]{2,1,0:T(8,128)(2,1)} %bitcast.22), custom_call_target="tpu_custom_call" | custom-call | tf_op jit(solution)/shard_map/send_blocks/pallas_call | solution.py:56
  23.8 12.1 %all-to-all-start = ((bf16[8,64,896]{2,1,0:T(8,128)(2,1)}), bf16[8,64,896]{2,1,0:T(8,128)(2,1)S(1)}, u32[]{:S(2)}, u32[]{:S(2)}) async-start(bf16[8,64,896]{2,1,0:T(8,128)(2,1)} %send_blocks.1), calls=%async_computation | async-start | bytes 1835008 | tf_op jit(solution)/shard_map/all_to_all | solution.py:275
  35.8 37.5 %all-gather.1 = bf16[512,896]{1,0:T(8,128)(2,1)S(1)} all-gather(bf16[32,896]{1,0:T(8,128)(2,1)S(1)} %fusion.5), channel_id=3, replica_groups=mesh['z'=16,'x'=4,'y'=4,'c'=2] {'z'}, dimensions={0}, use_global_device_ids=true | all-gather | bytes 974848 | tf_op jit(solution)/shard_map/all_gather | solution.py:276
  73.4 0.0 all-to-all-done.recv_ref
  73.4 3.6 %collective-permute-start = (bf16[16,32,896]{2,1,0:T(8,128)(2,1)S(1)}, bf16[16,32,896]{2,1,0:T(8,128)(2,1)S(1)}, u32[]{:S(2)}, u32[]{:S(2)}) collective-permute-start(bf16[16,32,896]{2,1,0:T(8,128)(2,1)S(1)} %bitcast.15), channel_id=1, source_target_pairs={{0,2},{1,9},{2,4},{3,11},{4,6},{5,13},{6,0},{7,15},{8,10},{9,17},{... | collective-permute-start | bytes 2752520 | tf_op jit(solution)/shard_map/ppermute | solution.py:43
  77.0 3.1 %collective-permute-start.1 = (bf16[16,32,896]{2,1,0:T(8,128)(2,1)S(1)}, bf16[16,32,896]{2,1,0:T(8,128)(2,1)S(1)}, u32[]{:S(2)}, u32[]{:S(2)}) collective-permute-start(bf16[16,32,896]{2,1,0:T(8,128)(2,1)S(1)} %bitcast.16), channel_id=1, source_target_pairs={{0,6},{1,25},{2,0},{3,27},{4,2},{5,29},{6,4},{7,31},{8,14},{9,1},{... | collective-permute-start | bytes 2752520 | tf_op jit(solution)/shard_map/ppermute | solution.py:43
  80.1 9.5 %collective-permute-start.4 = (bf16[16,32,896]{2,1,0:T(8,128)(2,1)S(1)}, bf16[16,32,896]{2,1,0:T(8,128)(2,1)S(1)}, u32[]{:S(2)}, u32[]{:S(2)}) collective-permute-start(bf16[16,32,896]{2,1,0:T(8,128)(2,1)S(1)} %bitcast.17), channel_id=1, source_target_pairs={{0,1},{1,0},{2,3},{3,2},{4,5},{5,4},{6,7},{7,6},{8,9},{9,8},{10,11... | collective-permute-start | bytes 2752520 | tf_op jit(solution)/shard_map/ppermute | solution.py:47
  89.6 0.0 collective-permute-done.o1
  89.6 2.3 %collective-permute-start.2 = (bf16[8,32,896]{2,1,0:T(8,128)(2,1)S(1)}, bf16[8,32,896]{2,1,0:T(8,128)(2,1)S(1)}, u32[]{:S(2)}, u32[]{:S(2)}) collective-permute-start(bf16[8,32,896]{2,1,0:T(8,128)(2,1)S(1)} %slice.35), channel_id=1, source_target_pairs={{0,2},{1,9},{2,4},{3,11},{4,6},{5,13},{6,0},{7,15},{8,10},{9,17},{... | collective-permute-start | bytes 1376264 | tf_op jit(solution)/shard_map/ppermute | solution.py:43
  92.0 0.0 collective-permute-done.1.o2
  92.0 4.2 %collective-permute-start.3 = (bf16[8,32,896]{2,1,0:T(8,128)(2,1)S(1)}, bf16[8,32,896]{2,1,0:T(8,128)(2,1)S(1)}, u32[]{:S(2)}, u32[]{:S(2)}) collective-permute-start(bf16[8,32,896]{2,1,0:T(8,128)(2,1)S(1)} %slice.36), channel_id=1, source_target_pairs={{0,6},{1,25},{2,0},{3,27},{4,2},{5,29},{6,4},{7,31},{8,14},{9,1},{... | collective-permute-start | bytes 1376264 | tf_op jit(solution)/shard_map/ppermute | solution.py:43
  96.2 10.0 %collective-permute-start.5 = (bf16[16,32,896]{2,1,0:T(8,128)(2,1)S(1)}, bf16[16,32,896]{2,1,0:T(8,128)(2,1)S(1)}, u32[]{:S(2)}, u32[]{:S(2)}) collective-permute-start(bf16[16,32,896]{2,1,0:T(8,128)(2,1)S(1)} %collective-permute-done.o1), channel_id=1, source_target_pairs={{0,1},{1,0},{2,3},{3,2},{4,5},{5,4},{6,7},{7,6},{8,9},{9,8},{10,11... | collective-permute-start | bytes 2752520 | tf_op jit(solution)/shard_map/ppermute | solution.py:47
  106.2 1.9 %collective-permute-start.6 = (bf16[16,32,896]{2,1,0:T(8,128)(2,1)S(1)}, bf16[16,32,896]{2,1,0:T(8,128)(2,1)S(1)}, u32[]{:S(2)}, u32[]{:S(2)}) collective-permute-start(bf16[16,32,896]{2,1,0:T(8,128)(2,1)S(1)} %collective-permute-done.1.o2), channel_id=1, source_target_pairs={{0,1},{1,0},{2,3},{3,2},{4,5},{5,4},{6,7},{7,6},{8,9},{9,8},{10,11... | collective-permute-start | bytes 2752520 | tf_op jit(solution)/shard_map/ppermute | solution.py:47
  108.1 0.0 collective-permute-done.2.o3
  108.1 2.5 %collective-permute-start.7 = (bf16[8,32,896]{2,1,0:T(8,128)(2,1)S(1)}, bf16[8,32,896]{2,1,0:T(8,128)(2,1)S(1)}, u32[]{:S(2)}, u32[]{:S(2)}) collective-permute-start(bf16[8,32,896]{2,1,0:T(8,128)(2,1)S(1)} %collective-permute-done.2.o3), channel_id=1, source_target_pairs={{0,1},{1,0},{2,3},{3,2},{4,5},{5,4},{6,7},{7,6},{8,9},{9,8},{10,11... | collective-permute-start | bytes 1376264 | tf_op jit(solution)/shard_map/ppermute | solution.py:47
  110.6 0.0 collective-permute-done.3.o4
  110.6 1.9 %collective-permute-start.8 = (bf16[8,32,896]{2,1,0:T(8,128)(2,1)S(1)}, bf16[8,32,896]{2,1,0:T(8,128)(2,1)S(1)}, u32[]{:S(2)}, u32[]{:S(2)}) collective-permute-start(bf16[8,32,896]{2,1,0:T(8,128)(2,1)S(1)} %collective-permute-done.3.o4), channel_id=1, source_target_pairs={{0,1},{1,0},{2,3},{3,2},{4,5},{5,4},{6,7},{7,6},{8,9},{9,8},{10,11... | collective-permute-start | bytes 1376264 | tf_op jit(solution)/shard_map/ppermute | solution.py:47
  112.6 0.0 copy-done.2
  112.6 0.0 collective-permute-done.4.s0
  112.6 0.0 collective-permute-done.7.s3
  112.6 1.7 %collective-permute-done.8.s4 = bf16[8,32,896]{2,1,0:T(8,128)(2,1)S(1)} collective-permute-done((bf16[8,32,896]{2,1,0:T(8,128)(2,1)S(1)}, bf16[8,32,896]{2,1,0:T(8,128)(2,1)S(1)}, u32[]{:S(2)}, u32[]{:S(2)}) %collective-permute-start.8) | collective-permute-done | bytes 458784 | tf_op jit(solution)/shard_map/ppermute | solution.py:47
  114.3 0.0 collective-permute-done.5.s1
  114.3 0.0 collective-permute-done.6.s2
  114.3 0.0 copy-start.1
  114.3 0.7 copy-done.1
  115.0 7.9 %encode_rows.1.enc_ref = bf16[256,896]{1,0:T(8,128)(2,1)S(1)} custom-call(s32[36]{0:T(128)S(1)} %copy-done.1, bf16[8,64,896]{2,1,0:T(8,128)(2,1)S(1)} %all-to-all-done.recv_ref, f32[1,896]{1,0:T(1,128)S(1)} %reshape.17.gain_ref, bf16[16,32,896]{2,1,0:T(8,128)(2,1)S(1)} %bitcast.18, bf16[16,32,896]{2,1,0:T(8,128)(2,1)S(1)} %collective-permute-done.o1, ...), custom_call_target="tpu_custom_call" | custom-call | tf_op jit(solution)/shard_map/encode_rows/pallas_call | solution.py:145
  122.9 0.0 copy-start
  122.9 0.8 copy-done
  123.6 0.0 all-gather.4.cloned.1.call-done.w_hbm
  123.6 11.9 %attend_spans.1 = (bf16[128,2048]{1,0:T(8,128)(2,1)}, bf16[128,2048]{1,0:T(8,128)(2,1)}, bf16[256,896]{1,0:T(8,128)(2,1)}) custom-call(bf16[256,896]{1,0:T(8,128)(2,1)} %copy-done, bf16[32,128,896]{2,1,0:T(8,128)(2,1)} %all-gather.4.cloned.1.call-done.w_hbm, bf16[128,2048]{1,0:T(8,128)(2,1)} %q_hbm.1, bf16[128,2048]{1,0:T(8,128)(2,1)} %g_hbm.1), custom_call_target="tpu_custom_call" | custom-call | tf_op jit(solution)/shard_map/attend_spans/pallas_call | solution.py:234
  (6 shorter events, 0.2 us)
Async XLA Ops:
  7.2 105.4 %copy-start.2 = (f32[896]{0:T(1024)S(1)}, f32[896]{0:T(1024)}, u32[]{:S(2)}) copy-start(f32[896]{0:T(1024)} %param.12) | copy-start | bytes 10756
  7.2 116.5 %all-gather.4.cloned.1.call-start = ((), (), s32[]{:S(2)}) async-start(), calls=%async_computation.1 | async-start | bytes 7569408 | tf_op jit(solution)/shard_map/all_gather | solution.py:270
  23.8 49.6 %all-to-all-start = ((bf16[8,64,896]{2,1,0:T(8,128)(2,1)}), bf16[8,64,896]{2,1,0:T(8,128)(2,1)S(1)}, u32[]{:S(2)}, u32[]{:S(2)}) async-start(bf16[8,64,896]{2,1,0:T(8,128)(2,1)} %send_blocks.1), calls=%async_computation | async-start | bytes 1835008 | tf_op jit(solution)/shard_map/all_to_all | solution.py:275
  73.4 16.2 %collective-permute-start = (bf16[16,32,896]{2,1,0:T(8,128)(2,1)S(1)}, bf16[16,32,896]{2,1,0:T(8,128)(2,1)S(1)}, u32[]{:S(2)}, u32[]{:S(2)}) collective-permute-start(bf16[16,32,896]{2,1,0:T(8,128)(2,1)S(1)} %bitcast.15), channel_id=1, source_target_pairs={{0,2},{1,9},{2,4},{3,11},{4,6},{5,13},{6,0},{7,15},{8,10},{9,17},{... | collective-permute-start | bytes 2752520 | tf_op jit(solution)/shard_map/ppermute | solution.py:43
  77.0 15.0 %collective-permute-start.1 = (bf16[16,32,896]{2,1,0:T(8,128)(2,1)S(1)}, bf16[16,32,896]{2,1,0:T(8,128)(2,1)S(1)}, u32[]{:S(2)}, u32[]{:S(2)}) collective-permute-start(bf16[16,32,896]{2,1,0:T(8,128)(2,1)S(1)} %bitcast.16), channel_id=1, source_target_pairs={{0,6},{1,25},{2,0},{3,27},{4,2},{5,29},{6,4},{7,31},{8,14},{9,1},{... | collective-permute-start | bytes 2752520 | tf_op jit(solution)/shard_map/ppermute | solution.py:43
  80.1 32.5 %collective-permute-start.4 = (bf16[16,32,896]{2,1,0:T(8,128)(2,1)S(1)}, bf16[16,32,896]{2,1,0:T(8,128)(2,1)S(1)}, u32[]{:S(2)}, u32[]{:S(2)}) collective-permute-start(bf16[16,32,896]{2,1,0:T(8,128)(2,1)S(1)} %bitcast.17), channel_id=1, source_target_pairs={{0,1},{1,0},{2,3},{3,2},{4,5},{5,4},{6,7},{7,6},{8,9},{9,8},{10,11... | collective-permute-start | bytes 2752520 | tf_op jit(solution)/shard_map/ppermute | solution.py:47
  89.6 18.5 %collective-permute-start.2 = (bf16[8,32,896]{2,1,0:T(8,128)(2,1)S(1)}, bf16[8,32,896]{2,1,0:T(8,128)(2,1)S(1)}, u32[]{:S(2)}, u32[]{:S(2)}) collective-permute-start(bf16[8,32,896]{2,1,0:T(8,128)(2,1)S(1)} %slice.35), channel_id=1, source_target_pairs={{0,2},{1,9},{2,4},{3,11},{4,6},{5,13},{6,0},{7,15},{8,10},{9,17},{... | collective-permute-start | bytes 1376264 | tf_op jit(solution)/shard_map/ppermute | solution.py:43
  92.0 18.6 %collective-permute-start.3 = (bf16[8,32,896]{2,1,0:T(8,128)(2,1)S(1)}, bf16[8,32,896]{2,1,0:T(8,128)(2,1)S(1)}, u32[]{:S(2)}, u32[]{:S(2)}) collective-permute-start(bf16[8,32,896]{2,1,0:T(8,128)(2,1)S(1)} %slice.36), channel_id=1, source_target_pairs={{0,6},{1,25},{2,0},{3,27},{4,2},{5,29},{6,4},{7,31},{8,14},{9,1},{... | collective-permute-start | bytes 1376264 | tf_op jit(solution)/shard_map/ppermute | solution.py:43
  96.2 18.1 %collective-permute-start.5 = (bf16[16,32,896]{2,1,0:T(8,128)(2,1)S(1)}, bf16[16,32,896]{2,1,0:T(8,128)(2,1)S(1)}, u32[]{:S(2)}, u32[]{:S(2)}) collective-permute-start(bf16[16,32,896]{2,1,0:T(8,128)(2,1)S(1)} %collective-permute-done.o1), channel_id=1, source_target_pairs={{0,1},{1,0},{2,3},{3,2},{4,5},{5,4},{6,7},{7,6},{8,9},{9,8},{10,11... | collective-permute-start | bytes 2752520 | tf_op jit(solution)/shard_map/ppermute | solution.py:47
  106.2 8.2 %collective-permute-start.6 = (bf16[16,32,896]{2,1,0:T(8,128)(2,1)S(1)}, bf16[16,32,896]{2,1,0:T(8,128)(2,1)S(1)}, u32[]{:S(2)}, u32[]{:S(2)}) collective-permute-start(bf16[16,32,896]{2,1,0:T(8,128)(2,1)S(1)} %collective-permute-done.1.o2), channel_id=1, source_target_pairs={{0,1},{1,0},{2,3},{3,2},{4,5},{5,4},{6,7},{7,6},{8,9},{9,8},{10,11... | collective-permute-start | bytes 2752520 | tf_op jit(solution)/shard_map/ppermute | solution.py:47
  108.1 4.5 %collective-permute-start.7 = (bf16[8,32,896]{2,1,0:T(8,128)(2,1)S(1)}, bf16[8,32,896]{2,1,0:T(8,128)(2,1)S(1)}, u32[]{:S(2)}, u32[]{:S(2)}) collective-permute-start(bf16[8,32,896]{2,1,0:T(8,128)(2,1)S(1)} %collective-permute-done.2.o3), channel_id=1, source_target_pairs={{0,1},{1,0},{2,3},{3,2},{4,5},{5,4},{6,7},{7,6},{8,9},{9,8},{10,11... | collective-permute-start | bytes 1376264 | tf_op jit(solution)/shard_map/ppermute | solution.py:47
  110.6 3.7 %collective-permute-start.8 = (bf16[8,32,896]{2,1,0:T(8,128)(2,1)S(1)}, bf16[8,32,896]{2,1,0:T(8,128)(2,1)S(1)}, u32[]{:S(2)}, u32[]{:S(2)}) collective-permute-start(bf16[8,32,896]{2,1,0:T(8,128)(2,1)S(1)} %collective-permute-done.3.o4), channel_id=1, source_target_pairs={{0,1},{1,0},{2,3},{3,2},{4,5},{5,4},{6,7},{7,6},{8,9},{9,8},{10,11... | collective-permute-start | bytes 1376264 | tf_op jit(solution)/shard_map/ppermute | solution.py:47
  114.3 0.7 copy-start.1
  122.9 0.8 copy-start
Sparse Core Ops, SparseCore 0:
  20.5 88.2 all-gather.3

commit v2 on v1

v2 whole, which is shorter than its diff:
```python
import jax
import jax.numpy as jnp
from jax import lax
from jax.experimental import pallas as pl
from jax.experimental.pallas import tpu as pltpu
from jax.sharding import Mesh, PartitionSpec as P

E = 896
HEADS = 16
HD = 128
CL = 64
NLEN = 64
NPC = 2
CH_DEV = 2
NZ, NX, NY, NC = 16, 4, 4, 2
PER_DEV = CH_DEV * NPC
ROWS = PER_DEV * NLEN
UNITS = 28
HALF = UNITS // 2
QUART = UNITS // 4
EPS = 1e-06
SCALE = HD ** (-0.5)
ALL = ("z", "x", "y", "c")
NT = (((1,), (1,)), ((), ()))
NN = (((1,), (0,)), ((), ()))
TN = (((0,), (0,)), ((), ()))


def dot(a, b, dims):
    return lax.dot_general(a, b, dims, preferred_element_type=jnp.float32)


def ring_pairs(step):
    pairs = []
    for x in range(NX):
        for y in range(NY):
            pairs.append(((x * NY + y) * NC, (x * NY + (y + step) % NY) * NC))
            pairs.append(((x * NY + y) * NC + 1, ((x + step) % NX * NY + y) * NC + 1))
    return pairs


def ring(rows, step):
    return lax.ppermute(rows, ("x", "y", "c"), ring_pairs(step))


def swap(rows):
    return lax.ppermute(rows, "c", [(0, 1), (1, 0)])


def send_kernel(meta, raw_ref, out_ref):
    for i in range(PER_DEV):
        out_ref[meta[PER_DEV * meta[32] + i] // PER_DEV] = raw_ref[i]


def send_blocks(meta, raw):
    return pl.pallas_call(
        send_kernel,
        out_shape=jax.ShapeDtypeStruct((NY * NC, NLEN, E), jnp.bfloat16),
        in_specs=[
            pl.BlockSpec(memory_space=pltpu.SMEM),
            pl.BlockSpec(memory_space=pltpu.VMEM),
        ],
        out_specs=pl.BlockSpec(memory_space=pltpu.VMEM),
        compiler_params=pltpu.CompilerParams(vmem_limit_bytes=8 * 1024 * 1024),
        name="send_blocks",
    )(meta, raw)


def gelu(x):
    return 0.5 * x * (1.0 + jnp.tanh(0.7978845608028654 * (x + 0.044715 * (x * x * x))))


def place_kernel(meta, recv_ref, gain_ref, raw_ref, normed_ref):
    first = PER_DEV * meta[32]
    for n in range(NY * NC * PER_DEV):
        slot = meta[n] - first

        @pl.when((slot >= 0) & (slot < PER_DEV))
        def _():
            raw_ref[slot] = recv_ref[n // PER_DEV]

    floats = raw_ref[...].astype(jnp.float32)
    mean = jnp.mean(floats * floats, axis=-1, keepdims=True)
    normed_ref[...] = (floats * lax.rsqrt(mean + EPS) * gain_ref[...]).astype(jnp.bfloat16)


def place(meta, recv, gain):
    vmem = pl.BlockSpec(memory_space=pltpu.VMEM)
    rows = jax.ShapeDtypeStruct((PER_DEV, NLEN, E), jnp.bfloat16)
    return pl.pallas_call(
        place_kernel,
        out_shape=(rows, rows),
        in_specs=[pl.BlockSpec(memory_space=pltpu.SMEM), vmem, vmem],
        out_specs=(vmem, vmem),
        compiler_params=pltpu.CompilerParams(vmem_limit_bytes=8 * 1024 * 1024),
        name="place_rows",
    )(meta, recv, gain)


def both_cores(mine, other):
    return jnp.concatenate([mine[...].reshape(ROWS, E), other[...].reshape(ROWS, E)])


def blocks_y(pairs):
    return [(up[...].reshape(256, E), down[...].reshape(256, E)) for up, down in pairs]


def blocks_x(pieces):
    out = []
    for one, two in zip(pieces[::2], pieces[1::2]):
        ups, downs = [], []
        for piece in (one, two):
            ups.append(piece[:, 0:16].reshape(128, E))
            downs.append(piece[:, 16:32].reshape(128, E))
        out.append((jnp.concatenate(ups), jnp.concatenate(downs)))
    return out


def multiply(normed, blocks):
    total = None
    for up, down in blocks:
        hidden = gelu(dot(normed, up, NT)).astype(jnp.bfloat16)
        part = dot(hidden, down, NN)
        total = part if total is None else total + part
    return total


def by_case(meta, even, odd, x_pieces, write):
    core, parity = meta[33], meta[34] % 2

    @pl.when((core == 0) & (parity == 0))
    def _():
        write(blocks_y(even))

    @pl.when((core == 0) & (parity == 1))
    def _():
        write(blocks_y(odd))

    @pl.when(core != 0)
    def _():
        write(blocks_x(x_pieces))


def early_kernel(meta, mine, other, own_a, own_b, left_a, left_b, right_a, right_b, acc_ref):
    normed = both_cores(mine, other)

    def write(blocks):
        acc_ref[...] = multiply(normed, blocks)

    by_case(
        meta,
        ((own_a, right_a), (own_b, right_b)),
        ((left_a, own_a), (left_b, own_b)),
        (own_a, own_b, left_a, left_b, right_a, right_b),
        write,
    )


def late_kernel(
    meta, mine, other, acc, left_a, left_b, right_a, right_b, far_a, far_b, mine_ref, other_ref
):
    normed = both_cores(mine, other)

    def write(blocks):
        total = acc[...] + multiply(normed, blocks)
        mine_ref[...] = total[:ROWS]
        other_ref[...] = total[ROWS:]

    by_case(
        meta,
        ((far_a, left_a), (far_b, left_b)),
        ((right_a, far_a), (right_b, far_b)),
        (far_a, far_b),
        write,
    )


def encode_part(kernel, outs, meta, *arrays):
    vmem = pl.BlockSpec(memory_space=pltpu.VMEM)
    return pl.pallas_call(
        kernel,
        out_shape=outs,
        in_specs=[pl.BlockSpec(memory_space=pltpu.SMEM)] + [vmem] * len(arrays),
        out_specs=jax.tree.map(lambda _: vmem, outs),
        compiler_params=pltpu.CompilerParams(vmem_limit_bytes=28 * 1024 * 1024),
        name=kernel.__name__,
    )(meta, *arrays)


GROUP = 4
CHUNK = 4
CUT = 2 * GROUP
LAST = 256
LIMIT = 48 * 1024 * 1024


def attend_kernel(
    raw_ref, mine_ref, other_ref, w_hbm, q_hbm, g_hbm, att_hbm, gq_hbm, ge_ref, w, q_ref, g_ref, kv, gkv, att, gq, sems, outs
):
    def fetch(i):
        return pltpu.make_async_copy(
            w_hbm.at[i * CUT : (i + 1) * CUT], w.at[i * CUT : (i + 1) * CUT], sems.at[i]
        )

    loads = [fetch(i) for i in range(2 * HEADS // CUT)]
    loads.append(pltpu.make_async_copy(q_hbm, q_ref, sems.at[len(loads)]))
    loads.append(pltpu.make_async_copy(g_hbm, g_ref, sems.at[len(loads)]))
    for copy in loads:
        copy.start()

    floats = raw_ref[...].reshape(ROWS, E).astype(jnp.float32)
    enc = (floats + (mine_ref[...] + other_ref[...])).astype(jnp.bfloat16)
    first = lax.broadcasted_iota(jnp.int32, (NPC * NLEN, CH_DEV * CL), 1) < CL
    half = NPC * NLEN

    def fold(full):
        return jnp.where(first, full[:half], full[half:])

    def spread(part):
        zero = jnp.zeros_like(part)
        return jnp.concatenate([jnp.where(first, part, zero), jnp.where(first, zero, part)])

    for base in range(0, HEADS, GROUP):
        loads[base // GROUP].wait()
        for j in range(2 * base, 2 * (base + GROUP), CHUNK):
            rows = w[j : j + CHUNK].reshape(CHUNK * HD, E)
            kv[:, j * HD : (j + CHUNK) * HD] = dot(enc, rows, NT).astype(jnp.bfloat16)
        if base == 0:
            loads[-2].wait()
            loads[-1].wait()
        heads = range(base, base + GROUP)
        cols = [slice(h * HD, (h + 1) * HD) for h in heads]
        kcols = [slice(2 * h * HD, (2 * h + 1) * HD) for h in heads]
        vcols = [slice((2 * h + 1) * HD, (2 * h + 2) * HD) for h in heads]
        scores = [fold(dot(kv[:, k], q_ref[:, c], NT)) * SCALE for c, k in zip(cols, kcols)]
        grad_probs = [fold(dot(kv[:, v], g_ref[:, c], NT)) for c, v in zip(cols, vcols)]
        exponent = [jnp.exp(s - jnp.max(s, axis=0, keepdims=True)) for s in scores]
        probs = [e * (1.0 / jnp.sum(e, axis=0, keepdims=True)) for e in exponent]
        delta = [jnp.sum(p * gp, axis=0, keepdims=True) for p, gp in zip(probs, grad_probs)]
        low = [spread(p).astype(jnp.bfloat16) for p in probs]
        grad_scores = [
            spread(p * (gp - d) * SCALE).astype(jnp.bfloat16)
            for p, gp, d in zip(probs, grad_probs, delta)
        ]
        for i, (c, k, v) in enumerate(zip(cols, kcols, vcols)):
            att[:, c] = dot(low[i], kv[:, v], TN).astype(jnp.bfloat16)
            gkv[:, v] = dot(low[i], g_ref[:, c], NN).astype(jnp.bfloat16)
            gq[:, c] = dot(grad_scores[i], kv[:, k], TN).astype(jnp.bfloat16)
            gkv[:, k] = dot(grad_scores[i], q_ref[:, c], NN).astype(jnp.bfloat16)
    stores = [
        pltpu.make_async_copy(att, att_hbm, outs.at[0]),
        pltpu.make_async_copy(gq, gq_hbm, outs.at[1]),
    ]
    for copy in stores:
        copy.start()
    rows = w[...].reshape(2 * HEADS * HD, E)
    for j in range(0, E, LAST):
        wide = slice(j, min(j + LAST, E))
        ge_ref[:, wide] = dot(gkv[...], rows[:, wide], NN).astype(jnp.bfloat16)
    for copy in stores:
        copy.wait()


def attend(raw, mine, other, weights, queries, grads):
    tokens = CH_DEV * CL
    hbm = pl.BlockSpec(memory_space=pltpu.HBM)
    vmem = pl.BlockSpec(memory_space=pltpu.VMEM)
    wide = jax.ShapeDtypeStruct((tokens, HEADS * HD), jnp.bfloat16)
    full = pltpu.VMEM((tokens, HEADS * HD), jnp.bfloat16)
    both = pltpu.VMEM((ROWS, 2 * HEADS * HD), jnp.bfloat16)
    return pl.pallas_call(
        attend_kernel,
        out_shape=(wide, wide, jax.ShapeDtypeStruct((ROWS, E), jnp.bfloat16)),
        in_specs=[vmem, vmem, vmem, hbm, hbm, hbm],
        out_specs=(hbm, hbm, vmem),
        scratch_shapes=[
            pltpu.VMEM((2 * HEADS, HD, E), jnp.bfloat16),
            full,
            full,
            both,
            both,
            full,
            full,
            pltpu.SemaphoreType.DMA((2 * HEADS // CUT + 2,)),
            pltpu.SemaphoreType.DMA((2,)),
        ],
        compiler_params=pltpu.CompilerParams(vmem_limit_bytes=LIMIT),
        name="attend_spans",
    )(raw, mine, other, weights, queries, grads)


def body(queries, neighbours, slots, gain, up, down, key_proj, value_proj, grads):
    z, x, y, c = (lax.axis_index(name) for name in ALL)
    group = NY * NC * PER_DEV
    here = jnp.stack([y * NC + c, c, y, x]).astype(jnp.int32)
    meta = jnp.concatenate([slots - (z * NX + x) * group, here])

    up = up.T
    kv_unit = jnp.where(c == 0, key_proj.T, value_proj.T)
    halves = jnp.concatenate([up[:QUART], down[:QUART], up[QUART:HALF], down[QUART:HALF]])
    quarter = jnp.pad(lax.dynamic_slice_in_dim(halves, y * QUART, QUART), ((0, 1), (0, 0)))
    pad = ((0, 16 - HALF), (0, 0))
    whole = jnp.concatenate([jnp.pad(up[HALF:], pad), jnp.pad(down[HALF:], pad)])

    along_x = lax.all_gather(jnp.concatenate([kv_unit, quarter]), "x", axis=0, tiled=False)
    kv_head = along_x[:, :32].reshape(HD, E)
    weights = lax.all_gather(kv_head, ("z", "c"), axis=0, tiled=False)

    outgoing = send_blocks(meta, neighbours.reshape(PER_DEV, NLEN, E))
    ff_unit = jnp.where(c == 0, along_x[:, 32:].reshape(32, E), whole)
    ff_unit, outgoing = lax.optimization_barrier((ff_unit, outgoing))
    recv = lax.all_to_all(outgoing, ("y", "c"), 0, 0, tiled=True)
    own = lax.all_gather(ff_unit, "z", axis=0, tiled=False)
    own, recv = lax.optimization_barrier((own, recv))
    raw, normed = place(meta, recv, gain.reshape(1, E))
    other = swap(normed)
    own_a, own_b = own[: NZ // 2], own[NZ // 2 :]
    left_a, right_b = ring(own_a, 1), ring(own_b, -1)
    left_b, right_a = ring(own_b, 1), ring(own_a, -1)
    far_a, far_b = ring(left_a, 1), ring(right_b, -1)
    near = (left_a, left_b, right_a, right_b)
    one = jax.ShapeDtypeStruct((ROWS, E), jnp.float32)
    two = jax.ShapeDtypeStruct((2 * ROWS, E), jnp.float32)
    acc = encode_part(early_kernel, two, meta, normed, other, own_a, own_b, *near)
    mine, given = encode_part(
        late_kernel, (one, one), meta, normed, other, acc, *near, far_a, far_b
    )
    return attend(raw, mine, swap(given), weights, queries, grads)


def solution(mesh):
    wide = Mesh(mesh.devices.reshape(NZ, NX, NY, NC), ALL)
    rows = P(ALL, None)
    fsdp = ("z", "x")
    in_specs = (
        rows,
        rows,
        P(fsdp),
        P(),
        P(None, fsdp),
        P(fsdp, None),
        P(None, fsdp),
        P(None, fsdp),
        rows,
    )
    return jax.shard_map(
        body, mesh=wide, in_specs=in_specs, out_specs=(rows, rows, rows), check_vma=False
    )
```

time: 143 us -> 136 us (0.951)
  starting transfers between devices: 51.1 us -> 42.8 us
  Pallas kernels: 21.9 us -> 17.8 us
  waiting for transfers between devices: 1.78 us -> 4.26 us
  blocking collectives: 48.2 us -> 49.8 us
    ppermute x5 -> x2, starting transfers between devices: 25.8 us -> 11.4 us  [swap(): return lax.ppermute(rows, 'c', [(0, 1), (1, 0)])]
    ppermute x4 -> x6, starting transfers between devices: 13.2 us -> 19.3 us  [ring(): return lax.ppermute(rows, ('x', 'y', 'c'), ring_pairs(step))]
    ppermute x4 -> x6, waiting for transfers between devices: 0.01 us -> 2.34 us  [ring(): return lax.ppermute(rows, ('x', 'y', 'c'), ring_pairs(step))]
    pallas_call x1 -> x3, Pallas kernels: 7.86 us -> 5.99 us  [the longest x2 4.93 us: encode_part(): pl.pallas_call(kernel, out_shape=outs, in_specs=[pl.BlockSpec(memory_spac...]
    pallas_call x1, Pallas kernels: 11.9 us -> 10.2 us  [attend(): pl.pallas_call(attend_kernel, out_shape=(wide, wide, jax.ShapeDtypeStruct...]
    all_gather x1, blocking collectives: 37.5 us -> 39.2 us  [body(): own = lax.all_gather(ff_unit, 'z', axis=0, tiled=False)]
    slice x3 -> x4, local copies, waits for them, and re-layouts: 0.92 us -> 2.51 us  [the longest x1 0.84 us: body(): down[QUART:HALF]]
  transfers between devices with their start and end apart: 11 -> 10, of which waited for: 1 -> 3; matrix products, arithmetic and copies ran while one was open for 1% -> 2% of each run, Pallas kernels for 7% -> 6%
where the time goes in v2:
time: 136 us; the launch traced here: 135 us
  blocking collectives  49.8 us (37%)
  starting transfers between devices  42.8 us (31%)
  Pallas kernels  17.8 us (13%)
  between operations  14.3 us (11%)
  local copies, waits for them, and re-layouts  4.34 us (3%)
  waiting for transfers between devices  4.26 us (3%)
  other arithmetic  1.6 us (1%)
    all_gather x1, blocking collectives, body(): own = lax.all_gather(ff_unit, 'z', axis=0, tiled=False)  39.2 us
    ppermute x6, starting transfers between devices, ring(): return lax.ppermute(rows, ('x', 'y', 'c'), ring_pairs(step))  19.3 us
    all_to_all x1, starting transfers between devices, body(): recv = lax.all_to_all(outgoing, ('y', 'c'), 0, 0, tiled=True)  12.1 us
    ppermute x2, starting transfers between devices, swap(): return lax.ppermute(rows, 'c', [(0, 1), (1, 0)])  11.4 us
    all_gather x1, blocking collectives, body(): lax.all_gather(jnp.concatenate([kv_unit, quarter]), 'x', axis=0, tiled=Fa...  10.6 us
    pallas_call x1, Pallas kernels, attend(): pl.pallas_call(attend_kernel, out_shape=(wide, wide, jax.ShapeDtypeStruct...  10.2 us
    pallas_call x2, Pallas kernels, encode_part(): pl.pallas_call(kernel, out_shape=outs, in_specs=[pl.BlockSpec(memory_spac...  4.93 us
  transfers between devices with their start and end apart: 10, of which 3 were waited for; matrix products, arithmetic and copies ran while one was open for 2% of the time, Pallas kernels for 6%

profile of v2, /device:TPU:1, one launch (start us, length us, event | category | flops | bytes accessed | tf_op | source)
XLA Modules:
  0.0 134.8 jit_solution(17585788305729621396)
XLA Ops:
  7.2 0.0 copy-start.3
  7.2 0.0 all-gather.4.cloned.1.call-start
  7.2 0.8 fusion.10
  8.1 0.8 select_bitcast_fusion
  8.9 0.1 fusion.8
  9.0 10.6 %all-gather = bf16[160,896]{1,0:T(8,128)(2,1)S(1)} all-gather(bf16[40,896]{1,0:T(8,128)(2,1)S(1)} %fusion.3), channel_id=2, replica_groups=mesh['z'=16,'x'=4,'y'=4,'c'=2] {'x'}, dimensions={0}, use_global_device_ids=true | all-gather | bytes 358400 | tf_op jit(solution)/shard_map/all_gather | solution.py:305
  19.6 0.7 slice.44
  20.3 0.0 all-gather.4.cloned.1.call-update
  20.3 0.8 slice.43
  21.1 0.8 slice.36
  22.0 0.7 broadcast_subtract_fusion
  22.6 0.1 concatenate.12.meta
  22.7 0.0 copy-start.2
  22.7 1.0 copy-done.2
  23.7 1.6 %send_blocks.1 = bf16[8,64,896]{2,1,0:T(8,128)(2,1)} custom-call(s32[36]{0:T(128)S(1)} %concatenate.12.meta, bf16[4,64,896]{2,1,0:T(8,128)(2,1)S(1)} %bitcast.15), custom_call_target="tpu_custom_call" | custom-call | tf_op jit(solution)/shard_map/send_blocks/pallas_call | solution.py:56
  25.3 12.1 %all-to-all-start = ((bf16[8,64,896]{2,1,0:T(8,128)(2,1)}), bf16[8,64,896]{2,1,0:T(8,128)(2,1)S(1)}, u32[]{:S(2)}, u32[]{:S(2)}) async-start(bf16[8,64,896]{2,1,0:T(8,128)(2,1)} %send_blocks.1), calls=%async_computation | async-start | bytes 1835008 | tf_op jit(solution)/shard_map/all_to_all | solution.py:312
  37.4 0.0 copy-start
  37.4 0.0 copy-start.1
  37.4 39.2 %all-gather.1 = bf16[512,896]{1,0:T(8,128)(2,1)S(1)} all-gather(bf16[32,896]{1,0:T(8,128)(2,1)S(1)} %fusion.5), channel_id=3, replica_groups=mesh['z'=16,'x'=4,'y'=4,'c'=2] {'z'}, dimensions={0}, use_global_device_ids=true | all-gather | bytes 974848 | tf_op jit(solution)/shard_map/all_gather | solution.py:313
  76.6 0.0 all-to-all-done.recv_ref
  76.6 0.1 fusion.9
  76.6 2.6 %collective-permute-start.1 = (bf16[8,32,896]{2,1,0:T(8,128)(2,1)S(1)}, bf16[8,32,896]{2,1,0:T(8,128)(2,1)S(1)}, u32[]{:S(2)}, u32[]{:S(2)}) collective-permute-start(bf16[8,32,896]{2,1,0:T(8,128)(2,1)S(1)} %get-tuple-element.20.own_a), channel_id=1, source_target_pairs={{0,2},{1,9},{2,4},{3,11},{4,6},{5,13},{6,0},{7,15},{8,10},{9,17},{... | collective-permute-start | bytes 1376264 | tf_op jit(solution)/shard_map/ppermute | solution.py:43
  79.2 3.9 %collective-permute-start.4 = (bf16[8,32,896]{2,1,0:T(8,128)(2,1)S(1)}, bf16[8,32,896]{2,1,0:T(8,128)(2,1)S(1)}, u32[]{:S(2)}, u32[]{:S(2)}) collective-permute-start(bf16[8,32,896]{2,1,0:T(8,128)(2,1)S(1)} %get-tuple-element.19.own_b), channel_id=1, source_target_pairs={{0,6},{1,25},{2,0},{3,27},{4,2},{5,29},{6,4},{7,31},{8,14},{9,1},{... | collective-permute-start | bytes 1376264 | tf_op jit(solution)/shard_map/ppermute | solution.py:43
  83.2 0.0 copy-done.3
  83.2 1.9 %collective-permute-start.2 = (bf16[8,32,896]{2,1,0:T(8,128)(2,1)S(1)}, bf16[8,32,896]{2,1,0:T(8,128)(2,1)S(1)}, u32[]{:S(2)}, u32[]{:S(2)}) collective-permute-start(bf16[8,32,896]{2,1,0:T(8,128)(2,1)S(1)} %get-tuple-element.19.own_b), channel_id=1, source_target_pairs={{0,2},{1,9},{2,4},{3,11},{4,6},{5,13},{6,0},{7,15},{8,10},{9,17},{... | collective-permute-start | bytes 1376264 | tf_op jit(solution)/shard_map/ppermute | solution.py:43
  85.1 1.1 place_rows.1
  86.2 8.2 %collective-permute-start = (bf16[4,64,896]{2,1,0:T(8,128)(2,1)S(1)}, bf16[4,64,896]{2,1,0:T(8,128)(2,1)S(1)}, u32[]{:S(2)}, u32[]{:S(2)}) collective-permute-start(bf16[4,64,896]{2,1,0:T(8,128)(2,1)S(1)} %get-tuple-element.15.mine), channel_id=1, source_target_pairs={{0,1},{1,0},{2,3},{3,2},{4,5},{5,4},{6,7},{7,6},{8,9},{9,8},{10,11... | collective-permute-start | bytes 1376264 | tf_op jit(solution)/shard_map/ppermute | solution.py:47
  94.4 4.4 %collective-permute-start.3 = (bf16[8,32,896]{2,1,0:T(8,128)(2,1)S(1)}, bf16[8,32,896]{2,1,0:T(8,128)(2,1)S(1)}, u32[]{:S(2)}, u32[]{:S(2)}) collective-permute-start(bf16[8,32,896]{2,1,0:T(8,128)(2,1)S(1)} %get-tuple-element.20.own_a), channel_id=1, source_target_pairs={{0,6},{1,25},{2,0},{3,27},{4,2},{5,29},{6,4},{7,31},{8,14},{9,1},{... | collective-permute-start | bytes 1376264 | tf_op jit(solution)/shard_map/ppermute | solution.py:43
  98.8 0.0 collective-permute-done.1.left_a
  98.8 1.9 %collective-permute-start.5 = (bf16[8,32,896]{2,1,0:T(8,128)(2,1)S(1)}, bf16[8,32,896]{2,1,0:T(8,128)(2,1)S(1)}, u32[]{:S(2)}, u32[]{:S(2)}) collective-permute-start(bf16[8,32,896]{2,1,0:T(8,128)(2,1)S(1)} %collective-permute-done.1.left_a), channel_id=1, source_target_pairs={{0,2},{1,9},{2,4},{3,11},{4,6},{5,13},{6,0},{7,15},{8,10},{9,17},{... | collective-permute-start | bytes 1376264 | tf_op jit(solution)/shard_map/ppermute | solution.py:43
  100.8 0.0 collective-permute-done.4.right_b
  100.8 4.6 %collective-permute-start.6 = (bf16[8,32,896]{2,1,0:T(8,128)(2,1)S(1)}, bf16[8,32,896]{2,1,0:T(8,128)(2,1)S(1)}, u32[]{:S(2)}, u32[]{:S(2)}) collective-permute-start(bf16[8,32,896]{2,1,0:T(8,128)(2,1)S(1)} %collective-permute-done.4.right_b), channel_id=1, source_target_pairs={{0,6},{1,25},{2,0},{3,27},{4,2},{5,29},{6,4},{7,31},{8,14},{9,1},{... | collective-permute-start | bytes 1376264 | tf_op jit(solution)/shard_map/ppermute | solution.py:43
  105.4 0.0 collective-permute-done.other
  105.4 0.0 collective-permute-done.2.left_b
  105.4 0.0 collective-permute-done.3.right_a
  105.4 3.0 %early_kernel.1.acc = f32[512,896]{1,0:T(8,128)S(1)} custom-call(s32[36]{0:T(128)S(1)} %concatenate.12.meta, bf16[4,64,896]{2,1,0:T(8,128)(2,1)S(1)} %get-tuple-element.15.mine, bf16[4,64,896]{2,1,0:T(8,128)(2,1)S(1)} %collective-permute-done.other, bf16[8,32,896]{2,1,0:T(8,128)(2,1)S(1)} %get-tuple-element.20.own_a, ...), custom_call_target="tpu_custom_call" | custom-call | tf_op jit(solution)/shard_map/early_kernel/pallas_call | solution.py:180
  108.4 1.1 collective-permute-done.5.far_a
  109.6 1.2 collective-permute-done.6.far_b
  110.8 1.9 %late_kernel.1 = (f32[256,896]{1,0:T(8,128)S(1)}, f32[256,896]{1,0:T(8,128)S(1)}) custom-call(s32[36]{0:T(128)S(1)} %concatenate.12.meta, bf16[4,64,896]{2,1,0:T(8,128)(2,1)S(1)} %get-tuple-element.15.mine, bf16[4,64,896]{2,1,0:T(8,128)(2,1)S(1)} %collective-permute-done.other, f32[512,896]{1,0:T(8,128)S(1)} %early_kernel.1.acc, ...), custom_call_target="tpu_custom_call" | custom-call | tf_op jit(solution)/shard_map/late_kernel/pallas_call | solution.py:180
  112.6 3.2 %collective-permute-start.7 = (f32[256,896]{1,0:T(8,128)S(1)}, f32[256,896]{1,0:T(8,128)S(1)}, u32[]{:S(2)}, u32[]{:S(2)}) collective-permute-start(f32[256,896]{1,0:T(8,128)S(1)} %get-tuple-element.18), channel_id=1, source_target_pairs={{0,1},{1,0},{2,3},{3,2},{4,5},{5,4},{6,7},{7,6},{8,9},{9,8},{10,11... | collective-permute-start | bytes 2752520 | tf_op jit(solution)/shard_map/ppermute | solution.py:47
  115.8 1.9 %collective-permute-done.7.other_ref = f32[256,896]{1,0:T(8,128)S(1)} collective-permute-done((f32[256,896]{1,0:T(8,128)S(1)}, f32[256,896]{1,0:T(8,128)S(1)}, u32[]{:S(2)}, u32[]{:S(2)}) %collective-permute-start.7) | collective-permute-done | bytes 917536 | tf_op jit(solution)/shard_map/ppermute | solution.py:47
  117.7 0.0 all-gather.4.cloned.1.call-done.w_hbm
  117.7 0.0 copy-done
  117.7 0.0 copy-done.1
  117.7 10.2 %attend_spans.1 = (bf16[128,2048]{1,0:T(8,128)(2,1)}, bf16[128,2048]{1,0:T(8,128)(2,1)}, bf16[256,896]{1,0:T(8,128)(2,1)}) custom-call(bf16[4,64,896]{2,1,0:T(8,128)(2,1)S(1)} %get-tuple-element.14.raw_ref, f32[256,896]{1,0:T(8,128)S(1)} %get-tuple-element.17.mine_ref, f32[256,896]{1,0:T(8,128)S(1)} %collective-permute-done.7.other_ref, ...), custom_call_target="tpu_custom_call" | custom-call | tf_op jit(solution)/shard_map/attend_spans/pallas_call | solution.py:271
  (3 shorter events, 0.0 us)
Async XLA Ops:
  7.2 76.0 %copy-start.3 = (f32[896]{0:T(1024)S(1)}, f32[896]{0:T(1024)}, u32[]{:S(2)}) copy-start(f32[896]{0:T(1024)} %param.12) | copy-start | bytes 10756
  7.2 110.5 %all-gather.4.cloned.1.call-start = ((), (), s32[]{:S(2)}) async-start(), calls=%async_computation.1 | async-start | bytes 7569408 | tf_op jit(solution)/shard_map/all_gather | solution.py:307
  22.7 1.0 copy-start.2
  25.3 51.2 %all-to-all-start = ((bf16[8,64,896]{2,1,0:T(8,128)(2,1)}), bf16[8,64,896]{2,1,0:T(8,128)(2,1)S(1)}, u32[]{:S(2)}, u32[]{:S(2)}) async-start(bf16[8,64,896]{2,1,0:T(8,128)(2,1)} %send_blocks.1), calls=%async_computation | async-start | bytes 1835008 | tf_op jit(solution)/shard_map/all_to_all | solution.py:312
  37.4 80.3 %copy-start = (bf16[128,2048]{1,0:T(8,128)(2,1)S(1)}, bf16[128,2048]{1,0:T(8,128)(2,1)}, u32[]{:S(2)}) copy-start(bf16[128,2048]{1,0:T(8,128)(2,1)} %q_hbm.1) | copy-start | bytes 1572868
  37.4 80.3 %copy-start.1 = (bf16[128,2048]{1,0:T(8,128)(2,1)S(1)}, bf16[128,2048]{1,0:T(8,128)(2,1)}, u32[]{:S(2)}) copy-start(bf16[128,2048]{1,0:T(8,128)(2,1)} %g_hbm.1) | copy-start | bytes 1572868
  76.6 22.2 %collective-permute-start.1 = (bf16[8,32,896]{2,1,0:T(8,128)(2,1)S(1)}, bf16[8,32,896]{2,1,0:T(8,128)(2,1)S(1)}, u32[]{:S(2)}, u32[]{:S(2)}) collective-permute-start(bf16[8,32,896]{2,1,0:T(8,128)(2,1)S(1)} %get-tuple-element.20.own_a), channel_id=1, source_target_pairs={{0,2},{1,9},{2,4},{3,11},{4,6},{5,13},{6,0},{7,15},{8,10},{9,17},{... | collective-permute-start | bytes 1376264 | tf_op jit(solution)/shard_map/ppermute | solution.py:43
  79.2 21.6 %collective-permute-start.4 = (bf16[8,32,896]{2,1,0:T(8,128)(2,1)S(1)}, bf16[8,32,896]{2,1,0:T(8,128)(2,1)S(1)}, u32[]{:S(2)}, u32[]{:S(2)}) collective-permute-start(bf16[8,32,896]{2,1,0:T(8,128)(2,1)S(1)} %get-tuple-element.19.own_b), channel_id=1, source_target_pairs={{0,6},{1,25},{2,0},{3,27},{4,2},{5,29},{6,4},{7,31},{8,14},{9,1},{... | collective-permute-start | bytes 1376264 | tf_op jit(solution)/shard_map/ppermute | solution.py:43
  83.2 22.2 %collective-permute-start.2 = (bf16[8,32,896]{2,1,0:T(8,128)(2,1)S(1)}, bf16[8,32,896]{2,1,0:T(8,128)(2,1)S(1)}, u32[]{:S(2)}, u32[]{:S(2)}) collective-permute-start(bf16[8,32,896]{2,1,0:T(8,128)(2,1)S(1)} %get-tuple-element.19.own_b), channel_id=1, source_target_pairs={{0,2},{1,9},{2,4},{3,11},{4,6},{5,13},{6,0},{7,15},{8,10},{9,17},{... | collective-permute-start | bytes 1376264 | tf_op jit(solution)/shard_map/ppermute | solution.py:43
  86.2 19.2 %collective-permute-start = (bf16[4,64,896]{2,1,0:T(8,128)(2,1)S(1)}, bf16[4,64,896]{2,1,0:T(8,128)(2,1)S(1)}, u32[]{:S(2)}, u32[]{:S(2)}) collective-permute-start(bf16[4,64,896]{2,1,0:T(8,128)(2,1)S(1)} %get-tuple-element.15.mine), channel_id=1, source_target_pairs={{0,1},{1,0},{2,3},{3,2},{4,5},{5,4},{6,7},{7,6},{8,9},{9,8},{10,11... | collective-permute-start | bytes 1376264 | tf_op jit(solution)/shard_map/ppermute | solution.py:47
  94.4 11.0 %collective-permute-start.3 = (bf16[8,32,896]{2,1,0:T(8,128)(2,1)S(1)}, bf16[8,32,896]{2,1,0:T(8,128)(2,1)S(1)}, u32[]{:S(2)}, u32[]{:S(2)}) collective-permute-start(bf16[8,32,896]{2,1,0:T(8,128)(2,1)S(1)} %get-tuple-element.20.own_a), channel_id=1, source_target_pairs={{0,6},{1,25},{2,0},{3,27},{4,2},{5,29},{6,4},{7,31},{8,14},{9,1},{... | collective-permute-start | bytes 1376264 | tf_op jit(solution)/shard_map/ppermute | solution.py:43
  98.8 10.7 %collective-permute-start.5 = (bf16[8,32,896]{2,1,0:T(8,128)(2,1)S(1)}, bf16[8,32,896]{2,1,0:T(8,128)(2,1)S(1)}, u32[]{:S(2)}, u32[]{:S(2)}) collective-permute-start(bf16[8,32,896]{2,1,0:T(8,128)(2,1)S(1)} %collective-permute-done.1.left_a), channel_id=1, source_target_pairs={{0,2},{1,9},{2,4},{3,11},{4,6},{5,13},{6,0},{7,15},{8,10},{9,17},{... | collective-permute-start | bytes 1376264 | tf_op jit(solution)/shard_map/ppermute | solution.py:43
  100.8 10.0 %collective-permute-start.6 = (bf16[8,32,896]{2,1,0:T(8,128)(2,1)S(1)}, bf16[8,32,896]{2,1,0:T(8,128)(2,1)S(1)}, u32[]{:S(2)}, u32[]{:S(2)}) collective-permute-start(bf16[8,32,896]{2,1,0:T(8,128)(2,1)S(1)} %collective-permute-done.4.right_b), channel_id=1, source_target_pairs={{0,6},{1,25},{2,0},{3,27},{4,2},{5,29},{6,4},{7,31},{8,14},{9,1},{... | collective-permute-start | bytes 1376264 | tf_op jit(solution)/shard_map/ppermute | solution.py:43
  112.6 5.1 %collective-permute-start.7 = (f32[256,896]{1,0:T(8,128)S(1)}, f32[256,896]{1,0:T(8,128)S(1)}, u32[]{:S(2)}, u32[]{:S(2)}) collective-permute-start(f32[256,896]{1,0:T(8,128)S(1)} %get-tuple-element.18), channel_id=1, source_target_pairs={{0,1},{1,0},{2,3},{3,2},{4,5},{5,4},{6,7},{7,6},{8,9},{9,8},{10,11... | collective-permute-start | bytes 2752520 | tf_op jit(solution)/shard_map/ppermute | solution.py:47
Sparse Core Ops, SparseCore 0:
  20.5 88.5 all-gather.3

commit v3 on v2

--- a/solution.py
+++ b/solution.py
@@ -47,23 +47,68 @@
     return lax.ppermute(rows, "c", [(0, 1), (1, 0)])
 
 
-def send_kernel(meta, raw_ref, out_ref):
+def send_kernel(meta, raw_ref, out_ref, sems):
+    copies = []
     for i in range(PER_DEV):
-        out_ref[meta[PER_DEV * meta[32] + i] // PER_DEV] = raw_ref[i]
+        target = meta[PER_DEV * meta[32] + i] // PER_DEV
+        copies.append(pltpu.make_async_copy(raw_ref.at[i], out_ref.at[target], sems.at[i]))
+    for copy in copies:
+        copy.start()
+    for copy in copies:
+        copy.wait()
 
 
 def send_blocks(meta, raw):
+    hbm = pl.BlockSpec(memory_space=pl.ANY)
     return pl.pallas_call(
         send_kernel,
         out_shape=jax.ShapeDtypeStruct((NY * NC, NLEN, E), jnp.bfloat16),
-        in_specs=[
-            pl.BlockSpec(memory_space=pltpu.SMEM),
-            pl.BlockSpec(memory_space=pltpu.VMEM),
-        ],
-        out_specs=pl.BlockSpec(memory_space=pltpu.VMEM),
-        compiler_params=pltpu.CompilerParams(vmem_limit_bytes=8 * 1024 * 1024),
+        in_specs=[pl.BlockSpec(memory_space=pltpu.SMEM), hbm],
+        out_specs=hbm,
+        scratch_shapes=[pltpu.SemaphoreType.DMA((PER_DEV,))],
+        compiler_params=pltpu.CompilerParams(vmem_limit_bytes=56 * 1024 * 1024),
         name="send_blocks",
     )(meta, raw)
+
+
+def units_kernel(spot, key_ref, value_ref, up_ref, down_ref, unit_ref, whole_ref):
+    core, y = spot[0] % 2, spot[0] // 2 % NY
+
+    def pick(ref, count, start, rows, offset, length):
+        to = lax.broadcasted_iota(jnp.int32, (count, rows), 0) - offset
+        source = lax.broadcasted_iota(jnp.int32, (count, rows), 1) - start
+        hot = (to == source) & (to >= 0) & (to < length)
+        return dot(hot.astype(jnp.float32).astype(jnp.bfloat16), ref[...], NN)
+
+    def only(condition, value):
+        return jnp.where(condition, value, 0)
+
+    side = QUART * (y // 2)
+    quarter = pick(up_ref, 40, side, UNITS, 32, only(y % 2 == 0, QUART)) + pick(
+        down_ref, 40, side, UNITS, 32, only(y % 2 == 1, QUART)
+    )
+    rows = pick(key_ref, 40, 0, 32, 0, only(core == 0, 32)) + pick(
+        value_ref, 40, 0, 32, 0, only(core == 1, 32)
+    )
+    unit_ref[...] = (rows + quarter).astype(jnp.bfloat16)
+    whole_ref[...] = (
+        pick(up_ref, 32, HALF, UNITS, 0, HALF) + pick(down_ref, 32, HALF, UNITS, 16, HALF)
+    ).astype(jnp.bfloat16)
+
+
+def units(spot, key_rows, value_rows, up_rows, down_rows):
+    vmem = pl.BlockSpec(memory_space=pltpu.VMEM)
+    return pl.pallas_call(
+        units_kernel,
+        out_shape=(
+            jax.ShapeDtypeStruct((40, E), jnp.bfloat16),
+            jax.ShapeDtypeStruct((32, E), jnp.bfloat16),
+        ),
+        in_specs=[pl.BlockSpec(memory_space=pltpu.SMEM)] + [vmem] * 4,
+        out_specs=(vmem, vmem),
+        compiler_params=pltpu.CompilerParams(vmem_limit_bytes=56 * 1024 * 1024),
+        name="pick_units",
+    )(spot, key_rows, value_rows, up_rows, down_rows)
 
 
 def gelu(x):
@@ -157,13 +202,13 @@
 
 
 def late_kernel(
-    meta, mine, other, acc, left_a, left_b, right_a, right_b, far_a, far_b, mine_ref, other_ref
+    meta, raw, mine, other, acc, left_a, left_b, right_a, right_b, far_a, far_b, mine_ref, other_ref
 ):
     normed = both_cores(mine, other)
 
     def write(blocks):
         total = acc[...] + multiply(normed, blocks)
-        mine_ref[...] = total[:ROWS]
+        mine_ref[...] = total[:ROWS] + raw[...].reshape(ROWS, E).astype(jnp.float32)
         other_ref[...] = total[ROWS:]
 
     by_case(
@@ -182,7 +227,7 @@
         out_shape=outs,
         in_specs=[pl.BlockSpec(memory_space=pltpu.SMEM)] + [vmem] * len(arrays),
         out_specs=jax.tree.map(lambda _: vmem, outs),
-        compiler_params=pltpu.CompilerParams(vmem_limit_bytes=28 * 1024 * 1024),
+        compiler_params=pltpu.CompilerParams(vmem_limit_bytes=14 * 1024 * 1024),
         name=kernel.__name__,
     )(meta, *arrays)
 
@@ -195,7 +240,7 @@
 
 
 def attend_kernel(
-    raw_ref, mine_ref, other_ref, w_hbm, q_hbm, g_hbm, att_hbm, gq_hbm, ge_ref, w, q_ref, g_ref, kv, gkv, att, gq, sems, outs
+    mine_ref, other_ref, w_hbm, q_hbm, g_hbm, att_hbm, gq_hbm, ge_ref, w, q_ref, g_ref, kv, gkv, att, gq, sems, outs
 ):
     def fetch(i):
         return pltpu.make_async_copy(
@@ -208,8 +253,7 @@
     for copy in loads:
         copy.start()
 
-    floats = raw_ref[...].reshape(ROWS, E).astype(jnp.float32)
-    enc = (floats + (mine_ref[...] + other_ref[...])).astype(jnp.bfloat16)
+    enc = (mine_ref[...] + other_ref[...]).astype(jnp.bfloat16)
     first = lax.broadcasted_iota(jnp.int32, (NPC * NLEN, CH_DEV * CL), 1) < CL
     half = NPC * NLEN
 
@@ -261,7 +305,7 @@
         copy.wait()
 
 
-def attend(raw, mine, other, weights, queries, grads):
+def attend(mine, other, weights, queries, grads):
     tokens = CH_DEV * CL
     hbm = pl.BlockSpec(memory_space=pltpu.HBM)
     vmem = pl.BlockSpec(memory_space=pltpu.VMEM)
@@ -271,7 +315,7 @@
     return pl.pallas_call(
         attend_kernel,
         out_shape=(wide, wide, jax.ShapeDtypeStruct((ROWS, E), jnp.bfloat16)),
-        in_specs=[vmem, vmem, vmem, hbm, hbm, hbm],
+        in_specs=[vmem, vmem, hbm, hbm, hbm],
         out_specs=(hbm, hbm, vmem),
         scratch_shapes=[
             pltpu.VMEM((2 * HEADS, HD, E), jnp.bfloat16),
@@ -286,7 +330,7 @@
         ],
         compiler_params=pltpu.CompilerParams(vmem_limit_bytes=LIMIT),
         name="attend_spans",
-    )(raw, mine, other, weights, queries, grads)
+    )(mine, other, weights, queries, grads)
 
 
 def body(queries, neighbours, slots, gain, up, down, key_proj, value_proj, grads):
@@ -295,23 +339,17 @@
     here = jnp.stack([y * NC + c, c, y, x]).astype(jnp.int32)
     meta = jnp.concatenate([slots - (z * NX + x) * group, here])
 
-    up = up.T
-    kv_unit = jnp.where(c == 0, key_proj.T, value_proj.T)
-    halves = jnp.concatenate([up[:QUART], down[:QUART], up[QUART:HALF], down[QUART:HALF]])
-    quarter = jnp.pad(lax.dynamic_slice_in_dim(halves, y * QUART, QUART), ((0, 1), (0, 0)))
-    pad = ((0, 16 - HALF), (0, 0))
-    whole = jnp.concatenate([jnp.pad(up[HALF:], pad), jnp.pad(down[HALF:], pad)])
-
-    along_x = lax.all_gather(jnp.concatenate([kv_unit, quarter]), "x", axis=0, tiled=False)
+    spot = (y * NC + c).astype(jnp.int32).reshape(1)
+    unit, whole = units(spot, key_proj.T, value_proj.T, up.T, down)
+    along_x = lax.all_gather(unit, "x", axis=0, tiled=False)
     kv_head = along_x[:, :32].reshape(HD, E)
     weights = lax.all_gather(kv_head, ("z", "c"), axis=0, tiled=False)
 
-    outgoing = send_blocks(meta, neighbours.reshape(PER_DEV, NLEN, E))
     ff_unit = jnp.where(c == 0, along_x[:, 32:].reshape(32, E), whole)
-    ff_unit, outgoing = lax.optimization_barrier((ff_unit, outgoing))
+    own = lax.all_gather(ff_unit, "z", axis=0, tiled=False)
+    own, rows = lax.optimization_barrier((own, neighbours))
+    outgoing = send_blocks(meta, rows.reshape(PER_DEV, NLEN, E))
     recv = lax.all_to_all(outgoing, ("y", "c"), 0, 0, tiled=True)
-    own = lax.all_gather(ff_unit, "z", axis=0, tiled=False)
-    own, recv = lax.optimization_barrier((own, recv))
     raw, normed = place(meta, recv, gain.reshape(1, E))
     other = swap(normed)
     own_a, own_b = own[: NZ // 2], own[NZ // 2 :]
@@ -323,9 +361,9 @@
     two = jax.ShapeDtypeStruct((2 * ROWS, E), jnp.float32)
     acc = encode_part(early_kernel, two, meta, normed, other, own_a, own_b, *near)
     mine, given = encode_part(
-        late_kernel, (one, one), meta, normed, other, acc, *near, far_a, far_b
-    )
-    return attend(raw, mine, swap(given), weights, queries, grads)
+        late_kernel, (one, one), meta, raw, normed, other, acc, *near, far_a, far_b
+    )
+    return attend(mine, swap(given), weights, queries, grads)
 
 
 def solution(mesh):

time: 136 us -> 149 us (1.096)
  Pallas kernels: 17.8 us -> 34.2 us
  starting transfers between devices: 42.8 us -> 39.4 us
    pallas_call x1, Pallas kernels: 1.56 us -> 15.7 us  [send_blocks(): pl.pallas_call(send_kernel, out_shape=jax.ShapeDtypeStruct((NY * NC, NLEN...]
    ppermute x2, starting transfers between devices: 11.4 us -> 6.75 us  [swap(): return lax.ppermute(rows, 'c', [(0, 1), (1, 0)])]
    slice x3 -> x0, local copies, waits for them, and re-layouts: 2.44 us -> none  [the longest x1 0.84 us: body(): down[QUART:HALF]]
    unnamed x8 -> x10, local copies, waits for them, and re-layouts: 1.03 us -> 3.39 us
    pallas_call x0 -> x1, Pallas kernels: none -> 1.8 us  [units(): pl.pallas_call(units_kernel, out_shape=(jax.ShapeDtypeStruct((40, E), jnp...]
  transfers between devices with their start and end apart: 10 -> 10, of which waited for: 3 -> 2; matrix products, arithmetic and copies ran while one was open for 2% -> 2% of each run, Pallas kernels for 6% -> 15%
where the time goes in v3:
time: 149 us
  blocking collectives  50.5 us (34%)
  starting transfers between devices  39.4 us (26%)
  Pallas kernels  34.2 us (23%)
  between operations  14.3 us (10%)
  local copies, waits for them, and re-layouts  5.55 us (4%)
  waiting for transfers between devices  3.21 us (2%)
  other arithmetic  1.49 us (1%)
    all_gather x1, blocking collectives, body(): own = lax.all_gather(ff_unit, 'z', axis=0, tiled=False)  39.7 us
    ppermute x6, starting transfers between devices, ring(): return lax.ppermute(rows, ('x', 'y', 'c'), ring_pairs(step))  19.5 us
    pallas_call x1, Pallas kernels, send_blocks(): pl.pallas_call(send_kernel, out_shape=jax.ShapeDtypeStruct((NY * NC, NLEN...  15.7 us
    all_to_all x1, starting transfers between devices, body(): recv = lax.all_to_all(outgoing, ('y', 'c'), 0, 0, tiled=True)  13.2 us
    all_gather x1, blocking collectives, body(): along_x = lax.all_gather(unit, 'x', axis=0, tiled=False)  10.8 us
    pallas_call x1, Pallas kernels, attend(): pl.pallas_call(attend_kernel, out_shape=(wide, wide, jax.ShapeDtypeStruct...  10.2 us
    ppermute x2, starting transfers between devices, swap(): return lax.ppermute(rows, 'c', [(0, 1), (1, 0)])  6.75 us
    pallas_call x2, Pallas kernels, encode_part(): pl.pallas_call(kernel, out_shape=outs, in_specs=[pl.BlockSpec(memory_spac...  5.42 us
  transfers between devices with their start and end apart: 10, of which 2 were waited for; matrix products, arithmetic and copies ran while one was open for 2% of the time, Pallas kernels for 15%

profile of v3, /device:TPU:1, one launch (start us, length us, event | category | flops | bytes accessed | tf_op | source)
XLA Modules:
  0.0 148.6 jit_solution(7989006248630064679)
XLA Ops:
  7.2 0.0 copy-start.4
  7.2 0.0 all-gather.4.cloned.1.call-start
  7.2 1.8 %pick_units.1 = (bf16[40,896]{1,0:T(8,128)(2,1)}, bf16[32,896]{1,0:T(8,128)(2,1)}) custom-call(s32[1]{0:T(128)} %bitcast.spot, bf16[32,896]{1,0:T(8,128)(2,1)} %bitcast.20, bf16[32,896]{1,0:T(8,128)(2,1)} %bitcast.21, bf16[28,896]{1,0:T(8,128)(2,1)} %bitcast.22, bf16[28,896]{1,0:T(8,128)(2,1)} %down_ref.1), custom_call_target="tpu_custom_call" | custom-call | tf_op jit(solution)/shard_map/pick_units/pallas_call | solution.py:101
  9.0 10.8 %all-gather = bf16[160,896]{1,0:T(8,128)(2,1)S(1)} all-gather(bf16[40,896]{1,0:T(8,128)(2,1)} %get-tuple-element.11), channel_id=2, replica_groups=mesh['z'=16,'x'=4,'y'=4,'c'=2] {'x'}, dimensions={0}, use_global_device_ids=true | all-gather | bytes 358400 | tf_op jit(solution)/shard_map/all_gather | solution.py:344
  19.8 0.7 slice.17
  20.6 0.0 all-gather.4.cloned.1.call-update
  20.6 0.8 fusion
  21.4 39.7 %all-gather.1 = bf16[512,896]{1,0:T(8,128)(2,1)S(1)} all-gather(bf16[32,896]{1,0:T(8,128)(2,1)S(1)} %fusion), channel_id=3, replica_groups=mesh['z'=16,'x'=4,'y'=4,'c'=2] {'z'}, dimensions={0}, use_global_device_ids=true | all-gather | bytes 974848 | tf_op jit(solution)/shard_map/all_gather | solution.py:349
  61.1 0.7 broadcast_subtract_fusion
  61.8 0.6 concatenate.3.meta
  62.4 15.7 %send_blocks.1 = bf16[8,64,896]{2,1,0:T(8,128)(2,1)} custom-call(s32[36]{0:T(128)} %concatenate.3.meta, bf16[4,64,896]{2,1,0:T(8,128)(2,1)} %bitcast.19), custom_call_target="tpu_custom_call" | custom-call | tf_op jit(solution)/shard_map/send_blocks/pallas_call | solution.py:63
  78.1 13.2 %all-to-all-start = ((bf16[8,64,896]{2,1,0:T(8,128)(2,1)}), bf16[8,64,896]{2,1,0:T(8,128)(2,1)S(1)}, u32[]{:S(2)}, u32[]{:S(2)}) async-start(bf16[8,64,896]{2,1,0:T(8,128)(2,1)} %send_blocks.1), calls=%async_computation | async-start | bytes 1835008 | tf_op jit(solution)/shard_map/all_to_all | solution.py:352
  91.2 0.8 fusion.1
  92.1 2.5 %collective-permute-start.1 = (bf16[8,32,896]{2,1,0:T(8,128)(2,1)}, bf16[8,32,896]{2,1,0:T(8,128)(2,1)S(1)}, u32[]{:S(2)}, u32[]{:S(2)}) collective-permute-start(bf16[8,32,896]{2,1,0:T(8,128)(2,1)} %get-tuple-element.20.own_a), channel_id=1, source_target_pairs={{0,2},{1,9},{2,4},{3,11},{4,6},{5,13},{6,0},{7,15},{8,10},{9,17},{... | collective-permute-start | bytes 1376264 | tf_op jit(solution)/shard_map/ppermute | solution.py:43
  94.6 4.0 %collective-permute-start.4 = (bf16[8,32,896]{2,1,0:T(8,128)(2,1)S(1)}, bf16[8,32,896]{2,1,0:T(8,128)(2,1)S(1)}, u32[]{:S(2)}, u32[]{:S(2)}) collective-permute-start(bf16[8,32,896]{2,1,0:T(8,128)(2,1)S(1)} %get-tuple-element.19.own_b), channel_id=1, source_target_pairs={{0,6},{1,25},{2,0},{3,27},{4,2},{5,29},{6,4},{7,31},{8,14},{9,1},{... | collective-permute-start | bytes 1376264 | tf_op jit(solution)/shard_map/ppermute | solution.py:43
  98.6 1.9 %collective-permute-start.2 = (bf16[8,32,896]{2,1,0:T(8,128)(2,1)S(1)}, bf16[8,32,896]{2,1,0:T(8,128)(2,1)S(1)}, u32[]{:S(2)}, u32[]{:S(2)}) collective-permute-start(bf16[8,32,896]{2,1,0:T(8,128)(2,1)S(1)} %get-tuple-element.19.own_b), channel_id=1, source_target_pairs={{0,2},{1,9},{2,4},{3,11},{4,6},{5,13},{6,0},{7,15},{8,10},{9,17},{... | collective-permute-start | bytes 1376264 | tf_op jit(solution)/shard_map/ppermute | solution.py:43
  100.5 4.6 %collective-permute-start.3 = (bf16[8,32,896]{2,1,0:T(8,128)(2,1)}, bf16[8,32,896]{2,1,0:T(8,128)(2,1)S(1)}, u32[]{:S(2)}, u32[]{:S(2)}) collective-permute-start(bf16[8,32,896]{2,1,0:T(8,128)(2,1)} %get-tuple-element.20.own_a), channel_id=1, source_target_pairs={{0,6},{1,25},{2,0},{3,27},{4,2},{5,29},{6,4},{7,31},{8,14},{9,1},{... | collective-permute-start | bytes 1376264 | tf_op jit(solution)/shard_map/ppermute | solution.py:43
  105.1 0.0 copy-done.4
  105.1 0.0 all-to-all-done.recv_ref
  105.1 0.0 copy-start.2
  105.1 0.6 copy-done.2
  105.8 1.1 place_rows.1
  106.8 3.0 %collective-permute-start = (bf16[4,64,896]{2,1,0:T(8,128)(2,1)S(1)}, bf16[4,64,896]{2,1,0:T(8,128)(2,1)S(1)}, u32[]{:S(2)}, u32[]{:S(2)}) collective-permute-start(bf16[4,64,896]{2,1,0:T(8,128)(2,1)S(1)} %get-tuple-element.15.mine), channel_id=1, source_target_pairs={{0,1},{1,0},{2,3},{3,2},{4,5},{5,4},{6,7},{7,6},{8,9},{9,8},{10,11... | collective-permute-start | bytes 1376264 | tf_op jit(solution)/shard_map/ppermute | solution.py:47
  109.9 0.0 collective-permute-done.1.left_a
  109.9 2.5 %collective-permute-start.5 = (bf16[8,32,896]{2,1,0:T(8,128)(2,1)S(1)}, bf16[8,32,896]{2,1,0:T(8,128)(2,1)S(1)}, u32[]{:S(2)}, u32[]{:S(2)}) collective-permute-start(bf16[8,32,896]{2,1,0:T(8,128)(2,1)S(1)} %collective-permute-done.1.left_a), channel_id=1, source_target_pairs={{0,2},{1,9},{2,4},{3,11},{4,6},{5,13},{6,0},{7,15},{8,10},{9,17},{... | collective-permute-start | bytes 1376264 | tf_op jit(solution)/shard_map/ppermute | solution.py:43
  112.4 0.0 collective-permute-done.4.right_b
  112.4 4.0 %collective-permute-start.6 = (bf16[8,32,896]{2,1,0:T(8,128)(2,1)S(1)}, bf16[8,32,896]{2,1,0:T(8,128)(2,1)S(1)}, u32[]{:S(2)}, u32[]{:S(2)}) collective-permute-start(bf16[8,32,896]{2,1,0:T(8,128)(2,1)S(1)} %collective-permute-done.4.right_b), channel_id=1, source_target_pairs={{0,6},{1,25},{2,0},{3,27},{4,2},{5,29},{6,4},{7,31},{8,14},{9,1},{... | collective-permute-start | bytes 1376264 | tf_op jit(solution)/shard_map/ppermute | solution.py:43
  116.4 0.0 collective-permute-done.2.left_b
  116.4 0.0 collective-permute-done.3.right_a
  116.4 0.0 collective-permute-done.other
  116.5 0.0 copy-start.3
  116.5 0.6 copy-done.3
  117.1 3.5 %early_kernel.1.acc = f32[512,896]{1,0:T(8,128)S(1)} custom-call(s32[36]{0:T(128)S(1)} %copy-done.3, bf16[4,64,896]{2,1,0:T(8,128)(2,1)S(1)} %get-tuple-element.15.mine, bf16[4,64,896]{2,1,0:T(8,128)(2,1)S(1)} %collective-permute-done.other, bf16[8,32,896]{2,1,0:T(8,128)(2,1)} %get-tuple-element.20.own_a, bf16[8,32,896]{2,1,0:T(8,128)(2,1)S(1)} %get-tuple-element.19.own_b, ...), custom_call_target="tpu_custom_call" | custom-call | tf_op jit(solution)/shard_map/early_kernel/pallas_call | solution.py:225
  120.6 0.0 collective-permute-done.5.far_a
  120.6 1.3 collective-permute-done.6.far_b
  121.9 1.9 %late_kernel.1 = (f32[256,896]{1,0:T(8,128)S(1)}, f32[256,896]{1,0:T(8,128)S(1)}) custom-call(s32[36]{0:T(128)S(1)} %copy-done.3, bf16[4,64,896]{2,1,0:T(8,128)(2,1)S(1)} %get-tuple-element.14.raw, bf16[4,64,896]{2,1,0:T(8,128)(2,1)S(1)} %get-tuple-element.15.mine, bf16[4,64,896]{2,1,0:T(8,128)(2,1)S(1)} %collective-permute-done.other, ...), custom_call_target="tpu_custom_call" | custom-call | tf_op jit(solution)/shard_map/late_kernel/pallas_call | solution.py:225
  123.8 3.7 %collective-permute-start.7 = (f32[256,896]{1,0:T(8,128)S(1)}, f32[256,896]{1,0:T(8,128)S(1)}, u32[]{:S(2)}, u32[]{:S(2)}) collective-permute-start(f32[256,896]{1,0:T(8,128)S(1)} %get-tuple-element.18), channel_id=1, source_target_pairs={{0,1},{1,0},{2,3},{3,2},{4,5},{5,4},{6,7},{7,6},{8,9},{9,8},{10,11... | collective-permute-start | bytes 2752520 | tf_op jit(solution)/shard_map/ppermute | solution.py:47
  127.5 1.9 %collective-permute-done.7.other_ref = f32[256,896]{1,0:T(8,128)S(1)} collective-permute-done((f32[256,896]{1,0:T(8,128)S(1)}, f32[256,896]{1,0:T(8,128)S(1)}, u32[]{:S(2)}, u32[]{:S(2)}) %collective-permute-start.7) | collective-permute-done | bytes 917536 | tf_op jit(solution)/shard_map/ppermute | solution.py:47
  129.4 0.0 all-gather.4.cloned.1.call-done.w_hbm
  129.4 0.0 copy-start
  129.4 1.0 copy-done
  130.5 0.0 copy-start.1
  130.5 1.0 copy-done.1
  131.5 10.2 %attend_spans.1 = (bf16[128,2048]{1,0:T(8,128)(2,1)}, bf16[128,2048]{1,0:T(8,128)(2,1)}, bf16[256,896]{1,0:T(8,128)(2,1)}) custom-call(f32[256,896]{1,0:T(8,128)S(1)} %get-tuple-element.17.mine_ref, f32[256,896]{1,0:T(8,128)S(1)} %collective-permute-done.7.other_ref, bf16[32,128,896]{2,1,0:T(8,128)(2,1)} %all-gather.4.cloned.1.call-done.w_hbm, ...), custom_call_target="tpu_custom_call" | custom-call | tf_op jit(solution)/shard_map/attend_spans/pallas_call | solution.py:315
  (1 shorter events, 0.0 us)
Async XLA Ops:
  7.2 97.9 %copy-start.4 = (f32[896]{0:T(1024)S(1)}, f32[896]{0:T(1024)}, u32[]{:S(2)}) copy-start(f32[896]{0:T(1024)} %param.12) | copy-start | bytes 10756
  7.2 122.3 %all-gather.4.cloned.1.call-start = ((), (), s32[]{:S(2)}) async-start(), calls=%async_computation.1 | async-start | bytes 7569408 | tf_op jit(solution)/shard_map/all_gather | solution.py:346
  78.1 27.0 %all-to-all-start = ((bf16[8,64,896]{2,1,0:T(8,128)(2,1)}), bf16[8,64,896]{2,1,0:T(8,128)(2,1)S(1)}, u32[]{:S(2)}, u32[]{:S(2)}) async-start(bf16[8,64,896]{2,1,0:T(8,128)(2,1)} %send_blocks.1), calls=%async_computation | async-start | bytes 1835008 | tf_op jit(solution)/shard_map/all_to_all | solution.py:352
  92.1 17.8 %collective-permute-start.1 = (bf16[8,32,896]{2,1,0:T(8,128)(2,1)}, bf16[8,32,896]{2,1,0:T(8,128)(2,1)S(1)}, u32[]{:S(2)}, u32[]{:S(2)}) collective-permute-start(bf16[8,32,896]{2,1,0:T(8,128)(2,1)} %get-tuple-element.20.own_a), channel_id=1, source_target_pairs={{0,2},{1,9},{2,4},{3,11},{4,6},{5,13},{6,0},{7,15},{8,10},{9,17},{... | collective-permute-start | bytes 1376264 | tf_op jit(solution)/shard_map/ppermute | solution.py:43
  94.6 17.8 %collective-permute-start.4 = (bf16[8,32,896]{2,1,0:T(8,128)(2,1)S(1)}, bf16[8,32,896]{2,1,0:T(8,128)(2,1)S(1)}, u32[]{:S(2)}, u32[]{:S(2)}) collective-permute-start(bf16[8,32,896]{2,1,0:T(8,128)(2,1)S(1)} %get-tuple-element.19.own_b), channel_id=1, source_target_pairs={{0,6},{1,25},{2,0},{3,27},{4,2},{5,29},{6,4},{7,31},{8,14},{9,1},{... | collective-permute-start | bytes 1376264 | tf_op jit(solution)/shard_map/ppermute | solution.py:43
  98.6 17.9 %collective-permute-start.2 = (bf16[8,32,896]{2,1,0:T(8,128)(2,1)S(1)}, bf16[8,32,896]{2,1,0:T(8,128)(2,1)S(1)}, u32[]{:S(2)}, u32[]{:S(2)}) collective-permute-start(bf16[8,32,896]{2,1,0:T(8,128)(2,1)S(1)} %get-tuple-element.19.own_b), channel_id=1, source_target_pairs={{0,2},{1,9},{2,4},{3,11},{4,6},{5,13},{6,0},{7,15},{8,10},{9,17},{... | collective-permute-start | bytes 1376264 | tf_op jit(solution)/shard_map/ppermute | solution.py:43
  100.5 15.9 %collective-permute-start.3 = (bf16[8,32,896]{2,1,0:T(8,128)(2,1)}, bf16[8,32,896]{2,1,0:T(8,128)(2,1)S(1)}, u32[]{:S(2)}, u32[]{:S(2)}) collective-permute-start(bf16[8,32,896]{2,1,0:T(8,128)(2,1)} %get-tuple-element.20.own_a), channel_id=1, source_target_pairs={{0,6},{1,25},{2,0},{3,27},{4,2},{5,29},{6,4},{7,31},{8,14},{9,1},{... | collective-permute-start | bytes 1376264 | tf_op jit(solution)/shard_map/ppermute | solution.py:43
  105.1 0.7 copy-start.2
  106.8 9.6 %collective-permute-start = (bf16[4,64,896]{2,1,0:T(8,128)(2,1)S(1)}, bf16[4,64,896]{2,1,0:T(8,128)(2,1)S(1)}, u32[]{:S(2)}, u32[]{:S(2)}) collective-permute-start(bf16[4,64,896]{2,1,0:T(8,128)(2,1)S(1)} %get-tuple-element.15.mine), channel_id=1, source_target_pairs={{0,1},{1,0},{2,3},{3,2},{4,5},{5,4},{6,7},{7,6},{8,9},{9,8},{10,11... | collective-permute-start | bytes 1376264 | tf_op jit(solution)/shard_map/ppermute | solution.py:47
  109.9 10.7 %collective-permute-start.5 = (bf16[8,32,896]{2,1,0:T(8,128)(2,1)S(1)}, bf16[8,32,896]{2,1,0:T(8,128)(2,1)S(1)}, u32[]{:S(2)}, u32[]{:S(2)}) collective-permute-start(bf16[8,32,896]{2,1,0:T(8,128)(2,1)S(1)} %collective-permute-done.1.left_a), channel_id=1, source_target_pairs={{0,2},{1,9},{2,4},{3,11},{4,6},{5,13},{6,0},{7,15},{8,10},{9,17},{... | collective-permute-start | bytes 1376264 | tf_op jit(solution)/shard_map/ppermute | solution.py:43
  112.4 9.5 %collective-permute-start.6 = (bf16[8,32,896]{2,1,0:T(8,128)(2,1)S(1)}, bf16[8,32,896]{2,1,0:T(8,128)(2,1)S(1)}, u32[]{:S(2)}, u32[]{:S(2)}) collective-permute-start(bf16[8,32,896]{2,1,0:T(8,128)(2,1)S(1)} %collective-permute-done.4.right_b), channel_id=1, source_target_pairs={{0,6},{1,25},{2,0},{3,27},{4,2},{5,29},{6,4},{7,31},{8,14},{9,1},{... | collective-permute-start | bytes 1376264 | tf_op jit(solution)/shard_map/ppermute | solution.py:43
  116.5 0.7 copy-start.3
  123.8 5.6 %collective-permute-start.7 = (f32[256,896]{1,0:T(8,128)S(1)}, f32[256,896]{1,0:T(8,128)S(1)}, u32[]{:S(2)}, u32[]{:S(2)}) collective-permute-start(f32[256,896]{1,0:T(8,128)S(1)} %get-tuple-element.18), channel_id=1, source_target_pairs={{0,1},{1,0},{2,3},{3,2},{4,5},{5,4},{6,7},{7,6},{8,9},{9,8},{10,11... | collective-permute-start | bytes 2752520 | tf_op jit(solution)/shard_map/ppermute | solution.py:47
  129.4 1.0 copy-start
  130.5 1.0 copy-start.1
Sparse Core Ops, SparseCore 0:
  20.7 88.0 all-gather.3

commit v4 on v3

--- a/solution.py
+++ b/solution.py
@@ -47,26 +47,19 @@
     return lax.ppermute(rows, "c", [(0, 1), (1, 0)])
 
 
-def send_kernel(meta, raw_ref, out_ref, sems):
-    copies = []
+def send_kernel(meta, raw_ref, out_ref):
     for i in range(PER_DEV):
-        target = meta[PER_DEV * meta[32] + i] // PER_DEV
-        copies.append(pltpu.make_async_copy(raw_ref.at[i], out_ref.at[target], sems.at[i]))
-    for copy in copies:
-        copy.start()
-    for copy in copies:
-        copy.wait()
+        out_ref[meta[PER_DEV * meta[32] + i] // PER_DEV] = raw_ref[i]
 
 
 def send_blocks(meta, raw):
-    hbm = pl.BlockSpec(memory_space=pl.ANY)
+    vmem = pl.BlockSpec(memory_space=pltpu.VMEM)
     return pl.pallas_call(
         send_kernel,
         out_shape=jax.ShapeDtypeStruct((NY * NC, NLEN, E), jnp.bfloat16),
-        in_specs=[pl.BlockSpec(memory_space=pltpu.SMEM), hbm],
-        out_specs=hbm,
-        scratch_shapes=[pltpu.SemaphoreType.DMA((PER_DEV,))],
-        compiler_params=pltpu.CompilerParams(vmem_limit_bytes=56 * 1024 * 1024),
+        in_specs=[pl.BlockSpec(memory_space=pltpu.SMEM), vmem],
+        out_specs=vmem,
+        compiler_params=pltpu.CompilerParams(vmem_limit_bytes=8 * 1024 * 1024),
         name="send_blocks",
     )(meta, raw)
 
@@ -349,12 +342,13 @@
     own = lax.all_gather(ff_unit, "z", axis=0, tiled=False)
     own, rows = lax.optimization_barrier((own, neighbours))
     outgoing = send_blocks(meta, rows.reshape(PER_DEV, NLEN, E))
+    own_a, own_b = own[: NZ // 2], own[NZ // 2 :]
+    left_a, right_b = ring(own_a, 1), ring(own_b, -1)
+    left_b, right_a = ring(own_b, 1), ring(own_a, -1)
+    left_a, right_b, outgoing = lax.optimization_barrier((left_a, right_b, outgoing))
     recv = lax.all_to_all(outgoing, ("y", "c"), 0, 0, tiled=True)
     raw, normed = place(meta, recv, gain.reshape(1, E))
     other = swap(normed)
-    own_a, own_b = own[: NZ // 2], own[NZ // 2 :]
-    left_a, right_b = ring(own_a, 1), ring(own_b, -1)
-    left_b, right_a = ring(own_b, 1), ring(own_a, -1)
     far_a, far_b = ring(left_a, 1), ring(right_b, -1)
     near = (left_a, left_b, right_a, right_b)
     one = jax.ShapeDtypeStruct((ROWS, E), jnp.float32)

time: 149 us -> 144 us (0.966)
  Pallas kernels: 34.2 us -> 19.6 us
  waiting for transfers between devices: 3.21 us -> 12.6 us
    pallas_call x1, Pallas kernels: 15.7 us -> 1.55 us  [send_blocks(): pl.pallas_call(send_kernel, out_shape=jax.ShapeDtypeStruct((NY * NC, NLEN...]
    all_to_all x1, waiting for transfers between devices: 0.01 us -> 7.22 us  [body(): recv = lax.all_to_all(outgoing, ('y', 'c'), 0, 0, tiled=True)]
    ppermute x6, waiting for transfers between devices: 1.29 us -> 3.5 us  [ring(): return lax.ppermute(rows, ('x', 'y', 'c'), ring_pairs(step))]
    unnamed x10 -> x12, local copies, waits for them, and re-layouts: 3.39 us -> 4.13 us
  transfers between devices with their start and end apart: 10 -> 10, of which waited for: 2 -> 6; matrix products, arithmetic and copies ran while one was open for 2% -> 1% of each run, Pallas kernels for 15% -> 5%
where the time goes in v4:
time: 144 us
  blocking collectives  50.5 us (35%)
  starting transfers between devices  40.2 us (28%)
  Pallas kernels  19.6 us (14%)
  between operations  14.2 us (10%)
  waiting for transfers between devices  12.6 us (9%)
  local copies, waits for them, and re-layouts  5 us (3%)
  other arithmetic  1.5 us (1%)
    all_gather x1, blocking collectives, body(): own = lax.all_gather(ff_unit, 'z', axis=0, tiled=False)  39.6 us
    ppermute x6, starting transfers between devices, ring(): return lax.ppermute(rows, ('x', 'y', 'c'), ring_pairs(step))  19.5 us
    all_to_all x1, starting transfers between devices, body(): recv = lax.all_to_all(outgoing, ('y', 'c'), 0, 0, tiled=True)  14.6 us
    all_gather x1, blocking collectives, body(): along_x = lax.all_gather(unit, 'x', axis=0, tiled=False)  10.8 us
    pallas_call x1, Pallas kernels, attend(): pl.pallas_call(attend_kernel, out_shape=(wide, wide, jax.ShapeDtypeStruct...  10.2 us
    all_to_all x1, waiting for transfers between devices, body(): recv = lax.all_to_all(outgoing, ('y', 'c'), 0, 0, tiled=True)  7.22 us
    ppermute x2, starting transfers between devices, swap(): return lax.ppermute(rows, 'c', [(0, 1), (1, 0)])  6.16 us
    pallas_call x2, Pallas kernels, encode_part(): pl.pallas_call(kernel, out_shape=outs, in_specs=[pl.BlockSpec(memory_spac...  4.94 us
  transfers between devices with their start and end apart: 10, of which 6 were waited for; matrix products, arithmetic and copies ran while one was open for 1% of the time, Pallas kernels for 5%

profile of v4, /device:TPU:1, one launch (start us, length us, event | category | flops | bytes accessed | tf_op | source)
XLA Modules:
  0.0 143.6 jit_solution(8990367215122247007)
XLA Ops:
  7.2 0.0 copy-start.5
  7.2 0.0 all-gather.4.cloned.1.call-start
  7.2 1.8 %pick_units.1 = (bf16[40,896]{1,0:T(8,128)(2,1)}, bf16[32,896]{1,0:T(8,128)(2,1)}) custom-call(s32[1]{0:T(128)} %bitcast.spot, bf16[32,896]{1,0:T(8,128)(2,1)} %bitcast.20, bf16[32,896]{1,0:T(8,128)(2,1)} %bitcast.21, bf16[28,896]{1,0:T(8,128)(2,1)} %bitcast.22, bf16[28,896]{1,0:T(8,128)(2,1)} %down_ref.1), custom_call_target="tpu_custom_call" | custom-call | tf_op jit(solution)/shard_map/pick_units/pallas_call | solution.py:94
  9.0 10.8 %all-gather = bf16[160,896]{1,0:T(8,128)(2,1)S(1)} all-gather(bf16[40,896]{1,0:T(8,128)(2,1)} %get-tuple-element.14), channel_id=2, replica_groups=mesh['z'=16,'x'=4,'y'=4,'c'=2] {'x'}, dimensions={0}, use_global_device_ids=true | all-gather | bytes 358400 | tf_op jit(solution)/shard_map/all_gather | solution.py:337
  19.8 0.7 slice.17
  20.5 0.0 all-gather.4.cloned.1.call-update
  20.6 0.8 fusion
  21.4 39.6 %all-gather.1 = bf16[512,896]{1,0:T(8,128)(2,1)S(1)} all-gather(bf16[32,896]{1,0:T(8,128)(2,1)S(1)} %fusion), channel_id=3, replica_groups=mesh['z'=16,'x'=4,'y'=4,'c'=2] {'z'}, dimensions={0}, use_global_device_ids=true | all-gather | bytes 974848 | tf_op jit(solution)/shard_map/all_gather | solution.py:342
  61.1 0.1 fusion.1
  61.2 0.0 copy-start
  61.2 2.4 %collective-permute-start = (bf16[8,32,896]{2,1,0:T(8,128)(2,1)S(1)}, bf16[8,32,896]{2,1,0:T(8,128)(2,1)S(1)}, u32[]{:S(2)}, u32[]{:S(2)}) collective-permute-start(bf16[8,32,896]{2,1,0:T(8,128)(2,1)S(1)} %get-tuple-element.26.own_a), channel_id=1, source_target_pairs={{0,2},{1,9},{2,4},{3,11},{4,6},{5,13},{6,0},{7,15},{8,10},{9,17},{... | collective-permute-start | bytes 1376264 | tf_op jit(solution)/shard_map/ppermute | solution.py:43
  63.6 4.1 %collective-permute-start.1 = (bf16[8,32,896]{2,1,0:T(8,128)(2,1)S(1)}, bf16[8,32,896]{2,1,0:T(8,128)(2,1)S(1)}, u32[]{:S(2)}, u32[]{:S(2)}) collective-permute-start(bf16[8,32,896]{2,1,0:T(8,128)(2,1)S(1)} %get-tuple-element.25.own_b), channel_id=1, source_target_pairs={{0,6},{1,25},{2,0},{3,27},{4,2},{5,29},{6,4},{7,31},{8,14},{9,1},{... | collective-permute-start | bytes 1376264 | tf_op jit(solution)/shard_map/ppermute | solution.py:43
  67.7 0.7 broadcast_subtract_fusion
  68.3 0.1 concatenate.3.meta
  68.4 0.0 copy-start.4
  68.4 1.0 copy-done.4
  69.4 1.6 %send_blocks.1 = bf16[8,64,896]{2,1,0:T(8,128)(2,1)} custom-call(s32[36]{0:T(128)S(1)} %concatenate.3.meta, bf16[4,64,896]{2,1,0:T(8,128)(2,1)S(1)} %bitcast.15), custom_call_target="tpu_custom_call" | custom-call | tf_op jit(solution)/shard_map/send_blocks/pallas_call | solution.py:57
  71.0 1.0 collective-permute-done.left_a
  72.0 1.2 collective-permute-done.1.right_b
  73.2 0.0 copy-done
  73.2 14.6 %all-to-all-start = ((bf16[8,64,896]{2,1,0:T(8,128)(2,1)}), bf16[8,64,896]{2,1,0:T(8,128)(2,1)S(1)}, u32[]{:S(2)}, u32[]{:S(2)}) async-start(bf16[8,64,896]{2,1,0:T(8,128)(2,1)} %send_blocks.1), calls=%async_computation | async-start | bytes 1835008 | tf_op jit(solution)/shard_map/all_to_all | solution.py:349
  87.7 2.4 %collective-permute-start.3 = (bf16[8,32,896]{2,1,0:T(8,128)(2,1)S(1)}, bf16[8,32,896]{2,1,0:T(8,128)(2,1)S(1)}, u32[]{:S(2)}, u32[]{:S(2)}) collective-permute-start(bf16[8,32,896]{2,1,0:T(8,128)(2,1)S(1)} %get-tuple-element.25.own_b), channel_id=1, source_target_pairs={{0,2},{1,9},{2,4},{3,11},{4,6},{5,13},{6,0},{7,15},{8,10},{9,17},{... | collective-permute-start | bytes 1376264 | tf_op jit(solution)/shard_map/ppermute | solution.py:43
  90.1 4.1 %collective-permute-start.4 = (bf16[8,32,896]{2,1,0:T(8,128)(2,1)}, bf16[8,32,896]{2,1,0:T(8,128)(2,1)S(1)}, u32[]{:S(2)}, u32[]{:S(2)}) collective-permute-start(bf16[8,32,896]{2,1,0:T(8,128)(2,1)} %copy-done), channel_id=1, source_target_pairs={{0,6},{1,25},{2,0},{3,27},{4,2},{5,29},{6,4},{7,31},{8,14},{9,1},{... | collective-permute-start | bytes 1376264 | tf_op jit(solution)/shard_map/ppermute | solution.py:43
  94.2 0.0 copy-done.5
  94.3 7.2 %all-to-all-done.recv_ref = bf16[8,64,896]{2,1,0:T(8,128)(2,1)S(1)} async-done(((bf16[8,64,896]{2,1,0:T(8,128)(2,1)}), bf16[8,64,896]{2,1,0:T(8,128)(2,1)S(1)}, u32[]{:S(2)}, u32[]{:S(2)}) %all-to-all-start) | async-done | bytes 917536 | tf_op jit(solution)/shard_map/all_to_all | solution.py:349
  101.5 1.1 place_rows.1
  102.6 2.8 %collective-permute-start.2 = (bf16[4,64,896]{2,1,0:T(8,128)(2,1)S(1)}, bf16[4,64,896]{2,1,0:T(8,128)(2,1)S(1)}, u32[]{:S(2)}, u32[]{:S(2)}) collective-permute-start(bf16[4,64,896]{2,1,0:T(8,128)(2,1)S(1)} %get-tuple-element.20.mine), channel_id=1, source_target_pairs={{0,1},{1,0},{2,3},{3,2},{4,5},{5,4},{6,7},{7,6},{8,9},{9,8},{10,11... | collective-permute-start | bytes 1376264 | tf_op jit(solution)/shard_map/ppermute | solution.py:47
  105.4 2.4 %collective-permute-start.5 = (bf16[8,32,896]{2,1,0:T(8,128)(2,1)S(1)}, bf16[8,32,896]{2,1,0:T(8,128)(2,1)S(1)}, u32[]{:S(2)}, u32[]{:S(2)}) collective-permute-start(bf16[8,32,896]{2,1,0:T(8,128)(2,1)S(1)} %collective-permute-done.left_a), channel_id=1, source_target_pairs={{0,2},{1,9},{2,4},{3,11},{4,6},{5,13},{6,0},{7,15},{8,10},{9,17},{... | collective-permute-start | bytes 1376264 | tf_op jit(solution)/shard_map/ppermute | solution.py:43
  107.8 4.1 %collective-permute-start.6 = (bf16[8,32,896]{2,1,0:T(8,128)(2,1)S(1)}, bf16[8,32,896]{2,1,0:T(8,128)(2,1)S(1)}, u32[]{:S(2)}, u32[]{:S(2)}) collective-permute-start(bf16[8,32,896]{2,1,0:T(8,128)(2,1)S(1)} %collective-permute-done.1.right_b), channel_id=1, source_target_pairs={{0,6},{1,25},{2,0},{3,27},{4,2},{5,29},{6,4},{7,31},{8,14},{9,1},{... | collective-permute-start | bytes 1376264 | tf_op jit(solution)/shard_map/ppermute | solution.py:43
  111.9 0.0 collective-permute-done.3.left_b
  111.9 0.0 collective-permute-done.4.right_a
  111.9 0.0 collective-permute-done.2.other
  111.9 0.0 copy-start.1
  112.0 1.0 copy-done.1
  113.0 3.0 %early_kernel.1.acc = f32[512,896]{1,0:T(8,128)S(1)} custom-call(s32[36]{0:T(128)S(1)} %concatenate.3.meta, bf16[4,64,896]{2,1,0:T(8,128)(2,1)S(1)} %get-tuple-element.20.mine, bf16[4,64,896]{2,1,0:T(8,128)(2,1)S(1)} %collective-permute-done.2.other, bf16[8,32,896]{2,1,0:T(8,128)(2,1)S(1)} %copy-done.1, bf16[8,32,896]{2,1,0:T(8,128)(2,1)S(1)} %get-tuple-element.25.own_b, ...), custom_call_target="tpu_custom_call" | custom-call | tf_op jit(solution)/shard_map/early_kernel/pallas_call | solution.py:218
  116.0 0.1 collective-permute-done.5.far_a
  116.1 1.2 collective-permute-done.6.far_b
  117.3 1.9 %late_kernel.1 = (f32[256,896]{1,0:T(8,128)S(1)}, f32[256,896]{1,0:T(8,128)S(1)}) custom-call(s32[36]{0:T(128)S(1)} %concatenate.3.meta, bf16[4,64,896]{2,1,0:T(8,128)(2,1)S(1)} %get-tuple-element.19.raw, bf16[4,64,896]{2,1,0:T(8,128)(2,1)S(1)} %get-tuple-element.20.mine, bf16[4,64,896]{2,1,0:T(8,128)(2,1)S(1)} %collective-permute-done.2.other, ...), custom_call_target="tpu_custom_call" | custom-call | tf_op jit(solution)/shard_map/late_kernel/pallas_call | solution.py:218
  119.2 3.3 %collective-permute-start.7 = (f32[256,896]{1,0:T(8,128)S(1)}, f32[256,896]{1,0:T(8,128)S(1)}, u32[]{:S(2)}, u32[]{:S(2)}) collective-permute-start(f32[256,896]{1,0:T(8,128)S(1)} %get-tuple-element.24), channel_id=1, source_target_pairs={{0,1},{1,0},{2,3},{3,2},{4,5},{5,4},{6,7},{7,6},{8,9},{9,8},{10,11... | collective-permute-start | bytes 2752520 | tf_op jit(solution)/shard_map/ppermute | solution.py:47
  122.5 1.9 %collective-permute-done.7.other_ref = f32[256,896]{1,0:T(8,128)S(1)} collective-permute-done((f32[256,896]{1,0:T(8,128)S(1)}, f32[256,896]{1,0:T(8,128)S(1)}, u32[]{:S(2)}, u32[]{:S(2)}) %collective-permute-start.7) | collective-permute-done | bytes 917536 | tf_op jit(solution)/shard_map/ppermute | solution.py:47
  124.4 0.0 all-gather.4.cloned.1.call-done.w_hbm
  124.4 0.0 copy-start.2
  124.5 1.0 copy-done.2
  125.5 0.0 copy-start.3
  125.5 1.0 copy-done.3
  126.5 10.2 %attend_spans.1 = (bf16[128,2048]{1,0:T(8,128)(2,1)}, bf16[128,2048]{1,0:T(8,128)(2,1)}, bf16[256,896]{1,0:T(8,128)(2,1)}) custom-call(f32[256,896]{1,0:T(8,128)S(1)} %get-tuple-element.23.mine_ref, f32[256,896]{1,0:T(8,128)S(1)} %collective-permute-done.7.other_ref, bf16[32,128,896]{2,1,0:T(8,128)(2,1)} %all-gather.4.cloned.1.call-done.w_hbm, ...), custom_call_target="tpu_custom_call" | custom-call | tf_op jit(solution)/shard_map/attend_spans/pallas_call | solution.py:308
  (1 shorter events, 0.0 us)
Async XLA Ops:
  7.2 87.1 %copy-start.5 = (f32[896]{0:T(1024)S(1)}, f32[896]{0:T(1024)}, u32[]{:S(2)}) copy-start(f32[896]{0:T(1024)} %param.12) | copy-start | bytes 10756
  7.2 117.3 %all-gather.4.cloned.1.call-start = ((), (), s32[]{:S(2)}) async-start(), calls=%async_computation.1 | async-start | bytes 7569408 | tf_op jit(solution)/shard_map/all_gather | solution.py:339
  61.2 12.0 %copy-start = (bf16[8,32,896]{2,1,0:T(8,128)(2,1)}, bf16[8,32,896]{2,1,0:T(8,128)(2,1)S(1)}, u32[]{:S(2)}) copy-start(bf16[8,32,896]{2,1,0:T(8,128)(2,1)S(1)} %get-tuple-element.26.own_a) | copy-start | bytes 1376260
  61.2 10.8 %collective-permute-start = (bf16[8,32,896]{2,1,0:T(8,128)(2,1)S(1)}, bf16[8,32,896]{2,1,0:T(8,128)(2,1)S(1)}, u32[]{:S(2)}, u32[]{:S(2)}) collective-permute-start(bf16[8,32,896]{2,1,0:T(8,128)(2,1)S(1)} %get-tuple-element.26.own_a), channel_id=1, source_target_pairs={{0,2},{1,9},{2,4},{3,11},{4,6},{5,13},{6,0},{7,15},{8,10},{9,17},{... | collective-permute-start | bytes 1376264 | tf_op jit(solution)/shard_map/ppermute | solution.py:43
  63.6 9.6 %collective-permute-start.1 = (bf16[8,32,896]{2,1,0:T(8,128)(2,1)S(1)}, bf16[8,32,896]{2,1,0:T(8,128)(2,1)S(1)}, u32[]{:S(2)}, u32[]{:S(2)}) collective-permute-start(bf16[8,32,896]{2,1,0:T(8,128)(2,1)S(1)} %get-tuple-element.25.own_b), channel_id=1, source_target_pairs={{0,6},{1,25},{2,0},{3,27},{4,2},{5,29},{6,4},{7,31},{8,14},{9,1},{... | collective-permute-start | bytes 1376264 | tf_op jit(solution)/shard_map/ppermute | solution.py:43
  68.4 1.0 copy-start.4
  73.2 28.3 %all-to-all-start = ((bf16[8,64,896]{2,1,0:T(8,128)(2,1)}), bf16[8,64,896]{2,1,0:T(8,128)(2,1)S(1)}, u32[]{:S(2)}, u32[]{:S(2)}) async-start(bf16[8,64,896]{2,1,0:T(8,128)(2,1)} %send_blocks.1), calls=%async_computation | async-start | bytes 1835008 | tf_op jit(solution)/shard_map/all_to_all | solution.py:349
  87.7 24.2 %collective-permute-start.3 = (bf16[8,32,896]{2,1,0:T(8,128)(2,1)S(1)}, bf16[8,32,896]{2,1,0:T(8,128)(2,1)S(1)}, u32[]{:S(2)}, u32[]{:S(2)}) collective-permute-start(bf16[8,32,896]{2,1,0:T(8,128)(2,1)S(1)} %get-tuple-element.25.own_b), channel_id=1, source_target_pairs={{0,2},{1,9},{2,4},{3,11},{4,6},{5,13},{6,0},{7,15},{8,10},{9,17},{... | collective-permute-start | bytes 1376264 | tf_op jit(solution)/shard_map/ppermute | solution.py:43
  90.1 21.8 %collective-permute-start.4 = (bf16[8,32,896]{2,1,0:T(8,128)(2,1)}, bf16[8,32,896]{2,1,0:T(8,128)(2,1)S(1)}, u32[]{:S(2)}, u32[]{:S(2)}) collective-permute-start(bf16[8,32,896]{2,1,0:T(8,128)(2,1)} %copy-done), channel_id=1, source_target_pairs={{0,6},{1,25},{2,0},{3,27},{4,2},{5,29},{6,4},{7,31},{8,14},{9,1},{... | collective-permute-start | bytes 1376264 | tf_op jit(solution)/shard_map/ppermute | solution.py:43
  102.6 9.4 %collective-permute-start.2 = (bf16[4,64,896]{2,1,0:T(8,128)(2,1)S(1)}, bf16[4,64,896]{2,1,0:T(8,128)(2,1)S(1)}, u32[]{:S(2)}, u32[]{:S(2)}) collective-permute-start(bf16[4,64,896]{2,1,0:T(8,128)(2,1)S(1)} %get-tuple-element.20.mine), channel_id=1, source_target_pairs={{0,1},{1,0},{2,3},{3,2},{4,5},{5,4},{6,7},{7,6},{8,9},{9,8},{10,11... | collective-permute-start | bytes 1376264 | tf_op jit(solution)/shard_map/ppermute | solution.py:47
  105.4 10.7 %collective-permute-start.5 = (bf16[8,32,896]{2,1,0:T(8,128)(2,1)S(1)}, bf16[8,32,896]{2,1,0:T(8,128)(2,1)S(1)}, u32[]{:S(2)}, u32[]{:S(2)}) collective-permute-start(bf16[8,32,896]{2,1,0:T(8,128)(2,1)S(1)} %collective-permute-done.left_a), channel_id=1, source_target_pairs={{0,2},{1,9},{2,4},{3,11},{4,6},{5,13},{6,0},{7,15},{8,10},{9,17},{... | collective-permute-start | bytes 1376264 | tf_op jit(solution)/shard_map/ppermute | solution.py:43
  107.8 9.5 %collective-permute-start.6 = (bf16[8,32,896]{2,1,0:T(8,128)(2,1)S(1)}, bf16[8,32,896]{2,1,0:T(8,128)(2,1)S(1)}, u32[]{:S(2)}, u32[]{:S(2)}) collective-permute-start(bf16[8,32,896]{2,1,0:T(8,128)(2,1)S(1)} %collective-permute-done.1.right_b), channel_id=1, source_target_pairs={{0,6},{1,25},{2,0},{3,27},{4,2},{5,29},{6,4},{7,31},{8,14},{9,1},{... | collective-permute-start | bytes 1376264 | tf_op jit(solution)/shard_map/ppermute | solution.py:43
  111.9 1.0 copy-start.1
  119.2 5.2 %collective-permute-start.7 = (f32[256,896]{1,0:T(8,128)S(1)}, f32[256,896]{1,0:T(8,128)S(1)}, u32[]{:S(2)}, u32[]{:S(2)}) collective-permute-start(f32[256,896]{1,0:T(8,128)S(1)} %get-tuple-element.24), channel_id=1, source_target_pairs={{0,1},{1,0},{2,3},{3,2},{4,5},{5,4},{6,7},{7,6},{8,9},{9,8},{10,11... | collective-permute-start | bytes 2752520 | tf_op jit(solution)/shard_map/ppermute | solution.py:47
  124.4 1.0 copy-start.2
  125.5 1.0 copy-start.3
Sparse Core Ops, SparseCore 0:
  20.7 87.8 all-gather.3

commit v5 on v4

--- a/solution.py
+++ b/solution.py
@@ -338,15 +338,16 @@
     kv_head = along_x[:, :32].reshape(HD, E)
     weights = lax.all_gather(kv_head, ("z", "c"), axis=0, tiled=False)
 
+    outgoing = send_blocks(meta, neighbours.reshape(PER_DEV, NLEN, E))
     ff_unit = jnp.where(c == 0, along_x[:, 32:].reshape(32, E), whole)
+    ff_unit, outgoing = lax.optimization_barrier((ff_unit, outgoing))
+    recv = lax.all_to_all(outgoing, ("y", "c"), 0, 0, tiled=True)
     own = lax.all_gather(ff_unit, "z", axis=0, tiled=False)
-    own, rows = lax.optimization_barrier((own, neighbours))
-    outgoing = send_blocks(meta, rows.reshape(PER_DEV, NLEN, E))
+    own, recv = lax.optimization_barrier((own, recv))
     own_a, own_b = own[: NZ // 2], own[NZ // 2 :]
     left_a, right_b = ring(own_a, 1), ring(own_b, -1)
     left_b, right_a = ring(own_b, 1), ring(own_a, -1)
-    left_a, right_b, outgoing = lax.optimization_barrier((left_a, right_b, outgoing))
-    recv = lax.all_to_all(outgoing, ("y", "c"), 0, 0, tiled=True)
+    left_a, right_b, recv = lax.optimization_barrier((left_a, right_b, recv))
     raw, normed = place(meta, recv, gain.reshape(1, E))
     other = swap(normed)
     far_a, far_b = ring(left_a, 1), ring(right_b, -1)

time: 144 us -> 136 us (0.944)
  waiting for transfers between devices: 12.6 us -> 4.65 us
  starting transfers between devices: 40.2 us -> 43.8 us
  local copies, waits for them, and re-layouts: 5 us -> 1.9 us
    all_to_all x1, waiting for transfers between devices: 7.22 us -> 0.01 us  [body(): recv = lax.all_to_all(outgoing, ('y', 'c'), 0, 0, tiled=True)]
    ppermute x2, starting transfers between devices: 6.16 us -> 12.9 us  [swap(): return lax.ppermute(rows, 'c', [(0, 1), (1, 0)])]
    all_to_all x1, starting transfers between devices: 14.6 us -> 11.2 us  [body(): recv = lax.all_to_all(outgoing, ('y', 'c'), 0, 0, tiled=True)]
    unnamed x12 -> x8, local copies, waits for them, and re-layouts: 4.13 us -> 1.03 us
  transfers between devices with their start and end apart: 10 -> 10, of which waited for: 6 -> 3; matrix products, arithmetic and copies ran while one was open for 1% -> 1% of each run, Pallas kernels for 5% -> 6%
where the time goes in v5:
time: 136 us; the launch traced here: 135 us
  blocking collectives  49.4 us (36%)
  starting transfers between devices  43.8 us (32%)
  Pallas kernels  19.6 us (14%)
  between operations  14.2 us (10%)
  waiting for transfers between devices  4.65 us (3%)
  local copies, waits for them, and re-layouts  1.9 us (1%)
  other arithmetic  1.49 us (1%)
    all_gather x1, blocking collectives, body(): own = lax.all_gather(ff_unit, 'z', axis=0, tiled=False)  38.6 us
    ppermute x6, starting transfers between devices, ring(): return lax.ppermute(rows, ('x', 'y', 'c'), ring_pairs(step))  19.6 us
    ppermute x2, starting transfers between devices, swap(): return lax.ppermute(rows, 'c', [(0, 1), (1, 0)])  12.9 us
    all_to_all x1, starting transfers between devices, body(): recv = lax.all_to_all(outgoing, ('y', 'c'), 0, 0, tiled=True)  11.2 us
    all_gather x1, blocking collectives, body(): along_x = lax.all_gather(unit, 'x', axis=0, tiled=False)  10.8 us
    pallas_call x1, Pallas kernels, attend(): pl.pallas_call(attend_kernel, out_shape=(wide, wide, jax.ShapeDtypeStruct...  10.2 us
    pallas_call x2, Pallas kernels, encode_part(): pl.pallas_call(kernel, out_shape=outs, in_specs=[pl.BlockSpec(memory_spac...  4.94 us
    ppermute x6, waiting for transfers between devices, ring(): return lax.ppermute(rows, ('x', 'y', 'c'), ring_pairs(step))  2.73 us
  transfers between devices with their start and end apart: 10, of which 3 were waited for; matrix products, arithmetic and copies ran while one was open for 1% of the time, Pallas kernels for 6%

profile of v5, /device:TPU:1, one launch (start us, length us, event | category | flops | bytes accessed | tf_op | source)
XLA Modules:
  0.0 135.0 jit_solution(5052751317010112239)
XLA Ops:
  7.2 0.0 copy-start.3
  7.2 0.0 all-gather.4.cloned.1.call-start
  7.2 1.8 %pick_units.1 = (bf16[40,896]{1,0:T(8,128)(2,1)}, bf16[32,896]{1,0:T(8,128)(2,1)}) custom-call(s32[1]{0:T(128)} %bitcast.spot, bf16[32,896]{1,0:T(8,128)(2,1)} %bitcast.20, bf16[32,896]{1,0:T(8,128)(2,1)} %bitcast.21, bf16[28,896]{1,0:T(8,128)(2,1)} %bitcast.22, bf16[28,896]{1,0:T(8,128)(2,1)} %down_ref.1), custom_call_target="tpu_custom_call" | custom-call | tf_op jit(solution)/shard_map/pick_units/pallas_call | solution.py:94
  9.0 10.8 %all-gather = bf16[160,896]{1,0:T(8,128)(2,1)S(1)} all-gather(bf16[40,896]{1,0:T(8,128)(2,1)} %get-tuple-element.16), channel_id=2, replica_groups=mesh['z'=16,'x'=4,'y'=4,'c'=2] {'x'}, dimensions={0}, use_global_device_ids=true | all-gather | bytes 358400 | tf_op jit(solution)/shard_map/all_gather | solution.py:337
  19.8 0.7 slice.17
  20.6 0.0 all-gather.4.cloned.1.call-update
  20.6 0.7 broadcast_subtract_fusion
  21.2 0.1 concatenate.3.meta
  21.3 0.0 copy-start.2
  21.3 1.0 copy-done.2
  22.4 1.6 %send_blocks.1 = bf16[8,64,896]{2,1,0:T(8,128)(2,1)} custom-call(s32[36]{0:T(128)S(1)} %concatenate.3.meta, bf16[4,64,896]{2,1,0:T(8,128)(2,1)S(1)} %bitcast.15), custom_call_target="tpu_custom_call" | custom-call | tf_op jit(solution)/shard_map/send_blocks/pallas_call | solution.py:57
  23.9 0.8 fusion
  24.7 11.2 %all-to-all-start = ((bf16[8,64,896]{2,1,0:T(8,128)(2,1)}), bf16[8,64,896]{2,1,0:T(8,128)(2,1)S(1)}, u32[]{:S(2)}, u32[]{:S(2)}) async-start(bf16[8,64,896]{2,1,0:T(8,128)(2,1)} %send_blocks.1), calls=%async_computation | async-start | bytes 1835008 | tf_op jit(solution)/shard_map/all_to_all | solution.py:344
  36.0 38.6 %all-gather.1 = bf16[512,896]{1,0:T(8,128)(2,1)S(1)} all-gather(bf16[32,896]{1,0:T(8,128)(2,1)S(1)} %fusion), channel_id=3, replica_groups=mesh['z'=16,'x'=4,'y'=4,'c'=2] {'z'}, dimensions={0}, use_global_device_ids=true | all-gather | bytes 974848 | tf_op jit(solution)/shard_map/all_gather | solution.py:345
  74.6 0.0 copy-start
  74.6 0.0 copy-start.1
  74.6 0.0 all-to-all-done.recv_ref
  74.6 0.1 fusion.1
  74.7 2.6 %collective-permute-start = (bf16[8,32,896]{2,1,0:T(8,128)(2,1)S(1)}, bf16[8,32,896]{2,1,0:T(8,128)(2,1)S(1)}, u32[]{:S(2)}, u32[]{:S(2)}) collective-permute-start(bf16[8,32,896]{2,1,0:T(8,128)(2,1)S(1)} %get-tuple-element.30.own_a), channel_id=1, source_target_pairs={{0,2},{1,9},{2,4},{3,11},{4,6},{5,13},{6,0},{7,15},{8,10},{9,17},{... | collective-permute-start | bytes 1376264 | tf_op jit(solution)/shard_map/ppermute | solution.py:43
  77.4 4.0 %collective-permute-start.1 = (bf16[8,32,896]{2,1,0:T(8,128)(2,1)S(1)}, bf16[8,32,896]{2,1,0:T(8,128)(2,1)S(1)}, u32[]{:S(2)}, u32[]{:S(2)}) collective-permute-start(bf16[8,32,896]{2,1,0:T(8,128)(2,1)S(1)} %get-tuple-element.29.own_b), channel_id=1, source_target_pairs={{0,6},{1,25},{2,0},{3,27},{4,2},{5,29},{6,4},{7,31},{8,14},{9,1},{... | collective-permute-start | bytes 1376264 | tf_op jit(solution)/shard_map/ppermute | solution.py:43
  81.3 0.0 copy-done.3
  81.4 1.9 %collective-permute-start.3 = (bf16[8,32,896]{2,1,0:T(8,128)(2,1)S(1)}, bf16[8,32,896]{2,1,0:T(8,128)(2,1)S(1)}, u32[]{:S(2)}, u32[]{:S(2)}) collective-permute-start(bf16[8,32,896]{2,1,0:T(8,128)(2,1)S(1)} %get-tuple-element.29.own_b), channel_id=1, source_target_pairs={{0,2},{1,9},{2,4},{3,11},{4,6},{5,13},{6,0},{7,15},{8,10},{9,17},{... | collective-permute-start | bytes 1376264 | tf_op jit(solution)/shard_map/ppermute | solution.py:43
  83.3 4.6 %collective-permute-start.4 = (bf16[8,32,896]{2,1,0:T(8,128)(2,1)S(1)}, bf16[8,32,896]{2,1,0:T(8,128)(2,1)S(1)}, u32[]{:S(2)}, u32[]{:S(2)}) collective-permute-start(bf16[8,32,896]{2,1,0:T(8,128)(2,1)S(1)} %get-tuple-element.30.own_a), channel_id=1, source_target_pairs={{0,6},{1,25},{2,0},{3,27},{4,2},{5,29},{6,4},{7,31},{8,14},{9,1},{... | collective-permute-start | bytes 1376264 | tf_op jit(solution)/shard_map/ppermute | solution.py:43
  87.9 0.0 collective-permute-done.left_a
  87.9 0.0 collective-permute-done.1.right_b
  87.9 1.1 place_rows.1
  89.0 9.4 %collective-permute-start.2 = (bf16[4,64,896]{2,1,0:T(8,128)(2,1)S(1)}, bf16[4,64,896]{2,1,0:T(8,128)(2,1)S(1)}, u32[]{:S(2)}, u32[]{:S(2)}) collective-permute-start(bf16[4,64,896]{2,1,0:T(8,128)(2,1)S(1)} %get-tuple-element.24.mine), channel_id=1, source_target_pairs={{0,1},{1,0},{2,3},{3,2},{4,5},{5,4},{6,7},{7,6},{8,9},{9,8},{10,11... | collective-permute-start | bytes 1376264 | tf_op jit(solution)/shard_map/ppermute | solution.py:47
  98.4 2.8 %collective-permute-start.5 = (bf16[8,32,896]{2,1,0:T(8,128)(2,1)S(1)}, bf16[8,32,896]{2,1,0:T(8,128)(2,1)S(1)}, u32[]{:S(2)}, u32[]{:S(2)}) collective-permute-start(bf16[8,32,896]{2,1,0:T(8,128)(2,1)S(1)} %collective-permute-done.left_a), channel_id=1, source_target_pairs={{0,2},{1,9},{2,4},{3,11},{4,6},{5,13},{6,0},{7,15},{8,10},{9,17},{... | collective-permute-start | bytes 1376264 | tf_op jit(solution)/shard_map/ppermute | solution.py:43
  101.2 3.7 %collective-permute-start.6 = (bf16[8,32,896]{2,1,0:T(8,128)(2,1)S(1)}, bf16[8,32,896]{2,1,0:T(8,128)(2,1)S(1)}, u32[]{:S(2)}, u32[]{:S(2)}) collective-permute-start(bf16[8,32,896]{2,1,0:T(8,128)(2,1)S(1)} %collective-permute-done.1.right_b), channel_id=1, source_target_pairs={{0,6},{1,25},{2,0},{3,27},{4,2},{5,29},{6,4},{7,31},{8,14},{9,1},{... | collective-permute-start | bytes 1376264 | tf_op jit(solution)/shard_map/ppermute | solution.py:43
  104.9 0.0 collective-permute-done.3.left_b
  104.9 0.0 collective-permute-done.4.right_a
  105.0 0.0 collective-permute-done.2.other
  105.0 3.0 %early_kernel.1.acc = f32[512,896]{1,0:T(8,128)S(1)} custom-call(s32[36]{0:T(128)S(1)} %concatenate.3.meta, bf16[4,64,896]{2,1,0:T(8,128)(2,1)S(1)} %get-tuple-element.24.mine, bf16[4,64,896]{2,1,0:T(8,128)(2,1)S(1)} %collective-permute-done.2.other, bf16[8,32,896]{2,1,0:T(8,128)(2,1)S(1)} %get-tuple-element.30.own_a, ...), custom_call_target="tpu_custom_call" | custom-call | tf_op jit(solution)/shard_map/early_kernel/pallas_call | solution.py:218
  108.0 1.1 collective-permute-done.5.far_a
  109.2 1.6 %collective-permute-done.6.far_b = bf16[8,32,896]{2,1,0:T(8,128)(2,1)S(1)} collective-permute-done((bf16[8,32,896]{2,1,0:T(8,128)(2,1)S(1)}, bf16[8,32,896]{2,1,0:T(8,128)(2,1)S(1)}, u32[]{:S(2)}, u32[]{:S(2)}) %collective-permute-start.6) | collective-permute-done | bytes 458784 | tf_op jit(solution)/shard_map/ppermute | solution.py:43
  110.7 1.9 %late_kernel.1 = (f32[256,896]{1,0:T(8,128)S(1)}, f32[256,896]{1,0:T(8,128)S(1)}) custom-call(s32[36]{0:T(128)S(1)} %concatenate.3.meta, bf16[4,64,896]{2,1,0:T(8,128)(2,1)S(1)} %get-tuple-element.23.raw, bf16[4,64,896]{2,1,0:T(8,128)(2,1)S(1)} %get-tuple-element.24.mine, bf16[4,64,896]{2,1,0:T(8,128)(2,1)S(1)} %collective-permute-done.2.other, ...), custom_call_target="tpu_custom_call" | custom-call | tf_op jit(solution)/shard_map/late_kernel/pallas_call | solution.py:218
  112.6 3.4 %collective-permute-start.7 = (f32[256,896]{1,0:T(8,128)S(1)}, f32[256,896]{1,0:T(8,128)S(1)}, u32[]{:S(2)}, u32[]{:S(2)}) collective-permute-start(f32[256,896]{1,0:T(8,128)S(1)} %get-tuple-element.28), channel_id=1, source_target_pairs={{0,1},{1,0},{2,3},{3,2},{4,5},{5,4},{6,7},{7,6},{8,9},{9,8},{10,11... | collective-permute-start | bytes 2752520 | tf_op jit(solution)/shard_map/ppermute | solution.py:47
  116.1 1.9 %collective-permute-done.7.other_ref = f32[256,896]{1,0:T(8,128)S(1)} collective-permute-done((f32[256,896]{1,0:T(8,128)S(1)}, f32[256,896]{1,0:T(8,128)S(1)}, u32[]{:S(2)}, u32[]{:S(2)}) %collective-permute-start.7) | collective-permute-done | bytes 917536 | tf_op jit(solution)/shard_map/ppermute | solution.py:47
  118.0 0.0 all-gather.4.cloned.1.call-done.w_hbm
  118.0 0.0 copy-done
  118.0 0.0 copy-done.1
  118.0 10.2 %attend_spans.1 = (bf16[128,2048]{1,0:T(8,128)(2,1)}, bf16[128,2048]{1,0:T(8,128)(2,1)}, bf16[256,896]{1,0:T(8,128)(2,1)}) custom-call(f32[256,896]{1,0:T(8,128)S(1)} %get-tuple-element.27.mine_ref, f32[256,896]{1,0:T(8,128)S(1)} %collective-permute-done.7.other_ref, bf16[32,128,896]{2,1,0:T(8,128)(2,1)} %all-gather.4.cloned.1.call-done.w_hbm, ...), custom_call_target="tpu_custom_call" | custom-call | tf_op jit(solution)/shard_map/attend_spans/pallas_call | solution.py:308
  (1 shorter events, 0.0 us)
Async XLA Ops:
  7.2 74.2 %copy-start.3 = (f32[896]{0:T(1024)S(1)}, f32[896]{0:T(1024)}, u32[]{:S(2)}) copy-start(f32[896]{0:T(1024)} %param.12) | copy-start | bytes 10756
  7.2 110.8 %all-gather.4.cloned.1.call-start = ((), (), s32[]{:S(2)}) async-start(), calls=%async_computation.1 | async-start | bytes 7569408 | tf_op jit(solution)/shard_map/all_gather | solution.py:339
  21.3 1.0 copy-start.2
  24.7 49.9 %all-to-all-start = ((bf16[8,64,896]{2,1,0:T(8,128)(2,1)}), bf16[8,64,896]{2,1,0:T(8,128)(2,1)S(1)}, u32[]{:S(2)}, u32[]{:S(2)}) async-start(bf16[8,64,896]{2,1,0:T(8,128)(2,1)} %send_blocks.1), calls=%async_computation | async-start | bytes 1835008 | tf_op jit(solution)/shard_map/all_to_all | solution.py:344
  74.6 43.3 %copy-start = (bf16[128,2048]{1,0:T(8,128)(2,1)S(1)}, bf16[128,2048]{1,0:T(8,128)(2,1)}, u32[]{:S(2)}) copy-start(bf16[128,2048]{1,0:T(8,128)(2,1)} %q_hbm.1) | copy-start | bytes 1572868
  74.6 43.3 %copy-start.1 = (bf16[128,2048]{1,0:T(8,128)(2,1)S(1)}, bf16[128,2048]{1,0:T(8,128)(2,1)}, u32[]{:S(2)}) copy-start(bf16[128,2048]{1,0:T(8,128)(2,1)} %g_hbm.1) | copy-start | bytes 1572868
  74.7 13.2 %collective-permute-start = (bf16[8,32,896]{2,1,0:T(8,128)(2,1)S(1)}, bf16[8,32,896]{2,1,0:T(8,128)(2,1)S(1)}, u32[]{:S(2)}, u32[]{:S(2)}) collective-permute-start(bf16[8,32,896]{2,1,0:T(8,128)(2,1)S(1)} %get-tuple-element.30.own_a), channel_id=1, source_target_pairs={{0,2},{1,9},{2,4},{3,11},{4,6},{5,13},{6,0},{7,15},{8,10},{9,17},{... | collective-permute-start | bytes 1376264 | tf_op jit(solution)/shard_map/ppermute | solution.py:43
  77.4 10.5 %collective-permute-start.1 = (bf16[8,32,896]{2,1,0:T(8,128)(2,1)S(1)}, bf16[8,32,896]{2,1,0:T(8,128)(2,1)S(1)}, u32[]{:S(2)}, u32[]{:S(2)}) collective-permute-start(bf16[8,32,896]{2,1,0:T(8,128)(2,1)S(1)} %get-tuple-element.29.own_b), channel_id=1, source_target_pairs={{0,6},{1,25},{2,0},{3,27},{4,2},{5,29},{6,4},{7,31},{8,14},{9,1},{... | collective-permute-start | bytes 1376264 | tf_op jit(solution)/shard_map/ppermute | solution.py:43
  81.4 23.6 %collective-permute-start.3 = (bf16[8,32,896]{2,1,0:T(8,128)(2,1)S(1)}, bf16[8,32,896]{2,1,0:T(8,128)(2,1)S(1)}, u32[]{:S(2)}, u32[]{:S(2)}) collective-permute-start(bf16[8,32,896]{2,1,0:T(8,128)(2,1)S(1)} %get-tuple-element.29.own_b), channel_id=1, source_target_pairs={{0,2},{1,9},{2,4},{3,11},{4,6},{5,13},{6,0},{7,15},{8,10},{9,17},{... | collective-permute-start | bytes 1376264 | tf_op jit(solution)/shard_map/ppermute | solution.py:43
  83.3 21.6 %collective-permute-start.4 = (bf16[8,32,896]{2,1,0:T(8,128)(2,1)S(1)}, bf16[8,32,896]{2,1,0:T(8,128)(2,1)S(1)}, u32[]{:S(2)}, u32[]{:S(2)}) collective-permute-start(bf16[8,32,896]{2,1,0:T(8,128)(2,1)S(1)} %get-tuple-element.30.own_a), channel_id=1, source_target_pairs={{0,6},{1,25},{2,0},{3,27},{4,2},{5,29},{6,4},{7,31},{8,14},{9,1},{... | collective-permute-start | bytes 1376264 | tf_op jit(solution)/shard_map/ppermute | solution.py:43
  89.0 16.0 %collective-permute-start.2 = (bf16[4,64,896]{2,1,0:T(8,128)(2,1)S(1)}, bf16[4,64,896]{2,1,0:T(8,128)(2,1)S(1)}, u32[]{:S(2)}, u32[]{:S(2)}) collective-permute-start(bf16[4,64,896]{2,1,0:T(8,128)(2,1)S(1)} %get-tuple-element.24.mine), channel_id=1, source_target_pairs={{0,1},{1,0},{2,3},{3,2},{4,5},{5,4},{6,7},{7,6},{8,9},{9,8},{10,11... | collective-permute-start | bytes 1376264 | tf_op jit(solution)/shard_map/ppermute | solution.py:47
  98.4 10.7 %collective-permute-start.5 = (bf16[8,32,896]{2,1,0:T(8,128)(2,1)S(1)}, bf16[8,32,896]{2,1,0:T(8,128)(2,1)S(1)}, u32[]{:S(2)}, u32[]{:S(2)}) collective-permute-start(bf16[8,32,896]{2,1,0:T(8,128)(2,1)S(1)} %collective-permute-done.left_a), channel_id=1, source_target_pairs={{0,2},{1,9},{2,4},{3,11},{4,6},{5,13},{6,0},{7,15},{8,10},{9,17},{... | collective-permute-start | bytes 1376264 | tf_op jit(solution)/shard_map/ppermute | solution.py:43
  101.2 9.5 %collective-permute-start.6 = (bf16[8,32,896]{2,1,0:T(8,128)(2,1)S(1)}, bf16[8,32,896]{2,1,0:T(8,128)(2,1)S(1)}, u32[]{:S(2)}, u32[]{:S(2)}) collective-permute-start(bf16[8,32,896]{2,1,0:T(8,128)(2,1)S(1)} %collective-permute-done.1.right_b), channel_id=1, source_target_pairs={{0,6},{1,25},{2,0},{3,27},{4,2},{5,29},{6,4},{7,31},{8,14},{9,1},{... | collective-permute-start | bytes 1376264 | tf_op jit(solution)/shard_map/ppermute | solution.py:43
  112.6 5.3 %collective-permute-start.7 = (f32[256,896]{1,0:T(8,128)S(1)}, f32[256,896]{1,0:T(8,128)S(1)}, u32[]{:S(2)}, u32[]{:S(2)}) collective-permute-start(f32[256,896]{1,0:T(8,128)S(1)} %get-tuple-element.28), channel_id=1, source_target_pairs={{0,1},{1,0},{2,3},{3,2},{4,5},{5,4},{6,7},{7,6},{8,9},{9,8},{10,11... | collective-permute-start | bytes 2752520 | tf_op jit(solution)/shard_map/ppermute | solution.py:47
Sparse Core Ops, SparseCore 0:
  20.7 88.4 all-gather.3

commit v6 on v5

--- a/solution.py
+++ b/solution.py
@@ -15,6 +15,7 @@
 NZ, NX, NY, NC = 16, 4, 4, 2
 PER_DEV = CH_DEV * NPC
 ROWS = PER_DEV * NLEN
+GROUP_SLOTS = NY * NC * PER_DEV
 UNITS = 28
 HALF = UNITS // 2
 QUART = UNITS // 4
@@ -47,24 +48,11 @@
     return lax.ppermute(rows, "c", [(0, 1), (1, 0)])
 
 
-def send_kernel(meta, raw_ref, out_ref):
+def units_kernel(
+    slots, spot, raw_ref, key_ref, value_ref, up_ref, down_ref, unit_ref, whole_ref, out_ref
+):
     for i in range(PER_DEV):
-        out_ref[meta[PER_DEV * meta[32] + i] // PER_DEV] = raw_ref[i]
-
-
-def send_blocks(meta, raw):
-    vmem = pl.BlockSpec(memory_space=pltpu.VMEM)
-    return pl.pallas_call(
-        send_kernel,
-        out_shape=jax.ShapeDtypeStruct((NY * NC, NLEN, E), jnp.bfloat16),
-        in_specs=[pl.BlockSpec(memory_space=pltpu.SMEM), vmem],
-        out_specs=vmem,
-        compiler_params=pltpu.CompilerParams(vmem_limit_bytes=8 * 1024 * 1024),
-        name="send_blocks",
-    )(meta, raw)
-
-
-def units_kernel(spot, key_ref, value_ref, up_ref, down_ref, unit_ref, whole_ref):
+        out_ref[slots[PER_DEV * spot[0] + i] % GROUP_SLOTS // PER_DEV] = raw_ref[i]
     core, y = spot[0] % 2, spot[0] // 2 % NY
 
     def pick(ref, count, start, rows, offset, length):
@@ -89,29 +77,30 @@
     ).astype(jnp.bfloat16)
 
 
-def units(spot, key_rows, value_rows, up_rows, down_rows):
+def units(slots, spot, raw, key_rows, value_rows, up_rows, down_rows):
     vmem = pl.BlockSpec(memory_space=pltpu.VMEM)
     return pl.pallas_call(
         units_kernel,
         out_shape=(
             jax.ShapeDtypeStruct((40, E), jnp.bfloat16),
             jax.ShapeDtypeStruct((32, E), jnp.bfloat16),
+            jax.ShapeDtypeStruct((NY * NC, NLEN, E), jnp.bfloat16),
         ),
-        in_specs=[pl.BlockSpec(memory_space=pltpu.SMEM)] + [vmem] * 4,
-        out_specs=(vmem, vmem),
+        in_specs=[pl.BlockSpec(memory_space=pltpu.SMEM)] * 2 + [vmem] * 5,
+        out_specs=(vmem, vmem, vmem),
         compiler_params=pltpu.CompilerParams(vmem_limit_bytes=56 * 1024 * 1024),
         name="pick_units",
-    )(spot, key_rows, value_rows, up_rows, down_rows)
+    )(slots, spot, raw, key_rows, value_rows, up_rows, down_rows)
 
 
 def gelu(x):
     return 0.5 * x * (1.0 + jnp.tanh(0.7978845608028654 * (x + 0.044715 * (x * x * x))))
 
 
-def place_kernel(meta, recv_ref, gain_ref, raw_ref, normed_ref):
-    first = PER_DEV * meta[32]
-    for n in range(NY * NC * PER_DEV):
-        slot = meta[n] - first
+def place_kernel(slots, spot, recv_ref, gain_ref, raw_ref, normed_ref):
+    first = PER_DEV * spot[0]
+    for n in range(GROUP_SLOTS):
+        slot = slots[n] % GROUP_SLOTS - first
 
         @pl.when((slot >= 0) & (slot < PER_DEV))
         def _():
@@ -122,17 +111,17 @@
     normed_ref[...] = (floats * lax.rsqrt(mean + EPS) * gain_ref[...]).astype(jnp.bfloat16)
 
 
-def place(meta, recv, gain):
+def place(slots, spot, recv, gain):
     vmem = pl.BlockSpec(memory_space=pltpu.VMEM)
     rows = jax.ShapeDtypeStruct((PER_DEV, NLEN, E), jnp.bfloat16)
     return pl.pallas_call(
         place_kernel,
         out_shape=(rows, rows),
-        in_specs=[pl.BlockSpec(memory_space=pltpu.SMEM), vmem, vmem],
+        in_specs=[pl.BlockSpec(memory_space=pltpu.SMEM)] * 2 + [vmem, vmem],
         out_specs=(vmem, vmem),
         compiler_params=pltpu.CompilerParams(vmem_limit_bytes=8 * 1024 * 1024),
         name="place_rows",
-    )(meta, recv, gain)
+    )(slots, spot, recv, gain)
 
 
 def both_cores(mine, other):
@@ -163,8 +152,8 @@
     return total
 
 
-def by_case(meta, even, odd, x_pieces, write):
-    core, parity = meta[33], meta[34] % 2
+def by_case(spot, even, odd, x_pieces, write):
+    core, parity = spot[0] % 2, spot[0] // 2 % 2
 
     @pl.when((core == 0) & (parity == 0))
     def _():
@@ -179,14 +168,14 @@
         write(blocks_x(x_pieces))
 
 
-def early_kernel(meta, mine, other, own_a, own_b, left_a, left_b, right_a, right_b, acc_ref):
+def early_kernel(spot, mine, other, own_a, own_b, left_a, left_b, right_a, right_b, acc_ref):
     normed = both_cores(mine, other)
 
     def write(blocks):
         acc_ref[...] = multiply(normed, blocks)
 
     by_case(
-        meta,
+        spot,
         ((own_a, right_a), (own_b, right_b)),
         ((left_a, own_a), (left_b, own_b)),
         (own_a, own_b, left_a, left_b, right_a, right_b),
@@ -195,7 +184,7 @@
 
 
 def late_kernel(
-    meta, raw, mine, other, acc, left_a, left_b, right_a, right_b, far_a, far_b, mine_ref, other_ref
+    spot, raw, mine, other, acc, left_a, left_b, right_a, right_b, far_a, far_b, mine_ref, other_ref
 ):
     normed = both_cores(mine, other)
 
@@ -205,7 +194,7 @@
         other_ref[...] = total[ROWS:]
 
     by_case(
-        meta,
+        spot,
         ((far_a, left_a), (far_b, left_b)),
         ((right_a, far_a), (right_b, far_b)),
         (far_a, far_b),
@@ -213,7 +202,7 @@
     )
 
 
-def encode_part(kernel, outs, meta, *arrays):
+def encode_part(kernel, outs, spot, *arrays):
     vmem = pl.BlockSpec(memory_space=pltpu.VMEM)
     return pl.pallas_call(
         kernel,
@@ -222,7 +211,7 @@
         out_specs=jax.tree.map(lambda _: vmem, outs),
         compiler_params=pltpu.CompilerParams(vmem_limit_bytes=14 * 1024 * 1024),
         name=kernel.__name__,
-    )(meta, *arrays)
+    )(spot, *arrays)
 
 
 GROUP = 4
@@ -327,18 +316,14 @@
 
 
 def body(queries, neighbours, slots, gain, up, down, key_proj, value_proj, grads):
-    z, x, y, c = (lax.axis_index(name) for name in ALL)
-    group = NY * NC * PER_DEV
-    here = jnp.stack([y * NC + c, c, y, x]).astype(jnp.int32)
-    meta = jnp.concatenate([slots - (z * NX + x) * group, here])
-
+    y, c = lax.axis_index("y"), lax.axis_index("c")
     spot = (y * NC + c).astype(jnp.int32).reshape(1)
-    unit, whole = units(spot, key_proj.T, value_proj.T, up.T, down)
+    rows = neighbours.reshape(PER_DEV, NLEN, E)
+    unit, whole, outgoing = units(slots, spot, rows, key_proj.T, value_proj.T, up.T, down)
     along_x = lax.all_gather(unit, "x", axis=0, tiled=False)
     kv_head = along_x[:, :32].reshape(HD, E)
     weights = lax.all_gather(kv_head, ("z", "c"), axis=0, tiled=False)
 
-    outgoing = send_blocks(meta, neighbours.reshape(PER_DEV, NLEN, E))
     ff_unit = jnp.where(c == 0, along_x[:, 32:].reshape(32, E), whole)
     ff_unit, outgoing = lax.optimization_barrier((ff_unit, outgoing))
     recv = lax.all_to_all(outgoing, ("y", "c"), 0, 0, tiled=True)
@@ -348,15 +333,15 @@
     left_a, right_b = ring(own_a, 1), ring(own_b, -1)
     left_b, right_a = ring(own_b, 1), ring(own_a, -1)
     left_a, right_b, recv = lax.optimization_barrier((left_a, right_b, recv))
-    raw, normed = place(meta, recv, gain.reshape(1, E))
+    raw, normed = place(slots, spot, recv, gain.reshape(1, E))
     other = swap(normed)
     far_a, far_b = ring(left_a, 1), ring(right_b, -1)
     near = (left_a, left_b, right_a, right_b)
     one = jax.ShapeDtypeStruct((ROWS, E), jnp.float32)
     two = jax.ShapeDtypeStruct((2 * ROWS, E), jnp.float32)
-    acc = encode_part(early_kernel, two, meta, normed, other, own_a, own_b, *near)
+    acc = encode_part(early_kernel, two, spot, normed, other, own_a, own_b, *near)
     mine, given = encode_part(
-        late_kernel, (one, one), meta, raw, normed, other, acc, *near, far_a, far_b
+        late_kernel, (one, one), spot, raw, normed, other, acc, *near, far_a, far_b
     )
     return attend(mine, swap(given), weights, queries, grads)
 

time: 136 us -> 131 us (0.963)
  starting transfers between devices: 43.8 us -> 41.1 us
  Pallas kernels: 19.6 us -> 17.6 us
    ppermute x2, starting transfers between devices: 12.9 us -> 10.2 us  [swap(): return lax.ppermute(rows, 'c', [(0, 1), (1, 0)])]
    pallas_call x1 -> x0, Pallas kernels: 1.56 us -> none  [send_blocks(): pl.pallas_call(send_kernel, out_shape=jax.ShapeDtypeStruct((NY * NC, NLEN...]
  transfers between devices with their start and end apart: 10 -> 10, of which waited for: 3 -> 3; matrix products, arithmetic and copies ran while one was open for 1% -> 1% of each run, Pallas kernels for 6% -> 4%
where the time goes in v6:
time: 131 us; the launch traced here: 130 us
  blocking collectives  48.7 us (37%)
  starting transfers between devices  41.1 us (31%)
  Pallas kernels  17.6 us (13%)
  between operations  14.2 us (11%)
  waiting for transfers between devices  5.62 us (4%)
  local copies, waits for them, and re-layouts  2.14 us (2%)
    all_gather x1, blocking collectives, body(): own = lax.all_gather(ff_unit, 'z', axis=0, tiled=False)  37.9 us
    ppermute x6, starting transfers between devices, ring(): return lax.ppermute(rows, ('x', 'y', 'c'), ring_pairs(step))  19.6 us
    all_to_all x1, starting transfers between devices, body(): recv = lax.all_to_all(outgoing, ('y', 'c'), 0, 0, tiled=True)  11.2 us
    all_gather x1, blocking collectives, body(): along_x = lax.all_gather(unit, 'x', axis=0, tiled=False)  10.8 us
    pallas_call x1, Pallas kernels, attend(): pl.pallas_call(attend_kernel, out_shape=(wide, wide, jax.ShapeDtypeStruct...  10.2 us
    ppermute x2, starting transfers between devices, swap(): return lax.ppermute(rows, 'c', [(0, 1), (1, 0)])  10.2 us
    pallas_call x2, Pallas kernels, encode_part(): pl.pallas_call(kernel, out_shape=outs, in_specs=[pl.BlockSpec(memory_spac...  3.86 us
    ppermute x6, waiting for transfers between devices, ring(): return lax.ppermute(rows, ('x', 'y', 'c'), ring_pairs(step))  3.7 us
  transfers between devices with their start and end apart: 10, of which 3 were waited for; matrix products, arithmetic and copies ran while one was open for 1% of the time, Pallas kernels for 4%

profile of v6, /device:TPU:1, one launch (start us, length us, event | category | flops | bytes accessed | tf_op | source)
XLA Modules:
  0.0 130.2 jit_solution(9808436988974797108)
XLA Ops:
  7.2 0.0 all-gather.4.cloned.1.call-start
  7.2 2.4 %pick_units.1 = (bf16[40,896]{1,0:T(8,128)(2,1)}, bf16[32,896]{1,0:T(8,128)(2,1)}, bf16[8,64,896]{2,1,0:T(8,128)(2,1)}) custom-call(s32[32]{0:T(128)} %slots.3, s32[1]{0:T(128)} %bitcast.spot, bf16[4,64,896]{2,1,0:T(8,128)(2,1)} %bitcast.16, bf16[32,896]{1,0:T(8,128)(2,1)} %bitcast.17, bf16[32,896]{1,0:T(8,128)(2,1)} %bitcast.18, bf16[28,896]{1,0:T(8,128)(2,1)} %bitcast.19, ...), custom_call_target="tpu_custom_call" | custom-call | tf_op jit(solution)/shard_map/pick_units/pallas_call | solution.py:82
  9.6 10.8 %all-gather = bf16[160,896]{1,0:T(8,128)(2,1)S(1)} all-gather(bf16[40,896]{1,0:T(8,128)(2,1)} %get-tuple-element.17), channel_id=2, replica_groups=mesh['z'=16,'x'=4,'y'=4,'c'=2] {'x'}, dimensions={0}, use_global_device_ids=true | all-gather | bytes 358400 | tf_op jit(solution)/shard_map/all_gather | solution.py:323
  20.4 0.7 slice.17
  21.1 0.0 all-gather.4.cloned.1.call-update
  21.1 0.8 fusion
  22.0 11.2 %all-to-all-start = ((bf16[8,64,896]{2,1,0:T(8,128)(2,1)}), bf16[8,64,896]{2,1,0:T(8,128)(2,1)S(1)}, u32[]{:S(2)}, u32[]{:S(2)}) async-start(bf16[8,64,896]{2,1,0:T(8,128)(2,1)} %get-tuple-element.21), calls=%async_computation | async-start | bytes 1835008 | tf_op jit(solution)/shard_map/all_to_all | solution.py:329
  33.2 37.9 %all-gather.1 = bf16[512,896]{1,0:T(8,128)(2,1)S(1)} all-gather(bf16[32,896]{1,0:T(8,128)(2,1)S(1)} %fusion), channel_id=3, replica_groups=mesh['z'=16,'x'=4,'y'=4,'c'=2] {'z'}, dimensions={0}, use_global_device_ids=true | all-gather | bytes 974848 | tf_op jit(solution)/shard_map/all_gather | solution.py:330
  71.1 0.0 copy-start
  71.1 0.0 copy-start.1
  71.1 0.0 all-to-all-done.recv_ref
  71.1 0.1 fusion.1
  71.2 2.8 %collective-permute-start = (bf16[8,32,896]{2,1,0:T(8,128)(2,1)S(1)}, bf16[8,32,896]{2,1,0:T(8,128)(2,1)S(1)}, u32[]{:S(2)}, u32[]{:S(2)}) collective-permute-start(bf16[8,32,896]{2,1,0:T(8,128)(2,1)S(1)} %get-tuple-element.32.own_a), channel_id=1, source_target_pairs={{0,2},{1,9},{2,4},{3,11},{4,6},{5,13},{6,0},{7,15},{8,10},{9,17},{... | collective-permute-start | bytes 1376264 | tf_op jit(solution)/shard_map/ppermute | solution.py:44
  74.0 3.8 %collective-permute-start.1 = (bf16[8,32,896]{2,1,0:T(8,128)(2,1)S(1)}, bf16[8,32,896]{2,1,0:T(8,128)(2,1)S(1)}, u32[]{:S(2)}, u32[]{:S(2)}) collective-permute-start(bf16[8,32,896]{2,1,0:T(8,128)(2,1)S(1)} %get-tuple-element.31.own_b), channel_id=1, source_target_pairs={{0,6},{1,25},{2,0},{3,27},{4,2},{5,29},{6,4},{7,31},{8,14},{9,1},{... | collective-permute-start | bytes 1376264 | tf_op jit(solution)/shard_map/ppermute | solution.py:44
  77.8 0.7 reshape.21.gain_ref
  78.5 1.9 %collective-permute-start.3 = (bf16[8,32,896]{2,1,0:T(8,128)(2,1)S(1)}, bf16[8,32,896]{2,1,0:T(8,128)(2,1)S(1)}, u32[]{:S(2)}, u32[]{:S(2)}) collective-permute-start(bf16[8,32,896]{2,1,0:T(8,128)(2,1)S(1)} %get-tuple-element.31.own_b), channel_id=1, source_target_pairs={{0,2},{1,9},{2,4},{3,11},{4,6},{5,13},{6,0},{7,15},{8,10},{9,17},{... | collective-permute-start | bytes 1376264 | tf_op jit(solution)/shard_map/ppermute | solution.py:44
  80.4 4.6 %collective-permute-start.4 = (bf16[8,32,896]{2,1,0:T(8,128)(2,1)S(1)}, bf16[8,32,896]{2,1,0:T(8,128)(2,1)S(1)}, u32[]{:S(2)}, u32[]{:S(2)}) collective-permute-start(bf16[8,32,896]{2,1,0:T(8,128)(2,1)S(1)} %get-tuple-element.32.own_a), channel_id=1, source_target_pairs={{0,6},{1,25},{2,0},{3,27},{4,2},{5,29},{6,4},{7,31},{8,14},{9,1},{... | collective-permute-start | bytes 1376264 | tf_op jit(solution)/shard_map/ppermute | solution.py:44
  85.0 0.0 collective-permute-done.left_a
  85.0 0.0 collective-permute-done.1.right_b
  85.0 0.0 copy-start.2
  85.1 0.6 copy-done.2
  85.7 1.2 place_rows.1
  86.9 7.7 %collective-permute-start.2 = (bf16[4,64,896]{2,1,0:T(8,128)(2,1)S(1)}, bf16[4,64,896]{2,1,0:T(8,128)(2,1)S(1)}, u32[]{:S(2)}, u32[]{:S(2)}) collective-permute-start(bf16[4,64,896]{2,1,0:T(8,128)(2,1)S(1)} %get-tuple-element.26.mine), channel_id=1, source_target_pairs={{0,1},{1,0},{2,3},{3,2},{4,5},{5,4},{6,7},{7,6},{8,9},{9,8},{10,11... | collective-permute-start | bytes 1376264 | tf_op jit(solution)/shard_map/ppermute | solution.py:48
  94.6 3.1 %collective-permute-start.5 = (bf16[8,32,896]{2,1,0:T(8,128)(2,1)S(1)}, bf16[8,32,896]{2,1,0:T(8,128)(2,1)S(1)}, u32[]{:S(2)}, u32[]{:S(2)}) collective-permute-start(bf16[8,32,896]{2,1,0:T(8,128)(2,1)S(1)} %collective-permute-done.left_a), channel_id=1, source_target_pairs={{0,2},{1,9},{2,4},{3,11},{4,6},{5,13},{6,0},{7,15},{8,10},{9,17},{... | collective-permute-start | bytes 1376264 | tf_op jit(solution)/shard_map/ppermute | solution.py:44
  97.7 3.4 %collective-permute-start.6 = (bf16[8,32,896]{2,1,0:T(8,128)(2,1)S(1)}, bf16[8,32,896]{2,1,0:T(8,128)(2,1)S(1)}, u32[]{:S(2)}, u32[]{:S(2)}) collective-permute-start(bf16[8,32,896]{2,1,0:T(8,128)(2,1)S(1)} %collective-permute-done.1.right_b), channel_id=1, source_target_pairs={{0,6},{1,25},{2,0},{3,27},{4,2},{5,29},{6,4},{7,31},{8,14},{9,1},{... | collective-permute-start | bytes 1376264 | tf_op jit(solution)/shard_map/ppermute | solution.py:44
  101.1 0.0 collective-permute-done.3.left_b
  101.1 0.0 collective-permute-done.4.right_a
  101.1 0.0 collective-permute-done.2.other
  101.1 2.5 %early_kernel.1.acc = f32[512,896]{1,0:T(8,128)S(1)} custom-call(s32[1]{0:T(128)} %bitcast.spot, bf16[4,64,896]{2,1,0:T(8,128)(2,1)S(1)} %get-tuple-element.26.mine, bf16[4,64,896]{2,1,0:T(8,128)(2,1)S(1)} %collective-permute-done.2.other, bf16[8,32,896]{2,1,0:T(8,128)(2,1)S(1)} %get-tuple-element.32.own_a, bf16[8,32,896]{2,1,0:T(8,128)(2,1)S(1)} %get-tuple-element.31.own_b, ...), custom_call_target="tpu_custom_call" | custom-call | tf_op jit(solution)/shard_map/early_kernel/pallas_call | solution.py:207
  103.7 1.7 %collective-permute-done.5.far_a = bf16[8,32,896]{2,1,0:T(8,128)(2,1)S(1)} collective-permute-done((bf16[8,32,896]{2,1,0:T(8,128)(2,1)S(1)}, bf16[8,32,896]{2,1,0:T(8,128)(2,1)S(1)}, u32[]{:S(2)}, u32[]{:S(2)}) %collective-permute-start.5) | collective-permute-done | bytes 458784 | tf_op jit(solution)/shard_map/ppermute | solution.py:44
  105.3 2.0 %collective-permute-done.6.far_b = bf16[8,32,896]{2,1,0:T(8,128)(2,1)S(1)} collective-permute-done((bf16[8,32,896]{2,1,0:T(8,128)(2,1)S(1)}, bf16[8,32,896]{2,1,0:T(8,128)(2,1)S(1)}, u32[]{:S(2)}, u32[]{:S(2)}) %collective-permute-start.6) | collective-permute-done | bytes 458784 | tf_op jit(solution)/shard_map/ppermute | solution.py:44
  107.3 1.4 %late_kernel.1 = (f32[256,896]{1,0:T(8,128)S(1)}, f32[256,896]{1,0:T(8,128)S(1)}) custom-call(s32[1]{0:T(128)} %bitcast.spot, bf16[4,64,896]{2,1,0:T(8,128)(2,1)S(1)} %get-tuple-element.25.raw, bf16[4,64,896]{2,1,0:T(8,128)(2,1)S(1)} %get-tuple-element.26.mine, bf16[4,64,896]{2,1,0:T(8,128)(2,1)S(1)} %collective-permute-done.2.other, ...), custom_call_target="tpu_custom_call" | custom-call | tf_op jit(solution)/shard_map/late_kernel/pallas_call | solution.py:207
  108.7 2.5 %collective-permute-start.7 = (f32[256,896]{1,0:T(8,128)S(1)}, f32[256,896]{1,0:T(8,128)S(1)}, u32[]{:S(2)}, u32[]{:S(2)}) collective-permute-start(f32[256,896]{1,0:T(8,128)S(1)} %get-tuple-element.30), channel_id=1, source_target_pairs={{0,1},{1,0},{2,3},{3,2},{4,5},{5,4},{6,7},{7,6},{8,9},{9,8},{10,11... | collective-permute-start | bytes 2752520 | tf_op jit(solution)/shard_map/ppermute | solution.py:48
  111.2 1.9 %collective-permute-done.7.other_ref = f32[256,896]{1,0:T(8,128)S(1)} collective-permute-done((f32[256,896]{1,0:T(8,128)S(1)}, f32[256,896]{1,0:T(8,128)S(1)}, u32[]{:S(2)}, u32[]{:S(2)}) %collective-permute-start.7) | collective-permute-done | bytes 917536 | tf_op jit(solution)/shard_map/ppermute | solution.py:48
  113.1 0.0 all-gather.4.cloned.1.call-done.w_hbm
  113.1 0.0 copy-done
  113.1 0.0 copy-done.1
  113.1 10.2 %attend_spans.1 = (bf16[128,2048]{1,0:T(8,128)(2,1)}, bf16[128,2048]{1,0:T(8,128)(2,1)}, bf16[256,896]{1,0:T(8,128)(2,1)}) custom-call(f32[256,896]{1,0:T(8,128)S(1)} %get-tuple-element.29.mine_ref, f32[256,896]{1,0:T(8,128)S(1)} %collective-permute-done.7.other_ref, bf16[32,128,896]{2,1,0:T(8,128)(2,1)} %all-gather.4.cloned.1.call-done.w_hbm, ...), custom_call_target="tpu_custom_call" | custom-call | tf_op jit(solution)/shard_map/attend_spans/pallas_call | solution.py:297
Async XLA Ops:
  7.2 105.9 %all-gather.4.cloned.1.call-start = ((), (), s32[]{:S(2)}) async-start(), calls=%async_computation.1 | async-start | bytes 7569408 | tf_op jit(solution)/shard_map/all_gather | solution.py:325
  22.0 49.1 %all-to-all-start = ((bf16[8,64,896]{2,1,0:T(8,128)(2,1)}), bf16[8,64,896]{2,1,0:T(8,128)(2,1)S(1)}, u32[]{:S(2)}, u32[]{:S(2)}) async-start(bf16[8,64,896]{2,1,0:T(8,128)(2,1)} %get-tuple-element.21), calls=%async_computation | async-start | bytes 1835008 | tf_op jit(solution)/shard_map/all_to_all | solution.py:329
  71.1 42.0 %copy-start = (bf16[128,2048]{1,0:T(8,128)(2,1)S(1)}, bf16[128,2048]{1,0:T(8,128)(2,1)}, u32[]{:S(2)}) copy-start(bf16[128,2048]{1,0:T(8,128)(2,1)} %q_hbm.1) | copy-start | bytes 1572868
  71.1 42.0 %copy-start.1 = (bf16[128,2048]{1,0:T(8,128)(2,1)S(1)}, bf16[128,2048]{1,0:T(8,128)(2,1)}, u32[]{:S(2)}) copy-start(bf16[128,2048]{1,0:T(8,128)(2,1)} %g_hbm.1) | copy-start | bytes 1572868
  71.2 13.8 %collective-permute-start = (bf16[8,32,896]{2,1,0:T(8,128)(2,1)S(1)}, bf16[8,32,896]{2,1,0:T(8,128)(2,1)S(1)}, u32[]{:S(2)}, u32[]{:S(2)}) collective-permute-start(bf16[8,32,896]{2,1,0:T(8,128)(2,1)S(1)} %get-tuple-element.32.own_a), channel_id=1, source_target_pairs={{0,2},{1,9},{2,4},{3,11},{4,6},{5,13},{6,0},{7,15},{8,10},{9,17},{... | collective-permute-start | bytes 1376264 | tf_op jit(solution)/shard_map/ppermute | solution.py:44
  74.0 11.0 %collective-permute-start.1 = (bf16[8,32,896]{2,1,0:T(8,128)(2,1)S(1)}, bf16[8,32,896]{2,1,0:T(8,128)(2,1)S(1)}, u32[]{:S(2)}, u32[]{:S(2)}) collective-permute-start(bf16[8,32,896]{2,1,0:T(8,128)(2,1)S(1)} %get-tuple-element.31.own_b), channel_id=1, source_target_pairs={{0,6},{1,25},{2,0},{3,27},{4,2},{5,29},{6,4},{7,31},{8,14},{9,1},{... | collective-permute-start | bytes 1376264 | tf_op jit(solution)/shard_map/ppermute | solution.py:44
  78.5 22.6 %collective-permute-start.3 = (bf16[8,32,896]{2,1,0:T(8,128)(2,1)S(1)}, bf16[8,32,896]{2,1,0:T(8,128)(2,1)S(1)}, u32[]{:S(2)}, u32[]{:S(2)}) collective-permute-start(bf16[8,32,896]{2,1,0:T(8,128)(2,1)S(1)} %get-tuple-element.31.own_b), channel_id=1, source_target_pairs={{0,2},{1,9},{2,4},{3,11},{4,6},{5,13},{6,0},{7,15},{8,10},{9,17},{... | collective-permute-start | bytes 1376264 | tf_op jit(solution)/shard_map/ppermute | solution.py:44
  80.4 20.7 %collective-permute-start.4 = (bf16[8,32,896]{2,1,0:T(8,128)(2,1)S(1)}, bf16[8,32,896]{2,1,0:T(8,128)(2,1)S(1)}, u32[]{:S(2)}, u32[]{:S(2)}) collective-permute-start(bf16[8,32,896]{2,1,0:T(8,128)(2,1)S(1)} %get-tuple-element.32.own_a), channel_id=1, source_target_pairs={{0,6},{1,25},{2,0},{3,27},{4,2},{5,29},{6,4},{7,31},{8,14},{9,1},{... | collective-permute-start | bytes 1376264 | tf_op jit(solution)/shard_map/ppermute | solution.py:44
  85.0 0.7 copy-start.2
  86.9 14.2 %collective-permute-start.2 = (bf16[4,64,896]{2,1,0:T(8,128)(2,1)S(1)}, bf16[4,64,896]{2,1,0:T(8,128)(2,1)S(1)}, u32[]{:S(2)}, u32[]{:S(2)}) collective-permute-start(bf16[4,64,896]{2,1,0:T(8,128)(2,1)S(1)} %get-tuple-element.26.mine), channel_id=1, source_target_pairs={{0,1},{1,0},{2,3},{3,2},{4,5},{5,4},{6,7},{7,6},{8,9},{9,8},{10,11... | collective-permute-start | bytes 1376264 | tf_op jit(solution)/shard_map/ppermute | solution.py:48
  94.6 10.7 %collective-permute-start.5 = (bf16[8,32,896]{2,1,0:T(8,128)(2,1)S(1)}, bf16[8,32,896]{2,1,0:T(8,128)(2,1)S(1)}, u32[]{:S(2)}, u32[]{:S(2)}) collective-permute-start(bf16[8,32,896]{2,1,0:T(8,128)(2,1)S(1)} %collective-permute-done.left_a), channel_id=1, source_target_pairs={{0,2},{1,9},{2,4},{3,11},{4,6},{5,13},{6,0},{7,15},{8,10},{9,17},{... | collective-permute-start | bytes 1376264 | tf_op jit(solution)/shard_map/ppermute | solution.py:44
  97.7 9.6 %collective-permute-start.6 = (bf16[8,32,896]{2,1,0:T(8,128)(2,1)S(1)}, bf16[8,32,896]{2,1,0:T(8,128)(2,1)S(1)}, u32[]{:S(2)}, u32[]{:S(2)}) collective-permute-start(bf16[8,32,896]{2,1,0:T(8,128)(2,1)S(1)} %collective-permute-done.1.right_b), channel_id=1, source_target_pairs={{0,6},{1,25},{2,0},{3,27},{4,2},{5,29},{6,4},{7,31},{8,14},{9,1},{... | collective-permute-start | bytes 1376264 | tf_op jit(solution)/shard_map/ppermute | solution.py:44
  108.7 4.4 %collective-permute-start.7 = (f32[256,896]{1,0:T(8,128)S(1)}, f32[256,896]{1,0:T(8,128)S(1)}, u32[]{:S(2)}, u32[]{:S(2)}) collective-permute-start(f32[256,896]{1,0:T(8,128)S(1)} %get-tuple-element.30), channel_id=1, source_target_pairs={{0,1},{1,0},{2,3},{3,2},{4,5},{5,4},{6,7},{7,6},{8,9},{9,8},{10,11... | collective-permute-start | bytes 2752520 | tf_op jit(solution)/shard_map/ppermute | solution.py:48
Sparse Core Ops, SparseCore 0:
  21.3 87.9 all-gather.3

commit v7 on v6

--- a/solution.py
+++ b/solution.py
@@ -320,15 +320,14 @@
     spot = (y * NC + c).astype(jnp.int32).reshape(1)
     rows = neighbours.reshape(PER_DEV, NLEN, E)
     unit, whole, outgoing = units(slots, spot, rows, key_proj.T, value_proj.T, up.T, down)
+    recv = lax.all_to_all(outgoing, ("y", "c"), 0, 0, tiled=True)
     along_x = lax.all_gather(unit, "x", axis=0, tiled=False)
+    along_x, recv = lax.optimization_barrier((along_x, recv))
     kv_head = along_x[:, :32].reshape(HD, E)
     weights = lax.all_gather(kv_head, ("z", "c"), axis=0, tiled=False)
 
     ff_unit = jnp.where(c == 0, along_x[:, 32:].reshape(32, E), whole)
-    ff_unit, outgoing = lax.optimization_barrier((ff_unit, outgoing))
-    recv = lax.all_to_all(outgoing, ("y", "c"), 0, 0, tiled=True)
     own = lax.all_gather(ff_unit, "z", axis=0, tiled=False)
-    own, recv = lax.optimization_barrier((own, recv))
     own_a, own_b = own[: NZ // 2], own[NZ // 2 :]
     left_a, right_b = ring(own_a, 1), ring(own_b, -1)
     left_b, right_a = ring(own_b, 1), ring(own_a, -1)

time: 131 us -> 132 us (level)
  waiting for transfers between devices: 5.62 us -> 9.23 us
  blocking collectives: 48.7 us -> 45.8 us
    all_to_all x1, waiting for transfers between devices: 0.01 us -> 3.31 us  [body(): recv = lax.all_to_all(outgoing, ('y', 'c'), 0, 0, tiled=True)]
    all_gather x1, blocking collectives: 37.9 us -> 35.4 us  [body(): own = lax.all_gather(ff_unit, 'z', axis=0, tiled=False)]
    ppermute x2, starting transfers between devices: 10.2 us -> 11.8 us  [swap(): return lax.ppermute(rows, 'c', [(0, 1), (1, 0)])]
  transfers between devices with their start and end apart: 10 -> 10, of which waited for: 3 -> 5; matrix products, arithmetic and copies ran while one was open for 1% -> 1% of each run, Pallas kernels for 4% -> 4%
where the time goes in v7:
time: 132 us
  blocking collectives  45.8 us (35%)
  starting transfers between devices  41.8 us (32%)
  Pallas kernels  17.6 us (13%)
  between operations  14.2 us (11%)
  waiting for transfers between devices  9.23 us (7%)
  local copies, waits for them, and re-layouts  2.13 us (2%)
    all_gather x1, blocking collectives, body(): own = lax.all_gather(ff_unit, 'z', axis=0, tiled=False)  35.4 us
    ppermute x6, starting transfers between devices, ring(): return lax.ppermute(rows, ('x', 'y', 'c'), ring_pairs(step))  19.6 us
    ppermute x2, starting transfers between devices, swap(): return lax.ppermute(rows, 'c', [(0, 1), (1, 0)])  11.8 us
    all_gather x1, blocking collectives, body(): along_x = lax.all_gather(unit, 'x', axis=0, tiled=False)  10.4 us
    all_to_all x1, starting transfers between devices, body(): recv = lax.all_to_all(outgoing, ('y', 'c'), 0, 0, tiled=True)  10.3 us
    pallas_call x1, Pallas kernels, attend(): pl.pallas_call(attend_kernel, out_shape=(wide, wide, jax.ShapeDtypeStruct...  10.2 us
    pallas_call x2, Pallas kernels, encode_part(): pl.pallas_call(kernel, out_shape=outs, in_specs=[pl.BlockSpec(memory_spac...  3.86 us
    ppermute x6, waiting for transfers between devices, ring(): return lax.ppermute(rows, ('x', 'y', 'c'), ring_pairs(step))  3.64 us
  transfers between devices with their start and end apart: 10, of which 5 were waited for; matrix products, arithmetic and copies ran while one was open for 1% of the time, Pallas kernels for 4%

profile of v7, /device:TPU:1, one launch (start us, length us, event | category | flops | bytes accessed | tf_op | source)
XLA Modules:
  0.0 131.6 jit_solution(9969220301421796031)
XLA Ops:
  7.2 2.3 %pick_units.1 = (bf16[40,896]{1,0:T(8,128)(2,1)}, bf16[32,896]{1,0:T(8,128)(2,1)}, bf16[8,64,896]{2,1,0:T(8,128)(2,1)}) custom-call(s32[32]{0:T(128)} %slots.3, s32[1]{0:T(128)} %bitcast.spot, bf16[4,64,896]{2,1,0:T(8,128)(2,1)} %bitcast.20, bf16[32,896]{1,0:T(8,128)(2,1)} %bitcast.21, bf16[32,896]{1,0:T(8,128)(2,1)} %bitcast.22, bf16[28,896]{1,0:T(8,128)(2,1)} %bitcast.23, ...), custom_call_target="tpu_custom_call" | custom-call | tf_op jit(solution)/shard_map/pick_units/pallas_call | solution.py:82
  9.5 10.3 %all-to-all-start = ((bf16[8,64,896]{2,1,0:T(8,128)(2,1)}), bf16[8,64,896]{2,1,0:T(8,128)(2,1)S(1)}, u32[]{:S(2)}, u32[]{:S(2)}) async-start(bf16[8,64,896]{2,1,0:T(8,128)(2,1)} %get-tuple-element.16), calls=%async_computation | async-start | bytes 1835008 | tf_op jit(solution)/shard_map/all_to_all | solution.py:323
  19.8 0.0 all-gather.4.cloned.1.call-start
  19.8 10.4 %all-gather = bf16[160,896]{1,0:T(8,128)(2,1)S(1)} all-gather(bf16[40,896]{1,0:T(8,128)(2,1)} %get-tuple-element.15), channel_id=2, replica_groups=mesh['z'=16,'x'=4,'y'=4,'c'=2] {'x'}, dimensions={0}, use_global_device_ids=true | all-gather | bytes 358400 | tf_op jit(solution)/shard_map/all_gather | solution.py:324
  30.2 3.3 %all-to-all-done.recv_ref = bf16[8,64,896]{2,1,0:T(8,128)(2,1)S(1)} async-done(((bf16[8,64,896]{2,1,0:T(8,128)(2,1)}), bf16[8,64,896]{2,1,0:T(8,128)(2,1)S(1)}, u32[]{:S(2)}, u32[]{:S(2)}) %all-to-all-start) | async-done | bytes 917536 | tf_op jit(solution)/shard_map/all_to_all | solution.py:323
  33.5 0.7 slice.15
  34.3 0.0 all-gather.4.cloned.1.call-update
  34.3 0.8 bitcast_select_fusion
  35.1 35.4 %all-gather.1 = bf16[512,896]{1,0:T(8,128)(2,1)S(1)} all-gather(bf16[32,896]{1,0:T(8,128)(2,1)S(1)} %bitcast_select_fusion), channel_id=3, replica_groups=mesh['z'=16,'x'=4,'y'=4,'c'=2] {'z'}, dimensions={0}, use_global_device_ids=true | all-gather | bytes 974848 | tf_op jit(solution)/shard_map/all_gather | solution.py:330
  70.6 0.0 copy-start
  70.6 0.0 copy-start.1
  70.6 0.1 fusion
  70.6 3.1 %collective-permute-start = (bf16[8,32,896]{2,1,0:T(8,128)(2,1)S(1)}, bf16[8,32,896]{2,1,0:T(8,128)(2,1)S(1)}, u32[]{:S(2)}, u32[]{:S(2)}) collective-permute-start(bf16[8,32,896]{2,1,0:T(8,128)(2,1)S(1)} %bitcast.14), channel_id=1, source_target_pairs={{0,2},{1,9},{2,4},{3,11},{4,6},{5,13},{6,0},{7,15},{8,10},{9,17},{... | collective-permute-start | bytes 1376264 | tf_op jit(solution)/shard_map/ppermute | solution.py:44
  73.7 3.6 %collective-permute-start.1 = (bf16[8,32,896]{2,1,0:T(8,128)(2,1)S(1)}, bf16[8,32,896]{2,1,0:T(8,128)(2,1)S(1)}, u32[]{:S(2)}, u32[]{:S(2)}) collective-permute-start(bf16[8,32,896]{2,1,0:T(8,128)(2,1)S(1)} %bitcast.11), channel_id=1, source_target_pairs={{0,6},{1,25},{2,0},{3,27},{4,2},{5,29},{6,4},{7,31},{8,14},{9,1},{... | collective-permute-start | bytes 1376264 | tf_op jit(solution)/shard_map/ppermute | solution.py:44
  77.3 0.7 reshape.21.gain_ref
  78.0 1.9 %collective-permute-start.3 = (bf16[8,32,896]{2,1,0:T(8,128)(2,1)S(1)}, bf16[8,32,896]{2,1,0:T(8,128)(2,1)S(1)}, u32[]{:S(2)}, u32[]{:S(2)}) collective-permute-start(bf16[8,32,896]{2,1,0:T(8,128)(2,1)S(1)} %bitcast.12), channel_id=1, source_target_pairs={{0,2},{1,9},{2,4},{3,11},{4,6},{5,13},{6,0},{7,15},{8,10},{9,17},{... | collective-permute-start | bytes 1376264 | tf_op jit(solution)/shard_map/ppermute | solution.py:44
  79.9 4.6 %collective-permute-start.4 = (bf16[8,32,896]{2,1,0:T(8,128)(2,1)S(1)}, bf16[8,32,896]{2,1,0:T(8,128)(2,1)S(1)}, u32[]{:S(2)}, u32[]{:S(2)}) collective-permute-start(bf16[8,32,896]{2,1,0:T(8,128)(2,1)S(1)} %bitcast.15), channel_id=1, source_target_pairs={{0,6},{1,25},{2,0},{3,27},{4,2},{5,29},{6,4},{7,31},{8,14},{9,1},{... | collective-permute-start | bytes 1376264 | tf_op jit(solution)/shard_map/ppermute | solution.py:44
  84.5 0.0 collective-permute-done.left_a
  84.5 0.0 collective-permute-done.1.right_b
  84.5 0.0 copy-start.2
  84.5 0.6 copy-done.2
  85.2 1.2 place_rows.1
  86.4 9.3 %collective-permute-start.2 = (bf16[4,64,896]{2,1,0:T(8,128)(2,1)S(1)}, bf16[4,64,896]{2,1,0:T(8,128)(2,1)S(1)}, u32[]{:S(2)}, u32[]{:S(2)}) collective-permute-start(bf16[4,64,896]{2,1,0:T(8,128)(2,1)S(1)} %get-tuple-element.22.mine), channel_id=1, source_target_pairs={{0,1},{1,0},{2,3},{3,2},{4,5},{5,4},{6,7},{7,6},{8,9},{9,8},{10,11... | collective-permute-start | bytes 1376264 | tf_op jit(solution)/shard_map/ppermute | solution.py:48
  95.6 2.9 %collective-permute-start.5 = (bf16[8,32,896]{2,1,0:T(8,128)(2,1)S(1)}, bf16[8,32,896]{2,1,0:T(8,128)(2,1)S(1)}, u32[]{:S(2)}, u32[]{:S(2)}) collective-permute-start(bf16[8,32,896]{2,1,0:T(8,128)(2,1)S(1)} %collective-permute-done.left_a), channel_id=1, source_target_pairs={{0,2},{1,9},{2,4},{3,11},{4,6},{5,13},{6,0},{7,15},{8,10},{9,17},{... | collective-permute-start | bytes 1376264 | tf_op jit(solution)/shard_map/ppermute | solution.py:44
  98.6 3.5 %collective-permute-start.6 = (bf16[8,32,896]{2,1,0:T(8,128)(2,1)S(1)}, bf16[8,32,896]{2,1,0:T(8,128)(2,1)S(1)}, u32[]{:S(2)}, u32[]{:S(2)}) collective-permute-start(bf16[8,32,896]{2,1,0:T(8,128)(2,1)S(1)} %collective-permute-done.1.right_b), channel_id=1, source_target_pairs={{0,6},{1,25},{2,0},{3,27},{4,2},{5,29},{6,4},{7,31},{8,14},{9,1},{... | collective-permute-start | bytes 1376264 | tf_op jit(solution)/shard_map/ppermute | solution.py:44
  102.1 0.0 collective-permute-done.3.left_b
  102.2 0.0 collective-permute-done.4.right_a
  102.2 0.0 collective-permute-done.2.other
  102.2 2.5 %early_kernel.1.acc = f32[512,896]{1,0:T(8,128)S(1)} custom-call(s32[1]{0:T(128)} %bitcast.spot, bf16[4,64,896]{2,1,0:T(8,128)(2,1)S(1)} %get-tuple-element.22.mine, bf16[4,64,896]{2,1,0:T(8,128)(2,1)S(1)} %collective-permute-done.2.other, bf16[8,32,896]{2,1,0:T(8,128)(2,1)S(1)} %bitcast.16, bf16[8,32,896]{2,1,0:T(8,128)(2,1)S(1)} %bitcast.13, ...), custom_call_target="tpu_custom_call" | custom-call | tf_op jit(solution)/shard_map/early_kernel/pallas_call | solution.py:207
  104.7 1.7 %collective-permute-done.5.far_a = bf16[8,32,896]{2,1,0:T(8,128)(2,1)S(1)} collective-permute-done((bf16[8,32,896]{2,1,0:T(8,128)(2,1)S(1)}, bf16[8,32,896]{2,1,0:T(8,128)(2,1)S(1)}, u32[]{:S(2)}, u32[]{:S(2)}) %collective-permute-start.5) | collective-permute-done | bytes 458784 | tf_op jit(solution)/shard_map/ppermute | solution.py:44
  106.4 1.9 %collective-permute-done.6.far_b = bf16[8,32,896]{2,1,0:T(8,128)(2,1)S(1)} collective-permute-done((bf16[8,32,896]{2,1,0:T(8,128)(2,1)S(1)}, bf16[8,32,896]{2,1,0:T(8,128)(2,1)S(1)}, u32[]{:S(2)}, u32[]{:S(2)}) %collective-permute-start.6) | collective-permute-done | bytes 458784 | tf_op jit(solution)/shard_map/ppermute | solution.py:44
  108.3 1.4 %late_kernel.1 = (f32[256,896]{1,0:T(8,128)S(1)}, f32[256,896]{1,0:T(8,128)S(1)}) custom-call(s32[1]{0:T(128)} %bitcast.spot, bf16[4,64,896]{2,1,0:T(8,128)(2,1)S(1)} %get-tuple-element.21.raw, bf16[4,64,896]{2,1,0:T(8,128)(2,1)S(1)} %get-tuple-element.22.mine, bf16[4,64,896]{2,1,0:T(8,128)(2,1)S(1)} %collective-permute-done.2.other, ...), custom_call_target="tpu_custom_call" | custom-call | tf_op jit(solution)/shard_map/late_kernel/pallas_call | solution.py:207
  109.7 2.6 %collective-permute-start.7 = (f32[256,896]{1,0:T(8,128)S(1)}, f32[256,896]{1,0:T(8,128)S(1)}, u32[]{:S(2)}, u32[]{:S(2)}) collective-permute-start(f32[256,896]{1,0:T(8,128)S(1)} %get-tuple-element.26), channel_id=1, source_target_pairs={{0,1},{1,0},{2,3},{3,2},{4,5},{5,4},{6,7},{7,6},{8,9},{9,8},{10,11... | collective-permute-start | bytes 2752520 | tf_op jit(solution)/shard_map/ppermute | solution.py:48
  112.2 1.9 %collective-permute-done.7.other_ref = f32[256,896]{1,0:T(8,128)S(1)} collective-permute-done((f32[256,896]{1,0:T(8,128)S(1)}, f32[256,896]{1,0:T(8,128)S(1)}, u32[]{:S(2)}, u32[]{:S(2)}) %collective-permute-start.7) | collective-permute-done | bytes 917536 | tf_op jit(solution)/shard_map/ppermute | solution.py:48
  114.1 0.4 all-gather.4.cloned.1.call-done.w_hbm
  114.5 0.0 copy-done
  114.5 0.0 copy-done.1
  114.5 10.2 %attend_spans.1 = (bf16[128,2048]{1,0:T(8,128)(2,1)}, bf16[128,2048]{1,0:T(8,128)(2,1)}, bf16[256,896]{1,0:T(8,128)(2,1)}) custom-call(f32[256,896]{1,0:T(8,128)S(1)} %get-tuple-element.25.mine_ref, f32[256,896]{1,0:T(8,128)S(1)} %collective-permute-done.7.other_ref, bf16[32,128,896]{2,1,0:T(8,128)(2,1)} %all-gather.4.cloned.1.call-done.w_hbm, ...), custom_call_target="tpu_custom_call" | custom-call | tf_op jit(solution)/shard_map/attend_spans/pallas_call | solution.py:297
Async XLA Ops:
  9.5 24.0 %all-to-all-start = ((bf16[8,64,896]{2,1,0:T(8,128)(2,1)}), bf16[8,64,896]{2,1,0:T(8,128)(2,1)S(1)}, u32[]{:S(2)}, u32[]{:S(2)}) async-start(bf16[8,64,896]{2,1,0:T(8,128)(2,1)} %get-tuple-element.16), calls=%async_computation | async-start | bytes 1835008 | tf_op jit(solution)/shard_map/all_to_all | solution.py:323
  19.8 94.7 %all-gather.4.cloned.1.call-start = ((), (), s32[]{:S(2)}) async-start(), calls=%async_computation.1 | async-start | bytes 7569408 | tf_op jit(solution)/shard_map/all_gather | solution.py:327
  70.6 43.9 %copy-start = (bf16[128,2048]{1,0:T(8,128)(2,1)S(1)}, bf16[128,2048]{1,0:T(8,128)(2,1)}, u32[]{:S(2)}) copy-start(bf16[128,2048]{1,0:T(8,128)(2,1)} %q_hbm.1) | copy-start | bytes 1572868
  70.6 43.9 %copy-start.1 = (bf16[128,2048]{1,0:T(8,128)(2,1)S(1)}, bf16[128,2048]{1,0:T(8,128)(2,1)}, u32[]{:S(2)}) copy-start(bf16[128,2048]{1,0:T(8,128)(2,1)} %g_hbm.1) | copy-start | bytes 1572868
  70.6 13.8 %collective-permute-start = (bf16[8,32,896]{2,1,0:T(8,128)(2,1)S(1)}, bf16[8,32,896]{2,1,0:T(8,128)(2,1)S(1)}, u32[]{:S(2)}, u32[]{:S(2)}) collective-permute-start(bf16[8,32,896]{2,1,0:T(8,128)(2,1)S(1)} %bitcast.14), channel_id=1, source_target_pairs={{0,2},{1,9},{2,4},{3,11},{4,6},{5,13},{6,0},{7,15},{8,10},{9,17},{... | collective-permute-start | bytes 1376264 | tf_op jit(solution)/shard_map/ppermute | solution.py:44
  73.7 10.8 %collective-permute-start.1 = (bf16[8,32,896]{2,1,0:T(8,128)(2,1)S(1)}, bf16[8,32,896]{2,1,0:T(8,128)(2,1)S(1)}, u32[]{:S(2)}, u32[]{:S(2)}) collective-permute-start(bf16[8,32,896]{2,1,0:T(8,128)(2,1)S(1)} %bitcast.11), channel_id=1, source_target_pairs={{0,6},{1,25},{2,0},{3,27},{4,2},{5,29},{6,4},{7,31},{8,14},{9,1},{... | collective-permute-start | bytes 1376264 | tf_op jit(solution)/shard_map/ppermute | solution.py:44
  78.0 24.2 %collective-permute-start.3 = (bf16[8,32,896]{2,1,0:T(8,128)(2,1)S(1)}, bf16[8,32,896]{2,1,0:T(8,128)(2,1)S(1)}, u32[]{:S(2)}, u32[]{:S(2)}) collective-permute-start(bf16[8,32,896]{2,1,0:T(8,128)(2,1)S(1)} %bitcast.12), channel_id=1, source_target_pairs={{0,2},{1,9},{2,4},{3,11},{4,6},{5,13},{6,0},{7,15},{8,10},{9,17},{... | collective-permute-start | bytes 1376264 | tf_op jit(solution)/shard_map/ppermute | solution.py:44
  79.9 22.3 %collective-permute-start.4 = (bf16[8,32,896]{2,1,0:T(8,128)(2,1)S(1)}, bf16[8,32,896]{2,1,0:T(8,128)(2,1)S(1)}, u32[]{:S(2)}, u32[]{:S(2)}) collective-permute-start(bf16[8,32,896]{2,1,0:T(8,128)(2,1)S(1)} %bitcast.15), channel_id=1, source_target_pairs={{0,6},{1,25},{2,0},{3,27},{4,2},{5,29},{6,4},{7,31},{8,14},{9,1},{... | collective-permute-start | bytes 1376264 | tf_op jit(solution)/shard_map/ppermute | solution.py:44
  84.5 0.7 copy-start.2
  86.4 15.8 %collective-permute-start.2 = (bf16[4,64,896]{2,1,0:T(8,128)(2,1)S(1)}, bf16[4,64,896]{2,1,0:T(8,128)(2,1)S(1)}, u32[]{:S(2)}, u32[]{:S(2)}) collective-permute-start(bf16[4,64,896]{2,1,0:T(8,128)(2,1)S(1)} %get-tuple-element.22.mine), channel_id=1, source_target_pairs={{0,1},{1,0},{2,3},{3,2},{4,5},{5,4},{6,7},{7,6},{8,9},{9,8},{10,11... | collective-permute-start | bytes 1376264 | tf_op jit(solution)/shard_map/ppermute | solution.py:48
  95.6 10.7 %collective-permute-start.5 = (bf16[8,32,896]{2,1,0:T(8,128)(2,1)S(1)}, bf16[8,32,896]{2,1,0:T(8,128)(2,1)S(1)}, u32[]{:S(2)}, u32[]{:S(2)}) collective-permute-start(bf16[8,32,896]{2,1,0:T(8,128)(2,1)S(1)} %collective-permute-done.left_a), channel_id=1, source_target_pairs={{0,2},{1,9},{2,4},{3,11},{4,6},{5,13},{6,0},{7,15},{8,10},{9,17},{... | collective-permute-start | bytes 1376264 | tf_op jit(solution)/shard_map/ppermute | solution.py:44
  98.6 9.7 %collective-permute-start.6 = (bf16[8,32,896]{2,1,0:T(8,128)(2,1)S(1)}, bf16[8,32,896]{2,1,0:T(8,128)(2,1)S(1)}, u32[]{:S(2)}, u32[]{:S(2)}) collective-permute-start(bf16[8,32,896]{2,1,0:T(8,128)(2,1)S(1)} %collective-permute-done.1.right_b), channel_id=1, source_target_pairs={{0,6},{1,25},{2,0},{3,27},{4,2},{5,29},{6,4},{7,31},{8,14},{9,1},{... | collective-permute-start | bytes 1376264 | tf_op jit(solution)/shard_map/ppermute | solution.py:44
  109.7 4.5 %collective-permute-start.7 = (f32[256,896]{1,0:T(8,128)S(1)}, f32[256,896]{1,0:T(8,128)S(1)}, u32[]{:S(2)}, u32[]{:S(2)}) collective-permute-start(f32[256,896]{1,0:T(8,128)S(1)} %get-tuple-element.26), channel_id=1, source_target_pairs={{0,1},{1,0},{2,3},{3,2},{4,5},{5,4},{6,7},{7,6},{8,9},{9,8},{10,11... | collective-permute-start | bytes 2752520 | tf_op jit(solution)/shard_map/ppermute | solution.py:48
Sparse Core Ops, SparseCore 0:
  34.4 80.0 all-gather.3
